TPU v7x, 32 devices: a whole 2x2x4 slice. The times are simulated.
32 devices in a mesh: row: 8 (over y, x, core), head: 4 (over z).
Axes of the slice: x: 2, y: 2, z: 4, core: 2. Of those that a mesh axis runs over, the one named last changes fastest.
Arguments:
- activations: bfloat16 [16384, 768], P('row', 'head'), may hold values from -6 to 6
- segment_ids: int32 [16, 1024], P('row'), may hold values from 0 to 31, never falling along the last dimension, each value on 1 to 512 neighbouring positions
- block_lists: int32 [16, 12, 16, 4], P('row', 'head'), may hold values from -1 to 15, as said below
- feature_proj: bfloat16 [64, 256], replicated, may hold values from -5 to 5
- input_norm_gain: float32 [768], replicated, may hold values from 0.1 to 1.9
- input_norm_bias: float32 [768], replicated, may hold values from -1.5 to 1.5
- qkv_weight: bfloat16 [768, 2304], P(None, 'head'), may hold values from -0.21875 to 0.21875
- out_weight: bfloat16 [768, 768], P('head'), may hold values from -0.875 to 0.875
- middle_norm_gain: float32 [768], replicated, may hold values from 0.2 to 6
- middle_norm_bias: float32 [768], replicated, may hold values from -1.5 to 1.5
- up_weight: bfloat16 [768, 3072], P(None, 'head'), may hold values from -0.21875 to 0.21875
- down_weight: bfloat16 [3072, 768], P('head'), may hold values from -0.109375 to 0.109375
- out_grad: bfloat16 [16384, 768], P('row', 'head'), may hold values from -6 to 6
Outputs:
- block_out: bfloat16 [16384, 768], P('row', 'head')
- input_grad: float32 [16384, 768], P('row', 'head')
- norm_gain_grad: float32 [768], P('head')
- norm_shift_grad: float32 [768], P('head')
- qkv_weight_grad: float32 [768, 2304], P(None, 'head')
- out_weight_grad: float32 [768, 768], P('head')
- middle_norm_gain_gradient: float32 [768], P('head')
- middle_norm_bias_gradient: float32 [768], P('head')
- up_weight_grad: float32 [768, 3072], P(None, 'head')
- down_weight_grad: float32 [3072, 768], P('head')
Inputs may be any that keep to these rules, and one draw needn't show every extreme that they name: `segment_ids`: never falling along a sequence; equal numbers in one sequence mark one document, which may be as long as 512 tokens. `block_lists`: each list holds its used entries first, at least one, and -1 in the slots after them; used entries are key blocks of the same sequence and may repeat.
All inputs are finite; a program needn't handle non-finite values.
Results may differ from a plain program's by a relative error of at most 0.018.
Values may be sent and summed in bfloat16 or wider, within the bound.
No kernel may reach another device: no remote copies, remote signals or barrier semaphores. Data moves between devices by JAX's collectives and lax.ppermute only.
A program may use at most 192 MiB of HBM per device.

v0:
```python
from functools import partial

import jax
import jax.numpy as jnp
from jax import lax
from jax.sharding import PartitionSpec as P

BLK = 64


norm_eps = 1e-05


def normalize_rows(values):
    center = values - jnp.mean(values, axis=1, keepdims=True)
    scale = lax.rsqrt(jnp.mean(center * center, axis=1, keepdims=True) + norm_eps)
    return (center * scale, scale)


def feature_map(values, proj):
    quarter = values.shape[-1] ** (-0.25)
    linear = jnp.einsum("lhe,ef->lhf", values, proj, preferred_element_type=jnp.float32)
    wide = values.astype(jnp.float32)
    pre = quarter * linear - 0.5 * quarter * quarter * jnp.sum(wide * wide, axis=-1, keepdims=True)
    return jnp.exp(pre) * proj.shape[1] ** (-0.5)


def feature_back(grad_feat, values, feat_full, proj_wide):
    quarter = values.shape[-1] ** (-0.25)
    d_pre = grad_feat.astype(jnp.bfloat16).astype(jnp.float32) * feat_full
    through = jnp.einsum("lhf,ef->lhe", d_pre, proj_wide, precision=lax.Precision.HIGHEST)
    return quarter * through - quarter * quarter * values.astype(jnp.float32) * jnp.sum(
        d_pre, axis=-1, keepdims=True
    )


def block_terms(
    query_blk, key_rows, query_feature_block, key_feature_rows, doc_blk, doc_ids, sets_blk
):
    head_dim = query_blk.shape[-1]
    scores = jnp.einsum(
        "rhe,khe->hrk", query_blk, key_rows, preferred_element_type=jnp.float32
    ) * head_dim ** (-0.5)
    exp_score = jnp.exp(scores)
    lowrank_estimate = jnp.einsum(
        "ewm,qwm->weq", query_feature_block, key_feature_rows, preferred_element_type=jnp.float32
    )
    same_doc = (doc_blk[:, None] == doc_ids[None, :]).astype(jnp.float32)
    heads_here, row_blocks, _ = sets_blk.shape
    key_blocks = doc_ids.shape[0] // BLK
    block_ids = lax.broadcasted_iota(jnp.int32, (1, 1, 1, key_blocks), 3)
    hit_blocks = jnp.minimum(
        jnp.sum((sets_blk[:, :, :, None] == block_ids).astype(jnp.float32), axis=2), 1.0
    )
    spread_hits = jnp.broadcast_to(
        hit_blocks[:, :, None, :, None], (heads_here, row_blocks, BLK, key_blocks, BLK)
    )
    sparse = spread_hits.reshape(heads_here, row_blocks * BLK, key_blocks * BLK) * same_doc[None]
    other_mask = same_doc[None] - sparse
    combined = sparse * exp_score + other_mask * lowrank_estimate
    row_sum = jnp.sum(combined, axis=2, keepdims=True)
    return (exp_score, sparse, other_mask, combined, row_sum)


def attend(packed):
    queries, key_rows, val_rows, query_feature_rows, key_feature_rows, doc_ids, block_sets = packed
    length = queries.shape[0]
    step_rows = min(512, length)
    outputs = []
    for offset in range(0, length, step_rows):
        upper = offset + step_rows
        exp_score, sparse, other_mask, combined, row_sum = block_terms(
            queries[offset:upper],
            key_rows,
            query_feature_rows[offset:upper],
            key_feature_rows,
            doc_ids[offset:upper],
            doc_ids,
            block_sets[:, offset // BLK : upper // BLK],
        )
        weights = (combined / row_sum).astype(jnp.bfloat16)
        outputs.append(
            jnp.einsum(
                "hrk,khe->rhe", weights, val_rows, preferred_element_type=jnp.float32
            ).astype(jnp.bfloat16)
        )
    return jnp.concatenate(outputs, axis=0)


def attend_back(packed, proj):
    queries, key_rows, val_rows, doc_ids, block_sets, d_out = packed
    length = queries.shape[0]
    step_rows = min(512, length)
    head_dim = queries.shape[-1]
    query_full = feature_map(queries, proj)
    key_full = feature_map(key_rows, proj)
    query_feature_rows = query_full.astype(jnp.bfloat16)
    key_feature_rows = key_full.astype(jnp.bfloat16)
    key_grad = jnp.zeros(key_rows.shape, jnp.float32)
    val_grad = jnp.zeros(val_rows.shape, jnp.float32)
    kfeat_grad = jnp.zeros(key_full.shape, jnp.float32)
    query_parts = []
    qfeat_parts = []
    for offset in range(0, length, step_rows):
        upper = offset + step_rows
        query_blk = queries[offset:upper]
        query_feature_block = query_feature_rows[offset:upper]
        dout_blk = d_out[offset:upper]
        exp_score, sparse, other_mask, combined, row_sum = block_terms(
            query_blk,
            key_rows,
            query_feature_block,
            key_feature_rows,
            doc_ids[offset:upper],
            doc_ids,
            block_sets[:, offset // BLK : upper // BLK],
        )
        normed = combined / row_sum
        weights = normed.astype(jnp.bfloat16)
        val_grad = val_grad + jnp.einsum(
            "hrk,rhe->khe", weights, dout_blk, preferred_element_type=jnp.float32
        )
        d_weights = jnp.einsum(
            "rhe,khe->hrk", dout_blk, val_rows, preferred_element_type=jnp.float32
        )
        d_weights = d_weights.astype(jnp.bfloat16).astype(jnp.float32)
        d_comb = (d_weights - jnp.sum(d_weights * normed, axis=2, keepdims=True)) / row_sum
        d_score = (d_comb * sparse * exp_score).astype(jnp.bfloat16)
        lowrank_estimate_grad = (d_comb * other_mask).astype(jnp.bfloat16)
        query_parts.append(
            jnp.einsum("hrk,khe->rhe", d_score, key_rows, preferred_element_type=jnp.float32)
            * head_dim ** (-0.5)
        )
        key_grad = key_grad + jnp.einsum(
            "hrk,rhe->khe", d_score, query_blk, preferred_element_type=jnp.float32
        ) * head_dim ** (-0.5)
        qfeat_parts.append(
            jnp.einsum(
                "qce,eqs->cqs",
                lowrank_estimate_grad,
                key_feature_rows,
                preferred_element_type=jnp.float32,
            )
        )
        kfeat_grad = kfeat_grad + jnp.einsum(
            "tic,itv->ctv",
            lowrank_estimate_grad,
            query_feature_block,
            preferred_element_type=jnp.float32,
        )
    proj_wide = proj.astype(jnp.float32)
    query_grad = jnp.concatenate(query_parts, axis=0) + feature_back(
        jnp.concatenate(qfeat_parts, axis=0), queries, query_full, proj_wide
    )
    key_grad = key_grad + feature_back(kfeat_grad, key_rows, key_full, proj_wide)
    return (
        query_grad.astype(jnp.bfloat16),
        key_grad.astype(jnp.bfloat16),
        val_grad.astype(jnp.bfloat16),
    )


def norm_backward_rows(normalized_grad, centered_partial_sum, gain_partial_sum):
    gain_gradient_total = jnp.sum(normalized_grad * centered_partial_sum, axis=0)
    shift_grad = jnp.sum(normalized_grad, axis=0)
    centered_grad = normalized_grad * gain_partial_sum
    return (
        centered_grad,
        gain_gradient_total,
        shift_grad,
        jnp.sum(centered_grad, axis=1),
        jnp.sum(centered_grad * centered_partial_sum, axis=1),
    )


def shards(
    activations,
    segment_ids,
    block_lists,
    feature_proj,
    input_norm_gain,
    input_norm_bias,
    qkv_weight,
    out_weight,
    middle_norm_gain,
    middle_norm_bias,
    up_weight,
    down_weight,
    out_grad,
):
    head_count = lax.axis_size("head")
    embedding_width = input_norm_gain.shape[0]
    feature_slice = embedding_width // head_count
    feature_begin = lax.axis_index("head") * feature_slice
    token_count = activations.shape[0]
    seq_count, seq_len = segment_ids.shape
    heads_here = block_lists.shape[1]
    head_dim = feature_proj.shape[0]
    input_full_stats = lax.all_gather(activations, "head", axis=1, tiled=True)
    centered_input, input_inverse_scale = normalize_rows(input_full_stats.astype(jnp.float32))
    normalized_input = (centered_input * input_norm_gain + input_norm_bias).astype(jnp.bfloat16)
    qkv = jnp.dot(normalized_input, qkv_weight, preferred_element_type=jnp.float32).astype(
        jnp.bfloat16
    )
    qkv = qkv.reshape(seq_count, seq_len, heads_here, 3, head_dim)
    queries = qkv[:, :, :, 0]
    key_rows = qkv[:, :, :, 1]
    val_rows = qkv[:, :, :, 2]
    query_feature_rows = jax.vmap(partial(feature_map, proj=feature_proj))(queries).astype(
        jnp.bfloat16
    )
    key_feature_rows = jax.vmap(partial(feature_map, proj=feature_proj))(key_rows).astype(
        jnp.bfloat16
    )
    heads_out = lax.map(
        attend,
        (
            queries,
            key_rows,
            val_rows,
            query_feature_rows,
            key_feature_rows,
            segment_ids,
            block_lists,
        ),
    )
    heads_flat = heads_out.reshape(token_count, heads_here * head_dim)
    branch_part = jnp.dot(heads_flat, out_weight, preferred_element_type=jnp.float32)
    branch = lax.psum_scatter(branch_part, "head", scatter_dimension=1, tiled=True)
    resid = activations.astype(jnp.float32) + branch
    middle_full_stats = lax.all_gather(resid.astype(jnp.bfloat16), "head", axis=1, tiled=True)
    centered_middle, middle_inverse_scale = normalize_rows(middle_full_stats.astype(jnp.float32))
    normalized_middle = (centered_middle * middle_norm_gain + middle_norm_bias).astype(jnp.bfloat16)
    pre_act = jnp.dot(normalized_middle, up_weight, preferred_element_type=jnp.float32)
    gelu_exact = partial(jax.nn.gelu, approximate=False)
    act_full, gelu_pull = jax.vjp(gelu_exact, pre_act)
    acted = act_full.astype(jnp.bfloat16)
    mlp_part = jnp.dot(acted, down_weight, preferred_element_type=jnp.float32)
    mlp_out = lax.psum_scatter(
        mlp_part.astype(jnp.bfloat16), "head", scatter_dimension=1, tiled=True
    ).astype(jnp.float32)
    block_out = (resid + mlp_out).astype(jnp.bfloat16)
    gathered = lax.all_gather(out_grad, "head", axis=1, tiled=True)
    down_grad = jnp.zeros((down_weight.shape[0], embedding_width), jnp.float32)
    columns = down_weight
    d_acted = lax.dot_general(
        gathered, columns, (((1,), (1,)), ((), ())), preferred_element_type=jnp.float32
    )
    block_grad = lax.dot_general(
        acted, gathered, (((0,), (0,)), ((), ())), preferred_element_type=jnp.float32
    )
    d_acted, down_grad = (
        d_acted,
        lax.dynamic_update_slice_in_dim(down_grad, block_grad, jnp.int32(0), 1),
    )
    d_pre = gelu_pull(d_acted)[0].astype(jnp.bfloat16)
    up_grad = lax.dot_general(
        normalized_middle, d_pre, (((0,), (0,)), ((), ())), preferred_element_type=jnp.float32
    )
    d_mid_part = lax.dot_general(
        d_pre, up_weight, (((1,), (1,)), ((), ())), preferred_element_type=jnp.float32
    )
    normalized_middle_grad = lax.psum_scatter(d_mid_part, "head", scatter_dimension=1, tiled=True)
    centered_middle_partial = lax.dynamic_slice_in_dim(
        centered_middle, feature_begin, feature_slice, 1
    )
    middle_gain_partial = lax.dynamic_slice_in_dim(
        middle_norm_gain, feature_begin, feature_slice, 0
    )
    (
        centered_middle_grad,
        middle_norm_gain_gradient,
        middle_norm_bias_gradient,
        middle_first_moment,
        middle_second_moment,
    ) = norm_backward_rows(normalized_middle_grad, centered_middle_partial, middle_gain_partial)
    middle_first_moment, middle_second_moment = lax.psum(
        (middle_first_moment, middle_second_moment), "head"
    )
    d_mid = middle_inverse_scale * (
        centered_middle_grad
        - middle_first_moment[:, None] / embedding_width
        - centered_middle_partial * middle_second_moment[:, None] / embedding_width
    )
    d_resid = out_grad.astype(jnp.float32) + d_mid
    gathered = lax.all_gather(d_resid.astype(jnp.bfloat16), "head", axis=1, tiled=True)
    offset = jnp.int32(0)
    d_heads = jnp.zeros((token_count, heads_here * head_dim), jnp.float32)
    out_grad_w = jnp.zeros((heads_here * head_dim, embedding_width), jnp.float32)
    piece_width = gathered.shape[1]
    columns = lax.dynamic_slice_in_dim(out_weight, offset, piece_width, 1)
    d_heads = d_heads + lax.dot_general(
        gathered, columns, (((1,), (1,)), ((), ())), preferred_element_type=jnp.float32
    )
    block_grad = lax.dot_general(
        heads_flat, gathered, (((0,), (0,)), ((), ())), preferred_element_type=jnp.float32
    )
    d_heads, out_weight_grad = (
        d_heads,
        lax.dynamic_update_slice_in_dim(out_grad_w, block_grad, offset, 1),
    )
    d_heads = d_heads.astype(jnp.bfloat16).reshape(seq_count, seq_len, heads_here, head_dim)
    query_grad, key_grad, val_grad = lax.map(
        partial(attend_back, proj=feature_proj),
        (queries, key_rows, val_rows, segment_ids, block_lists, d_heads),
    )
    d_qkv = jnp.stack([query_grad, key_grad, val_grad], axis=3).reshape(
        token_count, heads_here * 3 * head_dim
    )
    qkv_grad = lax.dot_general(
        normalized_input, d_qkv, (((0,), (0,)), ((), ())), preferred_element_type=jnp.float32
    )
    d_in_part = lax.dot_general(
        d_qkv, qkv_weight, (((1,), (1,)), ((), ())), preferred_element_type=jnp.float32
    )
    normalized_input_grad = lax.psum_scatter(
        d_in_part.astype(jnp.bfloat16), "head", scatter_dimension=1, tiled=True
    ).astype(jnp.float32)
    centered_input_partial = lax.dynamic_slice_in_dim(
        centered_input, feature_begin, feature_slice, 1
    )
    input_gain_partial = lax.dynamic_slice_in_dim(input_norm_gain, feature_begin, feature_slice, 0)
    (
        centered_input_grad,
        input_gain_gradient,
        input_bias_gradient,
        input_first_moment,
        input_second_moment,
    ) = norm_backward_rows(normalized_input_grad, centered_input_partial, input_gain_partial)
    input_first_moment, input_second_moment = lax.psum(
        (input_first_moment, input_second_moment), "head"
    )
    d_in = input_inverse_scale * (
        centered_input_grad
        - input_first_moment[:, None] / embedding_width
        - centered_input_partial * input_second_moment[:, None] / embedding_width
    )
    input_grad = d_resid + d_in
    (
        input_gain_gradient,
        input_bias_gradient,
        qkv_grad,
        out_weight_grad,
        middle_norm_gain_gradient,
        middle_norm_bias_gradient,
        up_grad,
        down_grad,
    ) = lax.psum(
        (
            input_gain_gradient,
            input_bias_gradient,
            qkv_grad,
            out_weight_grad,
            middle_norm_gain_gradient,
            middle_norm_bias_gradient,
            up_grad,
            down_grad,
        ),
        "row",
    )
    return (
        block_out,
        input_grad,
        input_gain_gradient,
        input_bias_gradient,
        qkv_grad,
        out_weight_grad,
        middle_norm_gain_gradient,
        middle_norm_bias_gradient,
        up_grad,
        down_grad,
    )


def solution(mesh):
    return jax.shard_map(
        shards,
        mesh=mesh,
        in_specs=(
            P("row", "head"),
            P("row", None),
            P("row", "head", None, None),
            P(),
            P(),
            P(),
            P(None, "head"),
            P("head", None),
            P(),
            P(),
            P(None, "head"),
            P("head", None),
            P("row", "head"),
        ),
        out_specs=(
            P("row", "head"),
            P("row", "head"),
            P("head"),
            P("head"),
            P(None, "head"),
            P("head", None),
            P("head"),
            P("head"),
            P(None, "head"),
            P("head", None),
        ),
        check_vma=False,
    )
```

profile of v0, /device:TPU:0, one launch (start us, length us, event | category | flops | bytes accessed | tf_op | source)
XLA Modules:
  0.0 1242.0 jit_solution(8289489062593593043)
XLA Ops:
  8.0 67.8 %all-gather.5.cloned.1.call-done = bf16[2048,768]{0,1:T(8,128)(2,1)} async-done(((bf16[2048,192]{0,1:T(8,128)(2,1)}), bf16[2048,768]{0,1:T(8,128)(2,1)}) %all-gather.5.cloned.1.call-update) | async-done | bytes 3145744 | tf_op jit(solution)/shard_map/all_gather | solution.py:199
  83.8 5.6 reshape.260
  102.9 128.8 %while.24 = (s32[]{:T(128)}, bf16[2,1024,3,64]{1,3,2,0:T(8,128)(2,1)}, bf16[2,1024,3,64]{1,3,2,0:T(8,128)(2,1)}, s32[2,3,16,4]{2,3,1,0:T(4,128)}, s32[2,1024]{1,...) while((s32[]{:T(128)}, ...), condition=%wide.region_9.10_spmd, body=%wide.region_4.9_spmd.sunk | while | flops 2447316992 | bytes 135865424 | solution.py:215
  114.5 5.4 broadcast_in_dim.25
  119.9 11.6 reshape.271
  131.5 8.1 fusion.254
  140.7 5.4 broadcast_in_dim.24
  146.1 11.6 reshape.270
  157.7 7.5 fusion.251
  178.8 5.4 broadcast_in_dim.25
  184.2 11.6 reshape.271
  195.7 8.1 fusion.254
  205.0 5.4 broadcast_in_dim.24
  210.4 11.6 reshape.270
  221.9 7.5 fusion.251
  238.6 109.5 %reduce-scatter.5.cloned.1.call-done = f32[2048,192]{0,1:T(8,128)} async-done(((f32[2048,768]{0,1:T(8,128)}), f32[2048,192]{0,1:T(8,128)}) %reduce-scatter.5.cloned.1.call-update) | async-done | bytes 1572880 | tf_op jit(solution)/shard_map/reduce_scatter | solution.py:229
  351.2 63.5 %all-gather.7.cloned.1.call-done = bf16[2048,768]{0,1:T(8,128)(2,1)} async-done(((bf16[2048,192]{0,1:T(8,128)(2,1)}), bf16[2048,768]{0,1:T(8,128)(2,1)}) %all-gather.7.cloned.1.call-update) | async-done | bytes 3145744 | tf_op jit(solution)/shard_map/all_gather | solution.py:231
  418.5 5.3 fusion.140
  423.8 54.6 %all-gather.9.cloned.1.call-done = bf16[2048,768]{0,1:T(8,128)(2,1)} async-done(((bf16[2048,192]{0,1:T(8,128)(2,1)}), bf16[2048,768]{0,1:T(8,128)(2,1)}) %all-gather.9.cloned.1.call-update) | async-done | bytes 3145744 | tf_op jit(solution)/shard_map/all_gather | solution.py:243
  478.4 19.5 %add_convert_fusion.1 = (bf16[2048,768]{1,0:T(8,128)(2,1)S(1)}, f32[2048,768]{1,0:T(8,128)}) fusion(f32[2048,768]{1,0:T(8,128)} %fusion.140, bf16[2048,768]{0,1:T(8,128)(2,1)} %all-gather.9.cloned.1.call-done, bf16[768,768]{1,0:T(8,128)(2,1)S(1)} %copy-done), kind=kOutput, calls=%fused_computation.190 | convolution fusion | flops 2529165312 | bytes 20054016 | tf_op jit(solution)/shard_map/dot_general | solution.py:246
  504.7 6.1 fusion.117
  510.9 102.9 %reduce-scatter.9.cloned.1.call-done = f32[2048,192]{0,1:T(8,128)} async-done(((f32[2048,768]{0,1:T(8,128)}), f32[2048,192]{0,1:T(8,128)}) %reduce-scatter.9.cloned.1.call-update) | async-done | bytes 1572880 | tf_op jit(solution)/shard_map/reduce_scatter | solution.py:263
  616.9 19.2 %all-reduce.3 = (f32[2048]{0:T(1024)S(1)}, f32[2048]{0:T(1024)}) all-reduce(f32[2048]{0:T(1024)} %get-tuple-element.154, f32[2048]{0:T(1024)} %get-tuple-element.157), channel_id=1, replica_groups=mesh['row'=8,'head'=4] {'head'}, use_global_device_ids=true, to_apply=%region_18.19 | all-reduce | flops 4096 | bytes 32768 | tf_op jit(solution)/shard_map/psum | solution.py:277
  640.3 5.5 multiply_convert_fusion.4
  651.6 50.7 %all-gather.11.cloned.1.call-done = bf16[2048,768]{0,1:T(8,128)(2,1)} async-done(((bf16[2048,192]{0,1:T(8,128)(2,1)}), bf16[2048,768]{0,1:T(8,128)(2,1)}) %all-gather.11.cloned.1.call-update) | async-done | bytes 3145744 | tf_op jit(solution)/shard_map/all_gather | solution.py:286
  711.7 329.9 %while.25 = (s32[]{:T(128)}, bf16[2,1024,3,64]{1,3,2,0:T(8,128)(2,1)}, bf16[2,1024,3,64]{1,3,2,0:T(8,128)(2,1)}, bf16[2,1024,3,64]{1,3,2,0:T(8,128)(2,1)}, bf16[...) while((s32[]{:T(128)}, ...), condition=%wide.region_30.31_spmd, body=%wide.region_19.30_spmd.sunk | while | flops 8363453440 | bytes 391725568 | solution.py:303
  759.6 5.4 broadcast_in_dim.48
  765.0 11.6 reshape.273
  776.6 8.6 fusion.289
  785.2 20.7 %multiply_convert_fusion.10 = (bf16[3,512,1024]{2,1,0:T(8,128)(2,1)}, bf16[3,512,1024]{2,1,0:T(8,128)(2,1)}) fusion(f32[3,512,1024]{2,1,0:T(8,128)} %fusion.288, f32[3,512,1024]{2,1,0:T(8,128)} %reshape.273, f32[512,1024]{1,0:T(8,128)} %get-tuple-element.443, f32[3,512]{1,0:T(4,128)S(1)} %get-tuple-element.444, ...), kind=kOutput, calls=%fused_computation.60.clone.1 | output fusion | flops 22022656 | bytes 30414848 | tf_op jit(solution)/shard_map/while/body/eval_jaxpr/sub | solution.py:127
  816.9 5.4 broadcast_in_dim.26
  822.3 11.6 reshape.272
  833.9 8.6 fusion.286
  842.5 21.0 %multiply_convert_fusion.9 = (bf16[3,512,1024]{2,1,0:T(8,128)(2,1)}, bf16[3,512,1024]{2,1,0:T(8,128)(2,1)}) fusion(f32[3,512,1024]{2,1,0:T(8,128)} %fusion.284, f32[3,512,1024]{2,1,0:T(8,128)} %reshape.272, f32[512,1024]{1,0:T(8,128)} %get-tuple-element.437, f32[3,512]{1,0:T(4,128)S(1)} %get-tuple-element.439, ...), kind=kOutput, calls=%fused_computation.57.clone.1 | output fusion | flops 22022656 | bytes 30414848 | tf_op jit(solution)/shard_map/while/body/eval_jaxpr/sub | solution.py:127
  912.0 5.4 broadcast_in_dim.48
  917.4 11.6 reshape.273
  928.9 8.6 fusion.289
  937.5 20.7 %multiply_convert_fusion.10 = (bf16[3,512,1024]{2,1,0:T(8,128)(2,1)}, bf16[3,512,1024]{2,1,0:T(8,128)(2,1)}) fusion(f32[3,512,1024]{2,1,0:T(8,128)} %fusion.288, f32[3,512,1024]{2,1,0:T(8,128)} %reshape.273, f32[512,1024]{1,0:T(8,128)} %get-tuple-element.443, f32[3,512]{1,0:T(4,128)S(1)} %get-tuple-element.444, ...), kind=kOutput, calls=%fused_computation.60.clone.1 | output fusion | flops 22022656 | bytes 30414848 | tf_op jit(solution)/shard_map/while/body/eval_jaxpr/sub | solution.py:127
  969.3 5.4 broadcast_in_dim.26
  974.7 11.6 reshape.272
  986.2 8.6 fusion.286
  994.8 21.0 %multiply_convert_fusion.9 = (bf16[3,512,1024]{2,1,0:T(8,128)(2,1)}, bf16[3,512,1024]{2,1,0:T(8,128)(2,1)}) fusion(f32[3,512,1024]{2,1,0:T(8,128)} %fusion.284, f32[3,512,1024]{2,1,0:T(8,128)} %reshape.272, f32[512,1024]{1,0:T(8,128)} %get-tuple-element.437, f32[3,512]{1,0:T(4,128)S(1)} %get-tuple-element.439, ...), kind=kOutput, calls=%fused_computation.57.clone.1 | output fusion | flops 22022656 | bytes 30414848 | tf_op jit(solution)/shard_map/while/body/eval_jaxpr/sub | solution.py:127
  1051.6 7.0 fusion.154
  1068.8 5.6 fusion.115
  1077.4 32.9 %reduce-scatter.11.cloned.1.call-done = bf16[2048,192]{0,1:T(8,128)(2,1)} async-done(((bf16[2048,768]{0,1:T(8,128)(2,1)}), bf16[2048,192]{0,1:T(8,128)(2,1)}) %reduce-scatter.11.cloned.1.call-update) | async-done | bytes 786448 | tf_op jit(solution)/shard_map/reduce_scatter | solution.py:316
  1112.6 14.2 %all-reduce = (f32[192]{0:T(256)}, f32[192]{0:T(256)}, f32[192]{0:T(256)}, f32[192]{0:T(256)}) all-reduce(f32[192]{0:T(256)S(1)} %get-tuple-element.155, f32[192]{0:T(256)S(1)} %get-tuple-element.160, f32[192]{0:T(256)S(1)} %copy-done.63, f32[192]{0:T(256)S(1)} %copy-done.64), channel_id=1, replica_groups=mesh['row'=8,'head'=4] {'row'}, use_global_device_ids=true, to_apply=%region_37.38 | all-reduce | flops 768 | bytes 6144 | tf_op jit(solution)/shard_map/psum | solution.py:348
  1126.8 17.9 %all-reduce.2 = (f32[2048]{0:T(1024)S(1)}, f32[2048]{0:T(1024)S(1)}) all-reduce(f32[2048]{0:T(1024)S(1)} %get-tuple-element.156, f32[2048]{0:T(1024)S(1)} %get-tuple-element.159), channel_id=1, replica_groups=mesh['row'=8,'head'=4] {'head'}, use_global_device_ids=true, to_apply=%region_35.36 | all-reduce | flops 4096 | bytes 32768 | tf_op jit(solution)/shard_map/psum | solution.py:330
  1149.1 79.5 %all-reduce.6.cloned.1.call-done = (f32[768,576]{0,1:T(8,128)}, f32[192,768]{1,0:T(8,128)}, f32[768,768]{1,0:T(8,128)}, f32[768,768]{1,0:T(8,128)}) async-done(((f32[768,576]{0,1:T(8,128)}, f32[192,768]{1,0:T(8,128)}, f32[768,768]{1,0:T(8,128)}, f32[768,768]{1,0:T(8,128)}), (f32[768,576]{0,1:T(8,128)}, f32[192,768]{1,0:T(8,128)}, f32[768,768]{1,0:T(8,128)}, ...) | async-done | bytes 7077904 | tf_op jit(solution)/shard_map/psum | solution.py:348
  (365 shorter events, 249.0 us)
Async XLA Ops:
  7.2 471.2 %copy-start = (bf16[768,768]{1,0:T(8,128)(2,1)S(1)}, bf16[768,768]{1,0:T(8,128)(2,1)}, u32[]{:S(2)}) copy-start(bf16[768,768]{1,0:T(8,128)(2,1)} %param.28) | copy-start | bytes 3538948
  7.2 68.6 %all-gather.5.cloned.1.call-start = ((), (), s32[]{:S(2)}) async-start(), calls=%async_computation.4 | async-start | bytes 3932160 | tf_op jit(solution)/shard_map/all_gather | solution.py:199
  7.9 340.2 %reduce-scatter.5.cloned.1.call-start = ((), (), s32[]{:S(2)}) async-start(), calls=%async_computation.5 | async-start | bytes 7864320 | tf_op jit(solution)/shard_map/reduce_scatter | solution.py:229
  8.0 72.2 %copy-start.67 = (f32[768]{0:T(1024)S(1)}, f32[768]{0:T(1024)}, u32[]{:S(2)}) copy-start(f32[768]{0:T(1024)} %param.21) | copy-start | bytes 9220
  8.0 72.2 %copy-start.74 = (f32[768]{0:T(1024)S(1)}, f32[768]{0:T(1024)}, u32[]{:S(2)}) copy-start(f32[768]{0:T(1024)} %param.22) | copy-start | bytes 9220
  75.8 4.3 copy-start.70
  131.5 8.1 copy-start.20
  157.7 7.5 copy-start.21
  195.7 8.1 copy-start.20
  221.9 7.5 copy-start.21
  238.5 109.6 %copy-start.33 = (bf16[2048,192]{0,1:T(8,128)(2,1)S(1)}, bf16[2048,192]{0,1:T(8,128)(2,1)}, u32[]{:S(2)}) copy-start(bf16[2048,192]{0,1:T(8,128)(2,1)} %param.17) | copy-start | bytes 2359300
  238.5 176.2 %all-gather.7.cloned.1.call-start = ((), (), s32[]{:S(2)}) async-start(), calls=%async_computation.6 | async-start | bytes 3932160 | tf_op jit(solution)/shard_map/all_gather | solution.py:231
  350.6 127.8 %all-gather.9.cloned.1.call-start = ((), (), s32[]{:S(2)}) async-start(), calls=%async_computation.8 | async-start | bytes 3932160 | tf_op jit(solution)/shard_map/all_gather | solution.py:243
  351.2 67.3 %copy-start.65 = (f32[768]{0:T(1024)S(1)}, f32[768]{0:T(1024)}, u32[]{:S(2)}) copy-start(f32[768]{0:T(1024)} %param.25) | copy-start | bytes 9220
  351.2 67.3 %copy-start.72 = (f32[768]{0:T(1024)S(1)}, f32[768]{0:T(1024)}, u32[]{:S(2)}) copy-start(f32[768]{0:T(1024)} %param.26) | copy-start | bytes 9220
  351.2 262.6 %reduce-scatter.9.cloned.1.call-start = ((), (), s32[]{:S(2)}) async-start(), calls=%async_computation.9 | async-start | bytes 7864320 | tf_op jit(solution)/shard_map/reduce_scatter | solution.py:263
  417.6 87.1 %copy-start.57 = (f32[2048]{0:T(1024)}, f32[2048]{0:T(1024)S(1)}, u32[]{:S(2)}) copy-start(f32[2048]{0:T(1024)S(1)} %broadcast_multiply_fusion.8) | copy-start | bytes 24580
  418.5 218.3 %copy-start.49 = (f32[2048]{0:T(1024)}, f32[2048]{0:T(1024)S(1)}, u32[]{:S(2)}) copy-start(f32[2048]{0:T(1024)S(1)} %add_rsqrt_fusion) | copy-start | bytes 24580
  504.2 198.1 %all-gather.11.cloned.1.call-start = ((), (), s32[]{:S(2)}) async-start(), calls=%async_computation.10 | async-start | bytes 3932160 | tf_op jit(solution)/shard_map/all_gather | solution.py:286
  504.7 109.0 %copy-start.61 = (f32[192]{0:T(256)}, f32[192]{0:T(256)S(1)}, u32[]{:S(2)}) copy-start(f32[192]{0:T(256)S(1)} %dynamic_slice.59) | copy-start | bytes 2308
  510.9 126.6 %copy-start.31 = (bf16[2048,192]{0,1:T(8,128)(2,1)S(1)}, bf16[2048,192]{0,1:T(8,128)(2,1)}, u32[]{:S(2)}) copy-start(bf16[2048,192]{0,1:T(8,128)(2,1)} %param.29) | copy-start | bytes 2359300
  613.8 23.6 %copy-start.25 = (f32[2048,192]{0,1:T(8,128)S(1)}, f32[2048,192]{0,1:T(8,128)}, u32[]{:S(2)}) copy-start(f32[2048,192]{0,1:T(8,128)} %reduce-scatter.9.cloned.1.call-done) | copy-start | bytes 4718596
  636.1 9.7 copy-start.59
  640.3 434.1 %reduce-scatter.7.cloned.1.call-start = ((), (), s32[]{:S(2)}) async-start(), calls=%async_computation.7 | async-start | bytes 3932160 | tf_op jit(solution)/shard_map/reduce_scatter | solution.py:239
  651.6 50.8 %copy-start.47 = (bf16[192,768]{1,0:T(8,128)(2,1)S(1)}, bf16[192,768]{1,0:T(8,128)(2,1)}, u32[]{:S(2)}) copy-start(bf16[192,768]{1,0:T(8,128)(2,1)} %param.24) | copy-start | bytes 884740
  651.6 458.7 %reduce-scatter.11.cloned.1.call-start = ((), (), s32[]{:S(2)}) async-start(), calls=%async_computation.11 | async-start | bytes 3932160 | tf_op jit(solution)/shard_map/reduce_scatter | solution.py:316
  705.0 6.7 copy-start.4
  705.0 6.7 copy-start.12
  705.0 6.7 copy-start.22
  867.3 5.3 copy-start.13
  1019.6 5.3 copy-start.13
  1051.3 7.4 copy-start.50
  1051.3 7.4 copy-start.58
  1051.3 7.4 copy-start.66
  1051.3 7.3 copy-start.73
  1051.3 177.4 %all-reduce.6.cloned.1.call-start = ((), (), s32[]{:S(2)}) async-start(), calls=%async_computation.12 | async-start | bytes 14155776 | tf_op jit(solution)/shard_map/psum | solution.py:348
  1051.6 7.1 copy-start.19
  1051.6 7.1 copy-start.77
  1058.7 4.4 copy-start.27
  1058.7 4.4 copy-start.30
  1068.8 5.7 copy-start.34
  1074.3 38.3 %copy-start.63 = (f32[192]{0:T(256)S(1)}, f32[192]{0:T(256)}, u32[]{:S(2)}) copy-start(f32[192]{0:T(256)} %get-tuple-element.153) | copy-start | bytes 2308
  1074.3 38.3 %copy-start.64 = (f32[192]{0:T(256)S(1)}, f32[192]{0:T(256)}, u32[]{:S(2)}) copy-start(f32[192]{0:T(256)} %get-tuple-element.158) | copy-start | bytes 2308
  1074.3 70.4 %copy-start.26 = (f32[2048,192]{0,1:T(8,128)S(1)}, f32[2048,192]{0,1:T(8,128)}, u32[]{:S(2)}) copy-start(f32[2048,192]{0,1:T(8,128)} %reduce-scatter.9.cloned.1.call-done) | copy-start | bytes 4718596
  1074.4 70.4 %copy-start.32 = (bf16[2048,192]{0,1:T(8,128)(2,1)S(1)}, bf16[2048,192]{0,1:T(8,128)(2,1)}, u32[]{:S(2)}) copy-start(bf16[2048,192]{0,1:T(8,128)(2,1)} %param.29) | copy-start | bytes 2359300
  1074.4 70.4 %copy-start.56 = (f32[2048]{0:T(1024)S(1)}, f32[2048]{0:T(1024)}, u32[]{:S(2)}) copy-start(f32[2048]{0:T(1024)} %copy-done.55) | copy-start | bytes 24580
  1074.4 70.4 %copy-start.60 = (f32[2048]{0:T(1024)S(1)}, f32[2048]{0:T(1024)}, u32[]{:S(2)}) copy-start(f32[2048]{0:T(1024)} %copy-done.59) | copy-start | bytes 24580
  1074.4 70.4 %copy-start.62 = (f32[192]{0:T(256)S(1)}, f32[192]{0:T(256)}, u32[]{:S(2)}) copy-start(f32[192]{0:T(256)} %copy-done.61) | copy-start | bytes 2308
  (64 other events, 147.9 us)
Sparse Core Ops, SparseCore 0:
  9.6 66.1 all-gather.4
  238.7 109.3 reduce-scatter.4
  350.7 64.0 all-gather.6
  416.2 62.1 all-gather.8
  504.3 109.3 reduce-scatter.8
  640.4 61.8 all-gather.10
  704.6 58.8 reduce-scatter.6
  1051.4 58.8 reduce-scatter.10
  1115.2 113.4 all-reduce.5
where the time goes:
time: 1250 us; the launch traced here: 1240 us
  waiting for transfers between devices  563 us (45%)
  matrix products  254 us (20%)
  local copies, waits for them, and re-layouts  193 us (15%)
  other arithmetic  139 us (11%)
  blocking collectives  51.3 us (4%)
  loops' own time  26.2 us (2%)
  between operations  14.6 us (1%)
    reduce_scatter x1, waiting for transfers between devices, shards(): lax.psum_scatter(branch_part, 'head', scatter_dimension=1, tiled=True)  110 us
    reduce_scatter x1, waiting for transfers between devices, shards(): lax.psum_scatter(d_mid_part, 'head', scatter_dimension=1, tiled=True)  103 us
    reshape x8, local copies, waits for them, and re-layouts, block_terms(): spread_hits.reshape(heads_here, row_blocks * BLK, key_blocks * BLK)  92.6 us
    sub x4, other arithmetic, attend_back(): d_weights - jnp.sum(d_weights * normed, axis=2, keepdims=True)  83.6 us
    psum x1, waiting for transfers between devices, shards(): lax.psum((input_gain_gradient, input_bias_gradient, qkv_grad, out_weight_...  79.5 us
    all_gather x1, waiting for transfers between devices, shards(): input_full_stats = lax.all_gather(activations, 'head', axis=1, tiled=True)  67.8 us
    dot_general x8, matrix products, block_terms(): jnp.einsum('ewm,qwm->weq', query_feature_block, key_feature_rows, preferr...  65.5 us
    all_gather x1, waiting for transfers between devices, shards(): lax.all_gather(resid.astype(jnp.bfloat16), 'head', axis=1, tiled=True)  63.5 us
  transfers between devices with their start and end apart: 9, of which 8 were waited for; matrix products, arithmetic and copies ran while one was open for 30% of the time, Pallas kernels for 0%

commit v1 on v0

v1 whole, which is shorter than its diff:
```python
from functools import partial

import math
import jax, jax.numpy as jnp
from jax import lax
from jax.experimental import pallas as pl
from jax.experimental.pallas import tpu as pltpu

BLK = 64
LOG2E = 1.4426950408889634

def dot(a, b, dims):
    return lax.dot_general(a, b, (dims, ((), ())), preferred_element_type=jnp.float32)

def key_span(seg_ref, first_row, rows, tk, length):
    first = seg_ref[0, first_row]
    last = seg_ref[0, first_row + rows - 1]
    lo = jnp.int32(0)
    hi = jnp.int32(0)
    for j in range(length // tk):
        lo += (seg_ref[0, j * tk + tk - 1] < first).astype(jnp.int32)
        hi += (seg_ref[0, j * tk] <= last).astype(jnp.int32)
    return lo, hi

def fwd_kernel(seg_s, qkv_ref, segc_ref, segr_ref, hit_ref, proj_ref,
               out_ref, qf_ref, kf_ref, rinv_ref, vext, *, tq, tk, dh):
    length = qkv_ref.shape[0]
    feats = proj_ref.shape[1]
    quarter = dh ** (-0.25)
    nh = 2
    for h in range(nh):
        base = h * 3 * dh
        for j, f_ref in ((0, qf_ref), (1, kf_ref)):
            def feat_body(i, _, base=base, j=j, f_ref=f_ref, h=h):
                rows = pl.ds(pl.multiple_of(i * 256, 256), 256)
                t = qkv_ref[rows, base + j * dh: base + (j + 1) * dh]
                lin = dot(t, proj_ref[...], ((1,), (0,)))
                tw = t.astype(jnp.float32)
                sq = jnp.sum(tw * tw, axis=1, keepdims=True) * (0.5 * quarter * quarter * LOG2E) + 0.5 * math.log2(feats)
                f_ref[h, rows, :] = jnp.exp2(lin * (quarter * LOG2E) - sq).astype(jnp.bfloat16)
                return 0
            lax.fori_loop(0, length // 256, feat_body, 0)
        v = qkv_ref[:, base + 2 * dh: base + 3 * dh]
        lane = lax.broadcasted_iota(jnp.int32, (length, dh), 1)
        vext[h, :, :] = jnp.concatenate([v, (lane < 1).astype(jnp.bfloat16)], axis=1)

    def q_body(i, _):
        r0 = pl.multiple_of(i * tq, tq)
        lo, hi = key_span(seg_s, r0, tq, tk, length)
        qs = [qkv_ref[pl.ds(r0, tq), h * 3 * dh: h * 3 * dh + dh] for h in range(nh)]
        qfs = [qf_ref[h, pl.ds(r0, tq), :] for h in range(nh)]
        segq = segc_ref[pl.ds(r0, tq), :]
        def k_body(j, acc):
            c0 = pl.multiple_of(j * tk, tk)
            same = segq == segr_ref[:, pl.ds(c0, tk)]
            new = []
            for h in range(nh):
                k = qkv_ref[pl.ds(c0, tk), h * 3 * dh + dh: h * 3 * dh + 2 * dh]
                s = dot(qs[h], k, ((1,), (1,)))
                e = jnp.exp2(s * (LOG2E * dh ** -0.5))
                a = dot(qfs[h], kf_ref[h, pl.ds(c0, tk), :], ((1,), (1,)))
                parts = []
                for b in range(tq // BLK):
                    hit = hit_ref[h, pl.ds(i * (tq // BLK) + b, 1), pl.ds(c0, tk)] > 0.5
                    rs = slice(b * BLK, (b + 1) * BLK)
                    parts.append(jnp.where(jnp.broadcast_to(hit, (BLK, tk)), e[rs], a[rs]))
                comb = jnp.where(same, jnp.concatenate(parts, axis=0), 0.0).astype(jnp.bfloat16)
                new.append(acc[h] + dot(comb, vext[h, pl.ds(c0, tk), :], ((1,), (0,))))
            return tuple(new)
        acc = lax.fori_loop(lo, hi, k_body, tuple(jnp.zeros((tq, 2 * dh), jnp.float32) for _ in range(nh)))
        for h in range(nh):
            rinv = 1.0 / acc[h][:, dh:dh + 1]
            out_ref[pl.ds(r0, tq), h * dh:(h + 1) * dh] = (acc[h][:, :dh] * rinv).astype(jnp.bfloat16)
            rinv_ref[h, pl.ds(r0, tq), :] = rinv
        return 0
    lax.fori_loop(0, length // tq, q_body, 0)

def attn_fwd(qkv, seg, hit, proj, *, tq=256, tk=256):
    length = qkv.shape[0]
    dh, feats = proj.shape
    heads = qkv.shape[1] // (3 * dh)
    pairs = heads // 2
    seg2 = seg.reshape(1, length)
    return pl.pallas_call(
        partial(fwd_kernel, tq=tq, tk=tk, dh=dh),
        grid=(pairs,),
        in_specs=[
            pl.BlockSpec(memory_space=pltpu.SMEM),
            pl.BlockSpec((length, 6 * dh), lambda p: (0, p)),
            pl.BlockSpec((length, 1), lambda p: (0, 0)),
            pl.BlockSpec((1, length), lambda p: (0, 0)),
            pl.BlockSpec((2, length // BLK, length), lambda p: (p, 0, 0)),
            pl.BlockSpec((dh, feats), lambda p: (0, 0)),
        ],
        out_specs=[
            pl.BlockSpec((length, 2 * dh), lambda p: (0, p)),
            pl.BlockSpec((2, length, feats), lambda p: (p, 0, 0)),
            pl.BlockSpec((2, length, feats), lambda p: (p, 0, 0)),
            pl.BlockSpec((2, length, 1), lambda p: (p, 0, 0)),
        ],
        out_shape=[
            jax.ShapeDtypeStruct((length, heads * dh), jnp.bfloat16),
            jax.ShapeDtypeStruct((heads, length, feats), jnp.bfloat16),
            jax.ShapeDtypeStruct((heads, length, feats), jnp.bfloat16),
            jax.ShapeDtypeStruct((heads, length, 1), jnp.float32),
        ],
        scratch_shapes=[pltpu.VMEM((2, length, 2 * dh), jnp.bfloat16)],
        compiler_params=pltpu.CompilerParams(vmem_limit_bytes=48 * 1024 * 1024),
        cost_estimate=pl.CostEstimate(flops=6 * 10**9, bytes_accessed=10**7, transcendentals=10**6),
        name="attn_fwd",
    )(seg2, qkv, seg.reshape(length, 1), seg2, hit, proj)

def bwd_kernel(seg_s, qkv_ref, segc_ref, segr_ref, hit_ref, proj_ref, pext_ref, qf_ref, kf_ref, rinv_ref, o_ref, do_ref,
               dqkv_ref, vext, doext, dq, dk, dv, dqf, dkf, *, tq, tk, dh):
    length = qkv_ref.shape[0]
    quarter = dh ** (-0.25)
    nh = 2
    lane = lax.broadcasted_iota(jnp.int32, (length, dh), 1)
    for h in range(nh):
        base = h * 3 * dh
        v = qkv_ref[:, base + 2 * dh: base + 3 * dh]
        vext[h, :, :] = jnp.concatenate([v, (lane < 2).astype(jnp.bfloat16)], axis=1)
        d_o = do_ref[:, h * dh:(h + 1) * dh].astype(jnp.float32)
        o = o_ref[:, h * dh:(h + 1) * dh].astype(jnp.float32)
        rinv = rinv_ref[h]
        delta = -jnp.sum(d_o * o, axis=1, keepdims=True) * rinv
        high = delta.astype(jnp.bfloat16).astype(jnp.float32)
        low = delta - high
        tail = jnp.where(lane == 0, high, jnp.where(lane == 1, low, 0.0))
        doext[h, :, :] = jnp.concatenate([d_o * rinv, tail], axis=1).astype(jnp.bfloat16)
    dq[...] = jnp.zeros_like(dq)
    dk[...] = jnp.zeros_like(dk)
    dv[...] = jnp.zeros_like(dv)
    dqf[...] = jnp.zeros_like(dqf)
    dkf[...] = jnp.zeros_like(dkf)

    def q_body(i, _):
        r0 = pl.multiple_of(i * tq, tq)
        lo, hi = key_span(seg_s, r0, tq, tk, length)
        rows = pl.ds(r0, tq)
        segq = segc_ref[rows, :]
        def k_body(j, _):
            c0 = pl.multiple_of(j * tk, tk)
            cols = pl.ds(c0, tk)
            same = segq == segr_ref[:, cols]
            for h in range(nh):
                base = h * 3 * dh
                q = qkv_ref[rows, base: base + dh]
                k = qkv_ref[cols, base + dh: base + 2 * dh]
                qf = qf_ref[h, rows, :]
                kf = kf_ref[h, cols, :]
                s = dot(q, k, ((1,), (1,)))
                e = jnp.exp2(s * (LOG2E * dh ** -0.5))
                a = dot(qf, kf, ((1,), (1,)))
                dc = dot(doext[h, rows, :], vext[h, cols, :], ((1,), (1,)))
                dc = jnp.where(same, dc, 0.0)
                combs, dss, das = [], [], []
                for b in range(tq // BLK):
                    hit = hit_ref[h, pl.ds(i * (tq // BLK) + b, 1), cols] > 0.5
                    hit = jnp.broadcast_to(hit, (BLK, tk))
                    rs = slice(b * BLK, (b + 1) * BLK)
                    combs.append(jnp.where(hit, e[rs], a[rs]))
                    dss.append(jnp.where(hit, dc[rs] * e[rs], 0.0))
                    das.append(jnp.where(hit, 0.0, dc[rs]))
                comb = jnp.where(same, jnp.concatenate(combs, axis=0), 0.0).astype(jnp.bfloat16)
                ds = jnp.concatenate(dss, axis=0).astype(jnp.bfloat16)
                da = jnp.concatenate(das, axis=0).astype(jnp.bfloat16)
                dq[h, rows, :] += dot(ds, k, ((1,), (0,)))
                dqf[h, rows, :] += dot(da, kf, ((1,), (0,)))
                dk[h, cols, :] += dot(ds, q, ((0,), (0,)))
                dkf[h, cols, :] += dot(da, qf, ((0,), (0,)))
                dv[h, cols, :] += dot(comb, doext[h, rows, :dh], ((0,), (0,)))
            return 0
        lax.fori_loop(lo, hi, k_body, 0)
        return 0
    lax.fori_loop(0, length // tq, q_body, 0)

    for h in range(nh):
        base = h * 3 * dh
        for j, dt, dfeat, f_ref in ((0, dq, dqf, qf_ref), (1, dk, dkf, kf_ref)):
            def back(i, _, base=base, j=j, dt=dt, dfeat=dfeat, f_ref=f_ref, h=h):
                rows = pl.ds(pl.multiple_of(i * 256, 256), 256)
                dpre = dfeat[h, rows, :] * f_ref[h, rows, :].astype(jnp.float32)
                hi_ = dpre.astype(jnp.bfloat16)
                lo_ = (dpre - hi_.astype(jnp.float32)).astype(jnp.bfloat16)
                thr = dot(hi_, pext_ref[...], ((1,), (0,))) + dot(lo_, pext_ref[...], ((1,), (0,)))
                t = qkv_ref[rows, base + j * dh: base + (j + 1) * dh].astype(jnp.float32)
                g = dt[h, rows, :] * dh ** -0.5 + quarter * thr[:, :dh] - (quarter * quarter) * t * thr[:, dh:dh + 1]
                dqkv_ref[rows, base + j * dh: base + (j + 1) * dh] = g.astype(jnp.bfloat16)
                return 0
            lax.fori_loop(0, length // 256, back, 0)
        dqkv_ref[:, base + 2 * dh: base + 3 * dh] = dv[h].astype(jnp.bfloat16)

def attn_bwd(qkv, seg, hit, proj, qf, kf, rinv, o, d_o, *, tq=256, tk=256):
    length = qkv.shape[0]
    dh, feats = proj.shape
    heads = qkv.shape[1] // (3 * dh)
    pairs = heads // 2
    seg2 = seg.reshape(1, length)
    pext = jnp.concatenate([proj.T, jnp.ones((feats, 1), proj.dtype), jnp.zeros((feats, dh - 1), proj.dtype)], axis=1)
    f32 = jnp.float32
    return pl.pallas_call(
        partial(bwd_kernel, tq=tq, tk=tk, dh=dh),
        grid=(pairs,),
        in_specs=[
            pl.BlockSpec(memory_space=pltpu.SMEM),
            pl.BlockSpec((length, 6 * dh), lambda p: (0, p)),
            pl.BlockSpec((length, 1), lambda p: (0, 0)),
            pl.BlockSpec((1, length), lambda p: (0, 0)),
            pl.BlockSpec((2, length // BLK, length), lambda p: (p, 0, 0)),
            pl.BlockSpec((dh, feats), lambda p: (0, 0)),
            pl.BlockSpec((feats, 2 * dh), lambda p: (0, 0)),
            pl.BlockSpec((2, length, feats), lambda p: (p, 0, 0)),
            pl.BlockSpec((2, length, feats), lambda p: (p, 0, 0)),
            pl.BlockSpec((2, length, 1), lambda p: (p, 0, 0)),
            pl.BlockSpec((length, 2 * dh), lambda p: (0, p)),
            pl.BlockSpec((length, 2 * dh), lambda p: (0, p)),
        ],
        out_specs=pl.BlockSpec((length, 6 * dh), lambda p: (0, p)),
        out_shape=jax.ShapeDtypeStruct((length, heads * 3 * dh), jnp.bfloat16),
        scratch_shapes=[
            pltpu.VMEM((2, length, 2 * dh), jnp.bfloat16),
            pltpu.VMEM((2, length, 2 * dh), jnp.bfloat16),
            pltpu.VMEM((2, length, dh), f32),
            pltpu.VMEM((2, length, dh), f32),
            pltpu.VMEM((2, length, dh), f32),
            pltpu.VMEM((2, length, feats), f32),
            pltpu.VMEM((2, length, feats), f32),
        ],
        compiler_params=pltpu.CompilerParams(vmem_limit_bytes=48 * 1024 * 1024),
        cost_estimate=pl.CostEstimate(flops=15 * 10**9, bytes_accessed=2 * 10**7, transcendentals=10**6),
        name="attn_bwd",
    )(seg2, qkv, seg.reshape(length, 1), seg2, hit, proj, pext, qf, kf, rinv, o, d_o)

def hit_lanes(lists, length):
    nb = lists.shape[1]
    ids = lax.broadcasted_iota(jnp.int32, (1, 1, length), 2) // BLK
    out = lists[:, :, 0:1] == ids
    for s in range(1, lists.shape[2]):
        out = out | (lists[:, :, s:s + 1] == ids)
    return out.astype(jnp.float32)

from jax.sharding import PartitionSpec as P


norm_eps = 1e-05


def xor_move(value, mask, total, only=None):
    pairs = [(i, i ^ mask) for i in range(total) if only is None or only(i)]
    return lax.ppermute(value, ("row", "head"), pairs)


def own_group(i):
    return (i & 3) // 2 == (i >> 2) & 1


def far_group(i):
    return not own_group(i)


def norm_rows(values):
    center = values - jnp.mean(values, axis=1, keepdims=True)
    scale = lax.rsqrt(jnp.mean(center * center, axis=1, keepdims=True) + norm_eps)
    return center * scale, scale


def norm_back(grad, xhat, scale, gain):
    dx = grad * gain
    return scale * (
        dx - jnp.mean(dx, axis=1, keepdims=True) - xhat * jnp.mean(dx * xhat, axis=1, keepdims=True)
    )


def place(pieces, index, mask_of):
    count = len(pieces)
    out = jnp.zeros((count,) + pieces[0].shape, pieces[0].dtype)
    for d, piece in enumerate(pieces):
        out = lax.dynamic_update_index_in_dim(out, piece, index ^ d, 0)
    return out


def shards(
    activations, segment_ids, block_lists, feature_proj, input_norm_gain, input_norm_bias, qkv_weight,
    out_weight, middle_norm_gain, middle_norm_bias, up_weight, down_weight, out_grad,
):
    rows_n, heads_n = lax.axis_size("row"), lax.axis_size("head")
    total = rows_n * heads_n
    r, z = lax.axis_index("row"), lax.axis_index("head")
    c, p = r % 2, (r // 2) % 4
    groups = rows_n // 8
    width = input_norm_gain.shape[0]
    quarter = width // heads_n
    seq_count, length = segment_ids.shape
    half = length // 2
    bf16, f32 = jnp.bfloat16, jnp.float32
    local = (z // 2) == c
    par = z % 2

    def core_swap(v):
        return xor_move(v, 4, total)

    def pick(v, i, axis=0):
        return lax.dynamic_index_in_dim(v, i, axis, keepdims=False)

    def halves(own, other):
        return jnp.where(c == 0, jnp.concatenate([own, other], 0), jnp.concatenate([other, own], 0))

    def spread(v):
        v = v.reshape(seq_count, 2, half, quarter)
        keep, send = pick(v, c, 1), pick(v, 1 - c, 1)
        got = core_swap(send)
        four = halves(keep, got)
        parts = [pick(four, z)] + [xor_move(pick(four, z ^ d), d, total) for d in (1, 2, 3)]
        return place(parts, z, None).transpose(1, 0, 2).reshape(half, width)

    def collect(v):
        v = v.reshape(half, heads_n, quarter).transpose(1, 0, 2)
        parts = [pick(v, z)] + [xor_move(pick(v, z ^ d), d, total) for d in (1, 2, 3)]
        four = place(parts, z, None)
        four = four.reshape(2, seq_count, half, quarter)
        keep, send = pick(four, c), pick(four, 1 - c)
        got = core_swap(send)
        both = jnp.where(c == 0, jnp.stack([keep, got], 1), jnp.stack([got, keep], 1))
        return both.reshape(seq_count * length, quarter)

    def gather_weights(piece):
        mine = pick(piece, p)
        got1 = xor_move(mine, 1, total, own_group)
        got2 = xor_move(mine, 2, total, own_group)
        got3 = xor_move(mine, 3, total, own_group)
        same = jnp.where(local, mine, got2)
        other = jnp.where(local, got1, got3)
        same_all = [same] + [xor_move(same, 8 * d, total, far_group) for d in (1, 2, 3)]
        other_all = [other] + [xor_move(other, 8 * d, total) for d in (1, 2, 3)]
        same_full = jnp.where(local, piece, place(same_all, p, None))
        other_full = place(other_all, p, None)
        return (
            jnp.where(par == 0, same_full, other_full),
            jnp.where(par == 0, other_full, same_full),
        )

    def reduce_grads(parts):
        low = parts.astype(bf16)
        acc = pick(low, p, 1).astype(f32)
        for d in (1, 2, 3):
            acc = acc + xor_move(pick(low, p ^ d, 1), 8 * d, total).astype(f32)
        low = acc.astype(bf16)
        fin = pick(low, par).astype(f32)
        fin = fin + xor_move(pick(low, 1 - par), 1, total, own_group).astype(f32)
        fin = fin + xor_move(pick(low, par), 2, total, far_group).astype(f32)
        fin = fin + xor_move(pick(low, 1 - par), 3, total, far_group).astype(f32)
        for b in range((groups - 1).bit_length()):
            fin = fin + xor_move(fin, 32 << b, total)
        fin = fin.astype(bf16)
        swapped = core_swap(fin)
        fin = jnp.where(local, fin, swapped)
        pieces = [fin] + [xor_move(fin, 8 * d, total) for d in (1, 2, 3)]
        return place(pieces, p, None).astype(f32)

    def sum_all(v):
        for b in range((total - 1).bit_length()):
            v = v + xor_move(v, 1 << b, total)
        return lax.dynamic_slice_in_dim(v, z * quarter, quarter, 1)

    x = spread(activations).astype(f32)
    wq_a, wq_b = gather_weights(qkv_weight.reshape(4, width // 4, -1))
    wq = jnp.concatenate([wq_a.reshape(width, -1), wq_b.reshape(width, -1)], 1)
    pack = jnp.concatenate(
        [
            up_weight.reshape(4, -1, width),
            down_weight.reshape(4, -1, width),
            out_weight.reshape(4, -1, width),
        ],
        1,
    )
    mlp_a, mlp_b = gather_weights(pack)
    hid = up_weight.shape[1]
    n_up, n_down, n_out = width // 4, hid // 4, out_weight.shape[0] // 4
    up = jnp.concatenate([w[:, :n_up].reshape(width, hid) for w in (mlp_a, mlp_b)], 1)
    down = jnp.concatenate([w[:, n_up:n_up + n_down].reshape(hid, width) for w in (mlp_a, mlp_b)], 0)
    outw = jnp.concatenate([w[:, n_up + n_down:].reshape(-1, width) for w in (mlp_a, mlp_b)], 0)

    seg_other = core_swap(segment_ids)
    lists_all = lax.all_gather(block_lists, "head", axis=1, tiled=True)
    lists_other = core_swap(lists_all)
    seg = pick(halves(segment_ids, seg_other), z)
    lists = pick(halves(lists_all, lists_other), z)
    heads_here = lists.shape[0] // 2
    lists = lax.dynamic_slice_in_dim(lists, c * heads_here, heads_here, 0)
    hit = hit_lanes(lists, length)

    xhat1, scale1 = norm_rows(x)
    n1_half = (xhat1 * input_norm_gain + input_norm_bias).astype(bf16)
    n1 = halves(n1_half, core_swap(n1_half))
    qkv = jnp.dot(n1, wq, preferred_element_type=f32).astype(bf16)
    heads_out, qf, kf, rinv = attn_fwd(qkv, seg, hit, feature_proj)

    def half_sum(left, right, dims):
        own = lax.dynamic_slice_in_dim(left, c * half, half, 0)
        oth = lax.dynamic_slice_in_dim(left, (1 - c) * half, half, 0)
        away = lax.dot_general(oth, right, (dims, ((), ())), preferred_element_type=f32).astype(bf16)
        got = core_swap(away)
        return lax.dot_general(own, right, (dims, ((), ())), preferred_element_type=f32) + got.astype(f32)

    nn, nt, tn = ((1,), (0,)), ((1,), (1,)), ((0,), (0,))
    resid = x + half_sum(heads_out, outw, nn)
    xhat2, scale2 = norm_rows(resid.astype(bf16).astype(f32))
    n2_half = (xhat2 * middle_norm_gain + middle_norm_bias).astype(bf16)
    n2 = halves(n2_half, core_swap(n2_half))
    dy_half = spread(out_grad)
    dy = halves(dy_half, core_swap(dy_half))
    pre_act = jnp.dot(n2, up, preferred_element_type=f32)
    act_full, gelu_pull = jax.vjp(partial(jax.nn.gelu, approximate=False), pre_act)
    acted = act_full.astype(bf16)
    d_acted = lax.dot_general(dy, down, (nt, ((), ())), preferred_element_type=f32)
    d_pre = gelu_pull(d_acted)[0].astype(bf16)
    d_n2 = half_sum(d_pre, up, nt)
    block_half = (resid + half_sum(acted, down, nn)).astype(bf16)
    block_out = collect(block_half)
    mid_vec = jnp.stack([jnp.sum(d_n2 * xhat2, 0), jnp.sum(d_n2, 0)])
    d_resid = dy_half.astype(f32) + norm_back(d_n2, xhat2, scale2, middle_norm_gain)
    d_half = d_resid.astype(bf16)
    d_branch = halves(d_half, core_swap(d_half))
    d_heads = lax.dot_general(d_branch, outw, (nt, ((), ())), preferred_element_type=f32).astype(bf16)
    up_g = lax.dot_general(n2, d_pre, (tn, ((), ())), preferred_element_type=f32)
    down_g = lax.dot_general(acted, dy, (tn, ((), ())), preferred_element_type=f32)
    out_g = lax.dot_general(heads_out, d_branch, (tn, ((), ())), preferred_element_type=f32)
    grads = jnp.concatenate(
        [
            up_g.astype(bf16).reshape(4, n_up, 2, hid).transpose(2, 0, 1, 3),
            down_g.astype(bf16).reshape(2, 4, n_down, width),
            out_g.astype(bf16).reshape(2, 4, n_out, width),
        ],
        2,
    )
    mlp_grads = reduce_grads(grads)
    up_grad = mlp_grads[:, :n_up].reshape(width, hid)
    down_grad = mlp_grads[:, n_up:n_up + n_down].reshape(hid, width)
    out_w_grad = mlp_grads[:, n_up + n_down:].reshape(-1, width)
    mid_vec = sum_all(mid_vec)

    d_qkv = attn_bwd(qkv, seg, hit, feature_proj, qf, kf, rinv, heads_out, d_heads)
    d_n1 = half_sum(d_qkv, wq, nt)
    qkv_g = lax.dot_general(n1, d_qkv, (tn, ((), ())), preferred_element_type=f32)
    qkv_g = qkv_g.astype(bf16).reshape(4, width // 4, 2, -1).transpose(2, 0, 1, 3)
    qkv_grad = reduce_grads(qkv_g).reshape(width, -1)
    in_vec = sum_all(jnp.stack([jnp.sum(d_n1 * xhat1, 0), jnp.sum(d_n1, 0)]))
    d_in = norm_back(d_n1, xhat1, scale1, input_norm_gain)
    input_grad = collect((d_resid + d_in).astype(bf16)).astype(f32)
    return (
        block_out, input_grad, in_vec[0], in_vec[1], qkv_grad, out_w_grad, mid_vec[0], mid_vec[1], up_grad, down_grad,
    )


def solution(mesh):
    return jax.shard_map(
        shards,
        mesh=mesh,
        in_specs=(
            P("row", "head"), P("row", None), P("row", "head", None, None), P(), P(), P(), P(None, "head"),
            P("head", None), P(), P(), P(None, "head"), P("head", None), P("row", "head"),
        ),
        out_specs=(
            P("row", "head"), P("row", "head"), P("head"), P("head"), P(None, "head"), P("head", None),
            P("head"), P("head"), P(None, "head"), P("head", None),
        ),
        check_vma=False,
    )
```

time: 1250 us -> 628 us (0.50)
  waiting for transfers between devices: 563 us -> 196 us
  matrix products: 254 us -> 66.7 us
  starting transfers between devices: 0.95 us -> 132 us
  local copies, waits for them, and re-layouts: 193 us -> 73.7 us
  other arithmetic: 139 us -> 25.3 us
  Pallas kernels: 0 us -> 107 us
  blocking collectives: 51.3 us -> 15.6 us
  loops' own time: 26.2 us -> 0 us
    reduce_scatter x4 -> x0, waiting for transfers between devices: 245 us -> none  [the longest x1 110 us: shards(): lax.psum_scatter(branch_part, 'head', scatter_dimension=1, tiled=True)]
    all_gather x4 -> x0, waiting for transfers between devices: 237 us -> none  [the longest x1 67.8 us: shards(): input_full_stats = lax.all_gather(activations, 'head', axis=1, tiled=True)]
    ppermute x0 -> x74, waiting for transfers between devices: none -> 196 us  [xor_move(): return lax.ppermute(value, ('row', 'head'), pairs)]
    dot_general x66 -> x16, matrix products: 254 us -> 66.7 us  [the longest x1 20.8 us: shards(): pre_act = jnp.dot(n2, up, preferred_element_type=f32)]
    ppermute x0 -> x74, starting transfers between devices: none -> 132 us  [xor_move(): return lax.ppermute(value, ('row', 'head'), pairs)]
    pallas_call x0 -> x2, Pallas kernels: none -> 107 us  [the longest x1 64.2 us: attn_bwd(): pl.pallas_call(partial(bwd_kernel, tq=tq, tk=tk, dh=dh), grid=(pairs,), i...]
    reshape x10 -> x7, local copies, waits for them, and re-layouts: 99.6 us -> 15.5 us  [the longest x2 9.54 us: shards(): up_g.astype(bf16).reshape(4, n_up, 2, hid).transpose(2, 0, 1, 3)]
    sub x4 -> x0, other arithmetic: 83.6 us -> none  [attend_back(): d_weights - jnp.sum(d_weights * normed, axis=2, keepdims=True)]
  transfers between devices with their start and end apart: 9 -> 74, of which waited for: 8 -> 29; matrix products, arithmetic and copies ran while one was open for 30% -> 22% of each run, Pallas kernels for 0% -> 7%
where the time goes in v1:
time: 628 us; the launch traced here: 618 us
  waiting for transfers between devices  196 us (31%)
  starting transfers between devices  132 us (21%)
  Pallas kernels  107 us (17%)
  local copies, waits for them, and re-layouts  73.7 us (12%)
  matrix products  66.7 us (11%)
  other arithmetic  25.3 us (4%)
  blocking collectives  15.6 us (2%)
    ppermute x74, waiting for transfers between devices, xor_move(): return lax.ppermute(value, ('row', 'head'), pairs)  196 us
    ppermute x74, starting transfers between devices, xor_move(): return lax.ppermute(value, ('row', 'head'), pairs)  132 us
    pallas_call x1, Pallas kernels, attn_bwd(): pl.pallas_call(partial(bwd_kernel, tq=tq, tk=tk, dh=dh), grid=(pairs,), i...  64.2 us
    pallas_call x1, Pallas kernels, attn_fwd(): pl.pallas_call(partial(fwd_kernel, tq=tq, tk=tk, dh=dh), grid=(pairs,), i...  42.3 us
    dot_general x1, matrix products, shards(): pre_act = jnp.dot(n2, up, preferred_element_type=f32)  20.8 us
    unnamed x120, local copies, waits for them, and re-layouts  18.2 us
    all_gather x1, blocking collectives, shards(): lists_all = lax.all_gather(block_lists, 'head', axis=1, tiled=True)  15.6 us
  transfers between devices with their start and end apart: 74, of which 29 were waited for; matrix products, arithmetic and copies ran while one was open for 22% of the time, Pallas kernels for 7%

profile of v1, /device:TPU:0, one launch (start us, length us, event | category | flops | bytes accessed | tf_op | source)
XLA Modules:
  0.0 618.1 jit_solution(13152201952221295730)
XLA Ops:
  3.1 4.9 collective-permute-start.10
  8.0 4.1 collective-permute-start.11
  14.1 15.6 %all_gather.3 = s32[2,12,16,4]{2,3,1,0:T(4,128)S(1)} all-gather(s32[2,3,16,4]{2,3,1,0:T(4,128)S(1)} %copy-done.47), channel_id=1, replica_groups=mesh['row'=8,'head'=4] {'head'}, dimensions={1}, use_global_device_ids=true | all-gather | bytes 7680 | tf_op jit(solution)/shard_map/all_gather | solution.py:385
  48.2 4.7 collective-permute-start.16
  55.8 6.6 %collective-permute-done.12 = bf16[192,576]{1,0:T(8,128)(2,1)S(1)} collective-permute-done((bf16[192,576]{1,0:T(8,128)(2,1)S(1)}, bf16[192,576]{1,0:T(8,128)(2,1)S(1)}, u32[]{:S(2)}, u32[]{:S(2)}) %collective-permute-start.12) | collective-permute-done | bytes 221216 | tf_op jit(solution)/shard_map/ppermute | solution.py:251
  64.8 4.6 collective-permute-done.13
  72.7 4.7 collective-permute-done.14
  78.1 3.7 collective-permute-start.1
  85.4 25.6 %collective-permute-start.2 = (bf16[512,192]{0,1:T(8,128)(2,1)S(1)}, bf16[512,192]{0,1:T(8,128)(2,1)S(1)}, u32[]{:S(2)}, u32[]{:S(2)}) collective-permute-start(bf16[512,192]{0,1:T(8,128)(2,1)S(1)} %get-tuple-element.100), channel_id=1, source_target_pairs={{0,2},{1,3},{2,0},{3,1},{4,6},{5,7},{6,4},{7,5},{8,10},{9,11},{10,... | collective-permute-start | bytes 589832 | tf_op jit(solution)/shard_map/ppermute | solution.py:251
  111.1 9.7 %collective-permute-done.2 = bf16[512,192]{0,1:T(8,128)(2,1)S(1)} collective-permute-done((bf16[512,192]{0,1:T(8,128)(2,1)S(1)}, bf16[512,192]{0,1:T(8,128)(2,1)S(1)}, u32[]{:S(2)}, u32[]{:S(2)}) %collective-permute-start.2) | collective-permute-done | bytes 196640 | tf_op jit(solution)/shard_map/ppermute | solution.py:251
  122.5 5.7 collective-permute-done.3
  138.9 9.3 %collective-permute-done.22 = bf16[432,768]{1,0:T(8,128)(2,1)S(1)} collective-permute-done((bf16[432,768]{1,0:T(8,128)(2,1)S(1)}, bf16[432,768]{1,0:T(8,128)(2,1)S(1)}, u32[]{:S(2)}, u32[]{:S(2)}) %collective-permute-start.22) | collective-permute-done | bytes 663584 | tf_op jit(solution)/shard_map/ppermute | solution.py:251
  149.0 11.0 %collective-permute-done.23 = bf16[432,768]{1,0:T(8,128)(2,1)S(1)} collective-permute-done((bf16[432,768]{1,0:T(8,128)(2,1)S(1)}, bf16[432,768]{1,0:T(8,128)(2,1)S(1)}, u32[]{:S(2)}, u32[]{:S(2)}) %collective-permute-start.23) | collective-permute-done | bytes 663584 | tf_op jit(solution)/shard_map/ppermute | solution.py:251
  170.9 42.3 %attn_fwd.1 = (bf16[1024,384]{1,0:T(8,128)(2,1)S(1)}, bf16[6,1024,256]{2,1,0:T(8,128)(2,1)}, bf16[6,1024,256]{2,1,0:T(8,128)(2,1)}, f32[6,1024,1]{2,1,0:T(8,128)}) custom-call(s32[1,1024]{1,0:T(1,128)S(1)} %broadcast_select_fusion.12.seg_s.segr_ref, bf16[1024,1152]{1,0:T(8,128)(2,1)S(1)} %convolution_convert_fusion.qkv_ref, s32[1024,1]{1,0:T(8,128)S(1)} %copy.76.segc_ref, ...), custom_call_target="tpu_custom_call" | custom-call | flops 6000000000 | bytes 10000000 | tf_op jit(solution)/shard_map/attn_fwd/pallas_call | solution.py:84
  214.6 9.6 %collective-permute-start.25 = (bf16[512,768]{1,0:T(8,128)(2,1)}, bf16[512,768]{1,0:T(8,128)(2,1)}, u32[]{:S(2)}, u32[]{:S(2)}) collective-permute-start(bf16[512,768]{1,0:T(8,128)(2,1)} %convolution_convert_fusion.6), channel_id=1, source_target_pairs={{0,4},{1,5},{2,6},{3,7},{4,0},{5,1},{6,2},{7,3},{8,12},{9,13},{10,... | collective-permute-start | bytes 2359304 | tf_op jit(solution)/shard_map/ppermute | solution.py:251
  228.3 8.0 %collective-permute-start.34 = (bf16[512,192]{0,1:T(8,128)(2,1)S(1)}, bf16[512,192]{0,1:T(8,128)(2,1)S(1)}, u32[]{:S(2)}, u32[]{:S(2)}) collective-permute-start(bf16[512,192]{0,1:T(8,128)(2,1)S(1)} %get-tuple-element.89), channel_id=1, source_target_pairs={{0,2},{1,3},{2,0},{3,1},{4,6},{5,7},{6,4},{7,5},{8,10},{9,11},{10,... | collective-permute-start | bytes 589832 | tf_op jit(solution)/shard_map/ppermute | solution.py:251
  236.4 2.9 convert_reduce_fusion
  240.7 9.8 %collective-permute-done.34 = bf16[512,192]{0,1:T(8,128)(2,1)S(1)} collective-permute-done((bf16[512,192]{0,1:T(8,128)(2,1)S(1)}, bf16[512,192]{0,1:T(8,128)(2,1)S(1)}, u32[]{:S(2)}, u32[]{:S(2)}) %collective-permute-start.34) | collective-permute-done | bytes 196640 | tf_op jit(solution)/shard_map/ppermute | solution.py:251
  255.5 20.8 %multiply_convert_fusion = (bf16[1024,1536]{1,0:T(8,128)(2,1)S(1)}, f32[1024,1536]{1,0:T(8,128)}, f32[1024,1536]{1,0:T(8,128)}) fusion(bf16[768,768]{1,0:T(8,128)(2,1)S(1)} %bitcast.260, bf16[768,768]{1,0:T(8,128)(2,1)S(1)} %bitcast.257, bf16[512,768]{1,0:T(8,128)(2,1)} %collective-permute-done.26, bf16[512,768]{1,0:T(8,128)(2,1)S(1)} %fusion.16, pred[]{:T(512)S(6)} %eq.42), kind=kOutput, calls=%fused_computation.3 | convolution fusion | flops 2529951744 | bytes 19660800 | tf_op jit(solution)/shard_map/dot_general | solution.py:413
  278.3 8.7 %add_convert_fusion = bf16[1024,1536]{1,0:T(8,128)(2,1)S(1)} fusion(f32[1024,1536]{1,0:T(8,128)} %get-tuple-element.53, f32[1024,1536]{1,0:T(8,128)} %get-tuple-element.116, bf16[768,768]{1,0:T(8,128)(2,1)S(1)} %bitcast.267, bf16[768,768]{1,0:T(8,128)(2,1)S(1)} %bitcast.264, bf16[512,768]{1,0:T(8,128)(2,1)S(1)} %collective-permute-done.36, ...), kind=kOutput, calls=%fused_computation.2 | convolution fusion | flops 2449735680 | bytes 19660800 | tf_op jit(solution)/shard_map/dot_general | solution.py:416
  289.4 4.1 convolution_convert_fusion.1
  299.3 4.4 collective-permute-start.28
  306.2 4.2 fusion.21
  311.5 5.6 collective-permute-done.69
  317.1 3.5 collective-permute-start.70
  320.7 3.9 collective-permute-done.70
  331.3 5.3 convolution_convert_fusion.2
  336.6 6.2 reshape.256
  342.8 3.4 copy.120
  354.1 64.2 %attn_bwd.1 = bf16[1024,1152]{1,0:T(8,128)(2,1)S(1)} custom-call(s32[1,1024]{1,0:T(1,128)S(1)} %broadcast_select_fusion.12.seg_s.segr_ref, bf16[1024,1152]{1,0:T(8,128)(2,1)} %copy-done.3, s32[1024,1]{1,0:T(8,128)S(1)} %copy.76.segc_ref, s32[1,1024]{1,0:T(1,128)S(1)} %broadcast_select_fusion.12.seg_s.segr_ref, f32[6,16,1024]{2,1,0:T(8,128)S(1)} %or_convert_fusion.hit_ref, ...), custom_call_target="tpu_custom_call" | custom-call | flops 15000000512 | bytes 20000000 | tf_op jit(solution)/shard_map/attn_bwd/pallas_call | solution.py:202
  422.0 3.2 reshape.253
  425.2 3.0 constant_dynamic-slice_fusion.7
  436.3 7.0 %collective-permute-done.51 = bf16[2,192,576]{2,1,0:T(8,128)(2,1)S(1)} collective-permute-done((bf16[2,192,576]{2,1,0:T(8,128)(2,1)S(1)}, bf16[2,192,576]{2,1,0:T(8,128)(2,1)S(1)}, u32[]{:S(2)}, u32[]{:S(2)}) %collective-permute-start.51) | collective-permute-done | bytes 442400 | tf_op jit(solution)/shard_map/ppermute | solution.py:251
  443.3 9.7 %collective-permute-done.50 = bf16[2,192,576]{2,1,0:T(8,128)(2,1)S(1)} collective-permute-done((bf16[2,192,576]{2,1,0:T(8,128)(2,1)S(1)}, bf16[2,192,576]{2,1,0:T(8,128)(2,1)S(1)}, u32[]{:S(2)}, u32[]{:S(2)}) %collective-permute-start.50) | collective-permute-done | bytes 442400 | tf_op jit(solution)/shard_map/ppermute | solution.py:251
  466.0 3.6 collective-permute-done.53
  472.8 3.6 collective-permute-done.44
  476.5 4.5 collective-permute-done.45
  483.3 37.3 %collective-permute-done.47 = f32[2,768]{1,0:T(2,128)S(1)} collective-permute-done((f32[2,768]{1,0:T(2,128)S(1)}, f32[2,768]{1,0:T(2,128)S(1)}, u32[]{:S(2)}, u32[]{:S(2)}) %collective-permute-start.47) | collective-permute-done | bytes 6176 | tf_op jit(solution)/shard_map/ppermute | solution.py:251
  524.2 3.8 collective-permute-start.40
  529.0 3.2 fusion.8
  533.6 3.6 collective-permute-start.62
  538.7 3.4 collective-permute-start.42
  542.9 10.9 %collective-permute-done.64 = bf16[432,768]{1,0:T(8,128)(2,1)S(1)} collective-permute-done((bf16[432,768]{1,0:T(8,128)(2,1)S(1)}, bf16[432,768]{1,0:T(8,128)(2,1)S(1)}, u32[]{:S(2)}, u32[]{:S(2)}) %collective-permute-start.64) | collective-permute-done | bytes 663584 | tf_op jit(solution)/shard_map/ppermute | solution.py:251
  554.8 19.5 %collective-permute-done.63 = bf16[432,768]{1,0:T(8,128)(2,1)S(1)} collective-permute-done((bf16[432,768]{1,0:T(8,128)(2,1)S(1)}, bf16[432,768]{1,0:T(8,128)(2,1)S(1)}, u32[]{:S(2)}, u32[]{:S(2)}) %collective-permute-start.63) | collective-permute-done | bytes 663584 | tf_op jit(solution)/shard_map/ppermute | solution.py:251
  583.9 3.0 copy.97
  590.7 3.4 reshape.263
  594.1 3.4 collective-permute-done.66
  598.6 13.2 %collective-permute-done.67 = bf16[432,768]{1,0:T(8,128)(2,1)} collective-permute-done((bf16[432,768]{1,0:T(8,128)(2,1)}, bf16[432,768]{1,0:T(8,128)(2,1)}, u32[]{:S(2)}, u32[]{:S(2)}) %collective-permute-start.67) | collective-permute-done | bytes 663584 | tf_op jit(solution)/shard_map/ppermute | solution.py:251
  (377 shorter events, 158.8 us)
Async XLA Ops:
  3.1 45.1 %collective-permute-start.10 = (bf16[192,576]{1,0:T(8,128)(2,1)}, bf16[192,576]{1,0:T(8,128)(2,1)}, u32[]{:S(2)}, u32[]{:S(2)}) collective-permute-start(bf16[192,576]{1,0:T(8,128)(2,1)} %dynamic-slice_bitcast_fusion.12), channel_id=1, source_target_pairs={{0,1},{1,0},{6,7},{7,6},{8,9},{9,8},{14,15},{15,14},{16,17},{17,16... | collective-permute-start | bytes 663560 | tf_op jit(solution)/shard_map/ppermute | solution.py:251
  8.0 44.8 %collective-permute-start.11 = (bf16[192,576]{1,0:T(8,128)(2,1)}, bf16[192,576]{1,0:T(8,128)(2,1)}, u32[]{:S(2)}, u32[]{:S(2)}) collective-permute-start(bf16[192,576]{1,0:T(8,128)(2,1)} %dynamic-slice_bitcast_fusion.12), channel_id=1, source_target_pairs={{0,3},{1,2},{6,5},{7,4},{8,11},{9,10},{14,13},{15,12},{16,19},{17,... | collective-permute-start | bytes 663560 | tf_op jit(solution)/shard_map/ppermute | solution.py:251
  12.1 35.8 %collective-permute-start.6 = (bf16[192,576]{1,0:T(8,128)(2,1)}, bf16[192,576]{1,0:T(8,128)(2,1)}, u32[]{:S(2)}, u32[]{:S(2)}) collective-permute-start(bf16[192,576]{1,0:T(8,128)(2,1)} %dynamic-slice_bitcast_fusion.12), channel_id=1, source_target_pairs={{0,2},{1,3},{6,4},{7,5},{8,10},{9,11},{14,12},{15,13},{16,18},{17,... | collective-permute-start | bytes 663560 | tf_op jit(solution)/shard_map/ppermute | solution.py:251
  14.1 31.3 %collective-permute-start.4 = (s32[2,1024]{1,0:T(2,128)S(1)}, s32[2,1024]{1,0:T(2,128)S(1)}, u32[]{:S(2)}, u32[]{:S(2)}) collective-permute-start(s32[2,1024]{1,0:T(2,128)S(1)} %copy-done.48), channel_id=1, source_target_pairs={{0,4},{1,5},{2,6},{3,7},{4,0},{5,1},{6,2},{7,3},{8,12},{9,13},{10,... | collective-permute-start | bytes 24584 | tf_op jit(solution)/shard_map/ppermute | solution.py:251
  42.4 89.6 %collective-permute-start.20 = (bf16[432,768]{1,0:T(8,128)(2,1)}, bf16[432,768]{1,0:T(8,128)(2,1)}, u32[]{:S(2)}, u32[]{:S(2)}) collective-permute-start(bf16[432,768]{1,0:T(8,128)(2,1)} %dynamic-slice_bitcast_fusion.5), channel_id=1, source_target_pairs={{0,1},{1,0},{6,7},{7,6},{8,9},{9,8},{14,15},{15,14},{16,17},{17,16... | collective-permute-start | bytes 1990664 | tf_op jit(solution)/shard_map/ppermute | solution.py:251
  45.3 86.6 %collective-permute-start.21 = (bf16[432,768]{1,0:T(8,128)(2,1)}, bf16[432,768]{1,0:T(8,128)(2,1)}, u32[]{:S(2)}, u32[]{:S(2)}) collective-permute-start(bf16[432,768]{1,0:T(8,128)(2,1)} %dynamic-slice_bitcast_fusion.5), channel_id=1, source_target_pairs={{0,3},{1,2},{6,5},{7,4},{8,11},{9,10},{14,13},{15,12},{16,19},{17,... | collective-permute-start | bytes 1990664 | tf_op jit(solution)/shard_map/ppermute | solution.py:251
  48.2 88.7 %collective-permute-start.16 = (bf16[432,768]{1,0:T(8,128)(2,1)}, bf16[432,768]{1,0:T(8,128)(2,1)}, u32[]{:S(2)}, u32[]{:S(2)}) collective-permute-start(bf16[432,768]{1,0:T(8,128)(2,1)} %dynamic-slice_bitcast_fusion.5), channel_id=1, source_target_pairs={{0,2},{1,3},{6,4},{7,5},{8,10},{9,11},{14,12},{15,13},{16,18},{17,... | collective-permute-start | bytes 1990664 | tf_op jit(solution)/shard_map/ppermute | solution.py:251
  52.8 173.7 %collective-permute-start.32 = (bf16[2,512,192]{1,2,0:T(8,128)(2,1)}, bf16[2,512,192]{1,2,0:T(8,128)(2,1)}, u32[]{:S(2)}, u32[]{:S(2)}) collective-permute-start(bf16[2,512,192]{1,2,0:T(8,128)(2,1)} %bitcast.230), channel_id=1, source_target_pairs={{0,4},{1,5},{2,6},{3,7},{4,0},{5,1},{6,2},{7,3},{8,12},{9,13},{10,... | collective-permute-start | bytes 1179656 | tf_op jit(solution)/shard_map/ppermute | solution.py:251
  85.4 35.3 %collective-permute-start.2 = (bf16[512,192]{0,1:T(8,128)(2,1)S(1)}, bf16[512,192]{0,1:T(8,128)(2,1)S(1)}, u32[]{:S(2)}, u32[]{:S(2)}) collective-permute-start(bf16[512,192]{0,1:T(8,128)(2,1)S(1)} %get-tuple-element.100), channel_id=1, source_target_pairs={{0,2},{1,3},{2,0},{3,1},{4,6},{5,7},{6,4},{7,5},{8,10},{9,11},{10,... | collective-permute-start | bytes 589832 | tf_op jit(solution)/shard_map/ppermute | solution.py:251
  133.4 14.9 %collective-permute-start.22 = (bf16[432,768]{1,0:T(8,128)(2,1)S(1)}, bf16[432,768]{1,0:T(8,128)(2,1)S(1)}, u32[]{:S(2)}, u32[]{:S(2)}) collective-permute-start(bf16[432,768]{1,0:T(8,128)(2,1)S(1)} %get-tuple-element.59), channel_id=1, source_target_pairs={{0,8},{1,9},{2,10},{3,11},{4,12},{5,13},{6,14},{7,15},{8,0},{9,1},... | collective-permute-start | bytes 1990664 | tf_op jit(solution)/shard_map/ppermute | solution.py:251
  135.0 25.0 %collective-permute-start.23 = (bf16[432,768]{1,0:T(8,128)(2,1)S(1)}, bf16[432,768]{1,0:T(8,128)(2,1)S(1)}, u32[]{:S(2)}, u32[]{:S(2)}) collective-permute-start(bf16[432,768]{1,0:T(8,128)(2,1)S(1)} %get-tuple-element.59), channel_id=1, source_target_pairs={{0,16},{1,17},{2,18},{3,19},{4,20},{5,21},{6,22},{7,23},{8,24},{9,... | collective-permute-start | bytes 1990664 | tf_op jit(solution)/shard_map/ppermute | solution.py:251
  136.8 29.2 %collective-permute-start.5 = (bf16[512,768]{1,0:T(8,128)(2,1)S(1)}, bf16[512,768]{1,0:T(8,128)(2,1)S(1)}, u32[]{:S(2)}, u32[]{:S(2)}) collective-permute-start(bf16[512,768]{1,0:T(8,128)(2,1)S(1)} %add_convert_fusion.3), channel_id=1, source_target_pairs={{0,4},{1,5},{2,6},{3,7},{4,0},{5,1},{6,2},{7,3},{8,12},{9,13},{10,... | collective-permute-start | bytes 2359304 | tf_op jit(solution)/shard_map/ppermute | solution.py:251
  136.9 26.6 %collective-permute-start.24 = (bf16[432,768]{1,0:T(8,128)(2,1)S(1)}, bf16[432,768]{1,0:T(8,128)(2,1)S(1)}, u32[]{:S(2)}, u32[]{:S(2)}) collective-permute-start(bf16[432,768]{1,0:T(8,128)(2,1)S(1)} %get-tuple-element.59), channel_id=1, source_target_pairs={{0,24},{1,25},{2,26},{3,27},{4,28},{5,29},{6,30},{7,31},{8,16},{9,... | collective-permute-start | bytes 1990664 | tf_op jit(solution)/shard_map/ppermute | solution.py:251
  148.3 16.0 %collective-permute-start.17 = (bf16[432,768]{1,0:T(8,128)(2,1)S(1)}, bf16[432,768]{1,0:T(8,128)(2,1)S(1)}, u32[]{:S(2)}, u32[]{:S(2)}) collective-permute-start(bf16[432,768]{1,0:T(8,128)(2,1)S(1)} %get-tuple-element.57), channel_id=1, source_target_pairs={{2,10},{3,11},{4,12},{5,13},{10,2},{11,3},{12,4},{13,5},{18,26},{1... | collective-permute-start | bytes 1990664 | tf_op jit(solution)/shard_map/ppermute | solution.py:251
  214.6 21.7 %collective-permute-start.25 = (bf16[512,768]{1,0:T(8,128)(2,1)}, bf16[512,768]{1,0:T(8,128)(2,1)}, u32[]{:S(2)}, u32[]{:S(2)}) collective-permute-start(bf16[512,768]{1,0:T(8,128)(2,1)} %convolution_convert_fusion.6), channel_id=1, source_target_pairs={{0,4},{1,5},{2,6},{3,7},{4,0},{5,1},{6,2},{7,3},{8,12},{9,13},{10,... | collective-permute-start | bytes 2359304 | tf_op jit(solution)/shard_map/ppermute | solution.py:251
  228.3 22.1 %collective-permute-start.34 = (bf16[512,192]{0,1:T(8,128)(2,1)S(1)}, bf16[512,192]{0,1:T(8,128)(2,1)S(1)}, u32[]{:S(2)}, u32[]{:S(2)}) collective-permute-start(bf16[512,192]{0,1:T(8,128)(2,1)S(1)} %get-tuple-element.89), channel_id=1, source_target_pairs={{0,2},{1,3},{2,0},{3,1},{4,6},{5,7},{6,4},{7,5},{8,10},{9,11},{10,... | collective-permute-start | bytes 589832 | tf_op jit(solution)/shard_map/ppermute | solution.py:251
  236.3 14.1 %collective-permute-start.35 = (bf16[512,192]{0,1:T(8,128)(2,1)S(1)}, bf16[512,192]{0,1:T(8,128)(2,1)S(1)}, u32[]{:S(2)}, u32[]{:S(2)}) collective-permute-start(bf16[512,192]{0,1:T(8,128)(2,1)S(1)} %get-tuple-element.88), channel_id=1, source_target_pairs={{0,3},{1,2},{2,1},{3,0},{4,7},{5,6},{6,5},{7,4},{8,11},{9,10},{10,... | collective-permute-start | bytes 589832 | tf_op jit(solution)/shard_map/ppermute | solution.py:251
  240.6 14.9 %collective-permute-start.26 = (bf16[512,768]{1,0:T(8,128)(2,1)S(1)}, bf16[512,768]{1,0:T(8,128)(2,1)}, u32[]{:S(2)}, u32[]{:S(2)}) collective-permute-start(bf16[512,768]{1,0:T(8,128)(2,1)S(1)} %fusion.16), channel_id=1, source_target_pairs={{0,4},{1,5},{2,6},{3,7},{4,0},{5,1},{6,2},{7,3},{8,12},{9,13},{10,... | collective-permute-start | bytes 2359304 | tf_op jit(solution)/shard_map/ppermute | solution.py:251
  252.8 25.6 %collective-permute-start.36 = (bf16[512,768]{1,0:T(8,128)(2,1)S(1)}, bf16[512,768]{1,0:T(8,128)(2,1)S(1)}, u32[]{:S(2)}, u32[]{:S(2)}) collective-permute-start(bf16[512,768]{1,0:T(8,128)(2,1)S(1)} %copy.82), channel_id=1, source_target_pairs={{0,4},{1,5},{2,6},{3,7},{4,0},{5,1},{6,2},{7,3},{8,12},{9,13},{10,... | collective-permute-start | bytes 2359304 | tf_op jit(solution)/shard_map/ppermute | solution.py:251
  277.8 15.7 %collective-permute-start.27 = (bf16[512,768]{1,0:T(8,128)(2,1)S(1)}, bf16[512,768]{1,0:T(8,128)(2,1)S(1)}, u32[]{:S(2)}, u32[]{:S(2)}) collective-permute-start(bf16[512,768]{1,0:T(8,128)(2,1)S(1)} %fusion.33), channel_id=1, source_target_pairs={{0,4},{1,5},{2,6},{3,7},{4,0},{5,1},{6,2},{7,3},{8,12},{9,13},{10,... | collective-permute-start | bytes 2359304 | tf_op jit(solution)/shard_map/ppermute | solution.py:251
  289.4 16.8 %collective-permute-start.37 = (bf16[512,768]{1,0:T(8,128)(2,1)}, bf16[512,768]{1,0:T(8,128)(2,1)}, u32[]{:S(2)}, u32[]{:S(2)}) collective-permute-start(bf16[512,768]{1,0:T(8,128)(2,1)} %fusion.36), channel_id=1, source_target_pairs={{0,4},{1,5},{2,6},{3,7},{4,0},{5,1},{6,2},{7,3},{8,12},{9,13},{10,... | collective-permute-start | bytes 2359304 | tf_op jit(solution)/shard_map/ppermute | solution.py:251
  299.3 31.7 %collective-permute-start.28 = (bf16[512,192]{0,1:T(8,128)(2,1)S(1)}, bf16[512,192]{0,1:T(8,128)(2,1)S(1)}, u32[]{:S(2)}, u32[]{:S(2)}) collective-permute-start(bf16[512,192]{0,1:T(8,128)(2,1)S(1)} %get-tuple-element.98), channel_id=1, source_target_pairs={{0,1},{1,0},{2,3},{3,2},{4,5},{5,4},{6,7},{7,6},{8,9},{9,8},{10,11... | collective-permute-start | bytes 589832 | tf_op jit(solution)/shard_map/ppermute | solution.py:251
  303.7 27.3 %collective-permute-start.29 = (bf16[512,192]{0,1:T(8,128)(2,1)S(1)}, bf16[512,192]{0,1:T(8,128)(2,1)S(1)}, u32[]{:S(2)}, u32[]{:S(2)}) collective-permute-start(bf16[512,192]{0,1:T(8,128)(2,1)S(1)} %get-tuple-element.97), channel_id=1, source_target_pairs={{0,2},{1,3},{2,0},{3,1},{4,6},{5,7},{6,4},{7,5},{8,10},{9,11},{10,... | collective-permute-start | bytes 589832 | tf_op jit(solution)/shard_map/ppermute | solution.py:251
  304.8 26.3 %collective-permute-start.30 = (bf16[512,192]{0,1:T(8,128)(2,1)S(1)}, bf16[512,192]{0,1:T(8,128)(2,1)S(1)}, u32[]{:S(2)}, u32[]{:S(2)}) collective-permute-start(bf16[512,192]{0,1:T(8,128)(2,1)S(1)} %get-tuple-element.96), channel_id=1, source_target_pairs={{0,3},{1,2},{2,1},{3,0},{4,7},{5,6},{6,5},{7,4},{8,11},{9,10},{10,... | collective-permute-start | bytes 589832 | tf_op jit(solution)/shard_map/ppermute | solution.py:251
  327.9 23.2 %collective-permute-start.38 = (bf16[512,768]{1,0:T(8,128)(2,1)}, bf16[512,768]{1,0:T(8,128)(2,1)}, u32[]{:S(2)}, u32[]{:S(2)}) collective-permute-start(bf16[512,768]{1,0:T(8,128)(2,1)} %get-tuple-element.50), channel_id=1, source_target_pairs={{0,4},{1,5},{2,6},{3,7},{4,0},{5,1},{6,2},{7,3},{8,12},{9,13},{10,... | collective-permute-start | bytes 2359304 | tf_op jit(solution)/shard_map/ppermute | solution.py:251
  329.5 16.7 %collective-permute-start.73 = (f32[2,768]{1,0:T(2,128)S(1)}, f32[2,768]{1,0:T(2,128)S(1)}, u32[]{:S(2)}, u32[]{:S(2)}) collective-permute-start(f32[2,768]{1,0:T(2,128)S(1)} %add.340), channel_id=1, source_target_pairs={{0,16},{1,17},{2,18},{3,19},{4,20},{5,21},{6,22},{7,23},{8,24},{9,... | collective-permute-start | bytes 18440 | tf_op jit(solution)/shard_map/ppermute | solution.py:251
  331.2 15.6 %collective-permute-start.31 = (bf16[2,512,192]{1,2,0:T(8,128)(2,1)S(1)}, bf16[2,512,192]{1,2,0:T(8,128)(2,1)S(1)}, u32[]{:S(2)}, u32[]{:S(2)}) collective-permute-start(bf16[2,512,192]{1,2,0:T(8,128)(2,1)S(1)} %get-tuple-element.95), channel_id=1, source_target_pairs={{0,4},{1,5},{2,6},{3,7},{4,0},{5,1},{6,2},{7,3},{8,12},{9,13},{10,... | collective-permute-start | bytes 1179656 | tf_op jit(solution)/shard_map/ppermute | solution.py:251
  428.3 15.0 %collective-permute-start.51 = (bf16[2,192,576]{2,1,0:T(8,128)(2,1)S(1)}, bf16[2,192,576]{2,1,0:T(8,128)(2,1)S(1)}, u32[]{:S(2)}, u32[]{:S(2)}) collective-permute-start(bf16[2,192,576]{2,1,0:T(8,128)(2,1)S(1)} %bitcast.285), channel_id=1, source_target_pairs={{0,24},{1,25},{2,26},{3,27},{4,28},{5,29},{6,30},{7,31},{8,16},{9,... | collective-permute-start | bytes 1327112 | tf_op jit(solution)/shard_map/ppermute | solution.py:251
  429.3 23.7 %collective-permute-start.50 = (bf16[2,192,576]{2,1,0:T(8,128)(2,1)S(1)}, bf16[2,192,576]{2,1,0:T(8,128)(2,1)S(1)}, u32[]{:S(2)}, u32[]{:S(2)}) collective-permute-start(bf16[2,192,576]{2,1,0:T(8,128)(2,1)S(1)} %bitcast.286), channel_id=1, source_target_pairs={{0,16},{1,17},{2,18},{3,19},{4,20},{5,21},{6,22},{7,23},{8,24},{9,... | collective-permute-start | bytes 1327112 | tf_op jit(solution)/shard_map/ppermute | solution.py:251
  430.8 22.2 %collective-permute-start.49 = (bf16[2,192,576]{2,1,0:T(8,128)(2,1)S(1)}, bf16[2,192,576]{2,1,0:T(8,128)(2,1)S(1)}, u32[]{:S(2)}, u32[]{:S(2)}) collective-permute-start(bf16[2,192,576]{2,1,0:T(8,128)(2,1)S(1)} %bitcast.287), channel_id=1, source_target_pairs={{0,8},{1,9},{2,10},{3,11},{4,12},{5,13},{6,14},{7,15},{8,0},{9,1},... | collective-permute-start | bytes 1327112 | tf_op jit(solution)/shard_map/ppermute | solution.py:251
  433.4 37.5 %collective-permute-start.39 = (bf16[512,768]{1,0:T(8,128)(2,1)S(1)}, bf16[512,768]{1,0:T(8,128)(2,1)S(1)}, u32[]{:S(2)}, u32[]{:S(2)}) collective-permute-start(bf16[512,768]{1,0:T(8,128)(2,1)S(1)} %convolution_convert_fusion.5), channel_id=1, source_target_pairs={{0,4},{1,5},{2,6},{3,7},{4,0},{5,1},{6,2},{7,3},{8,12},{9,13},{10,... | collective-permute-start | bytes 2359304 | tf_op jit(solution)/shard_map/ppermute | solution.py:251
  454.6 16.1 %collective-permute-start.52 = (bf16[192,576]{1,0:T(8,128)(2,1)S(1)}, bf16[192,576]{1,0:T(8,128)(2,1)S(1)}, u32[]{:S(2)}, u32[]{:S(2)}) collective-permute-start(bf16[192,576]{1,0:T(8,128)(2,1)S(1)} %get-tuple-element.106), channel_id=1, source_target_pairs={{0,1},{1,0},{6,7},{7,6},{8,9},{9,8},{14,15},{15,14},{16,17},{17,16... | collective-permute-start | bytes 663560 | tf_op jit(solution)/shard_map/ppermute | solution.py:251
  461.4 67.3 %collective-permute-start.61 = (bf16[2,432,768]{2,1,0:T(8,128)(2,1)}, bf16[2,432,768]{2,1,0:T(8,128)(2,1)}, u32[]{:S(2)}, u32[]{:S(2)}) collective-permute-start(bf16[2,432,768]{2,1,0:T(8,128)(2,1)} %get-tuple-element.67), channel_id=1, source_target_pairs={{0,24},{1,25},{2,26},{3,27},{4,28},{5,29},{6,30},{7,31},{8,16},{9,... | collective-permute-start | bytes 3981320 | tf_op jit(solution)/shard_map/ppermute | solution.py:251
  464.8 64.2 %collective-permute-start.60 = (bf16[2,432,768]{2,1,0:T(8,128)(2,1)}, bf16[2,432,768]{2,1,0:T(8,128)(2,1)}, u32[]{:S(2)}, u32[]{:S(2)}) collective-permute-start(bf16[2,432,768]{2,1,0:T(8,128)(2,1)} %get-tuple-element.68), channel_id=1, source_target_pairs={{0,16},{1,17},{2,18},{3,19},{4,20},{5,21},{6,22},{7,23},{8,24},{9,... | collective-permute-start | bytes 3981320 | tf_op jit(solution)/shard_map/ppermute | solution.py:251
  469.6 59.3 %collective-permute-start.59 = (bf16[2,432,768]{2,1,0:T(8,128)(2,1)S(1)}, bf16[2,432,768]{2,1,0:T(8,128)(2,1)}, u32[]{:S(2)}, u32[]{:S(2)}) collective-permute-start(bf16[2,432,768]{2,1,0:T(8,128)(2,1)S(1)} %get-tuple-element.66), channel_id=1, source_target_pairs={{0,8},{1,9},{2,10},{3,11},{4,12},{5,13},{6,14},{7,15},{8,0},{9,1},... | collective-permute-start | bytes 3981320 | tf_op jit(solution)/shard_map/ppermute | solution.py:251
  470.8 66.4 %collective-permute-start.55 = (bf16[192,576]{1,0:T(8,128)(2,1)S(1)}, bf16[192,576]{1,0:T(8,128)(2,1)S(1)}, u32[]{:S(2)}, u32[]{:S(2)}) collective-permute-start(bf16[192,576]{1,0:T(8,128)(2,1)S(1)} %add_convert_fusion.5), channel_id=1, source_target_pairs={{0,4},{1,5},{2,6},{3,7},{4,0},{5,1},{6,2},{7,3},{8,12},{9,13},{10,... | collective-permute-start | bytes 663560 | tf_op jit(solution)/shard_map/ppermute | solution.py:251
  482.3 38.3 %collective-permute-start.47 = (f32[2,768]{1,0:T(2,128)S(1)}, f32[2,768]{1,0:T(2,128)S(1)}, u32[]{:S(2)}, u32[]{:S(2)}) collective-permute-start(f32[2,768]{1,0:T(2,128)S(1)} %add.319), channel_id=1, source_target_pairs={{0,8},{1,9},{2,10},{3,11},{4,12},{5,13},{6,14},{7,15},{8,0},{9,1},... | collective-permute-start | bytes 18440 | tf_op jit(solution)/shard_map/ppermute | solution.py:251
  524.2 14.5 %collective-permute-start.40 = (bf16[512,192]{0,1:T(8,128)(2,1)S(1)}, bf16[512,192]{0,1:T(8,128)(2,1)S(1)}, u32[]{:S(2)}, u32[]{:S(2)}) collective-permute-start(bf16[512,192]{0,1:T(8,128)(2,1)S(1)} %get-tuple-element.87), channel_id=1, source_target_pairs={{0,1},{1,0},{2,3},{3,2},{4,5},{5,4},{6,7},{7,6},{8,9},{9,8},{10,11... | collective-permute-start | bytes 589832 | tf_op jit(solution)/shard_map/ppermute | solution.py:251
  528.7 13.4 %collective-permute-start.41 = (bf16[512,192]{0,1:T(8,128)(2,1)S(1)}, bf16[512,192]{0,1:T(8,128)(2,1)S(1)}, u32[]{:S(2)}, u32[]{:S(2)}) collective-permute-start(bf16[512,192]{0,1:T(8,128)(2,1)S(1)} %get-tuple-element.86), channel_id=1, source_target_pairs={{0,2},{1,3},{2,0},{3,1},{4,6},{5,7},{6,4},{7,5},{8,10},{9,11},{10,... | collective-permute-start | bytes 589832 | tf_op jit(solution)/shard_map/ppermute | solution.py:251
  532.3 21.5 %collective-permute-start.64 = (bf16[432,768]{1,0:T(8,128)(2,1)S(1)}, bf16[432,768]{1,0:T(8,128)(2,1)S(1)}, u32[]{:S(2)}, u32[]{:S(2)}) collective-permute-start(bf16[432,768]{1,0:T(8,128)(2,1)S(1)} %get-tuple-element.82), channel_id=1, source_target_pairs={{2,1},{3,0},{4,7},{5,6},{10,9},{11,8},{12,15},{13,14},{18,17},{19,... | collective-permute-start | bytes 1990664 | tf_op jit(solution)/shard_map/ppermute | solution.py:251
  533.6 42.1 %collective-permute-start.62 = (bf16[432,768]{1,0:T(8,128)(2,1)S(1)}, bf16[432,768]{1,0:T(8,128)(2,1)S(1)}, u32[]{:S(2)}, u32[]{:S(2)}) collective-permute-start(bf16[432,768]{1,0:T(8,128)(2,1)S(1)} %get-tuple-element.82), channel_id=1, source_target_pairs={{0,1},{1,0},{6,7},{7,6},{8,9},{9,8},{14,15},{15,14},{16,17},{17,16... | collective-permute-start | bytes 1990664 | tf_op jit(solution)/shard_map/ppermute | solution.py:251
  537.2 37.1 %collective-permute-start.63 = (bf16[432,768]{1,0:T(8,128)(2,1)S(1)}, bf16[432,768]{1,0:T(8,128)(2,1)S(1)}, u32[]{:S(2)}, u32[]{:S(2)}) collective-permute-start(bf16[432,768]{1,0:T(8,128)(2,1)S(1)} %get-tuple-element.81), channel_id=1, source_target_pairs={{2,0},{3,1},{4,6},{5,7},{10,8},{11,9},{12,14},{13,15},{18,16},{19,... | collective-permute-start | bytes 1990664 | tf_op jit(solution)/shard_map/ppermute | solution.py:251
  538.7 37.4 %collective-permute-start.42 = (bf16[512,192]{0,1:T(8,128)(2,1)S(1)}, bf16[512,192]{0,1:T(8,128)(2,1)S(1)}, u32[]{:S(2)}, u32[]{:S(2)}) collective-permute-start(bf16[512,192]{0,1:T(8,128)(2,1)S(1)} %get-tuple-element.85), channel_id=1, source_target_pairs={{0,3},{1,2},{2,1},{3,0},{4,7},{5,6},{6,5},{7,4},{8,11},{9,10},{10,... | collective-permute-start | bytes 589832 | tf_op jit(solution)/shard_map/ppermute | solution.py:251
  542.1 35.3 %collective-permute-start.56 = (bf16[192,576]{1,0:T(8,128)(2,1)S(1)}, bf16[192,576]{1,0:T(8,128)(2,1)S(1)}, u32[]{:S(2)}, u32[]{:S(2)}) collective-permute-start(bf16[192,576]{1,0:T(8,128)(2,1)S(1)} %get-tuple-element.49), channel_id=1, source_target_pairs={{0,8},{1,9},{2,10},{3,11},{4,12},{5,13},{6,14},{7,15},{8,0},{9,1},... | collective-permute-start | bytes 663560 | tf_op jit(solution)/shard_map/ppermute | solution.py:251
  553.8 23.7 %collective-permute-start.57 = (bf16[192,576]{1,0:T(8,128)(2,1)S(1)}, bf16[192,576]{1,0:T(8,128)(2,1)S(1)}, u32[]{:S(2)}, u32[]{:S(2)}) collective-permute-start(bf16[192,576]{1,0:T(8,128)(2,1)S(1)} %get-tuple-element.49), channel_id=1, source_target_pairs={{0,16},{1,17},{2,18},{3,19},{4,20},{5,21},{6,22},{7,23},{8,24},{9,... | collective-permute-start | bytes 663560 | tf_op jit(solution)/shard_map/ppermute | solution.py:251
  579.4 18.1 %collective-permute-start.66 = (bf16[432,768]{1,0:T(8,128)(2,1)}, bf16[432,768]{1,0:T(8,128)(2,1)}, u32[]{:S(2)}, u32[]{:S(2)}) collective-permute-start(bf16[432,768]{1,0:T(8,128)(2,1)} %get-tuple-element.47), channel_id=1, source_target_pairs={{0,8},{1,9},{2,10},{3,11},{4,12},{5,13},{6,14},{7,15},{8,0},{9,1},... | collective-permute-start | bytes 1990664 | tf_op jit(solution)/shard_map/ppermute | solution.py:251
  581.4 30.4 %collective-permute-start.67 = (bf16[432,768]{1,0:T(8,128)(2,1)}, bf16[432,768]{1,0:T(8,128)(2,1)}, u32[]{:S(2)}, u32[]{:S(2)}) collective-permute-start(bf16[432,768]{1,0:T(8,128)(2,1)} %get-tuple-element.47), channel_id=1, source_target_pairs={{0,16},{1,17},{2,18},{3,19},{4,20},{5,21},{6,22},{7,23},{8,24},{9,... | collective-permute-start | bytes 1990664 | tf_op jit(solution)/shard_map/ppermute | solution.py:251
  586.9 26.0 %collective-permute-start.68 = (bf16[432,768]{1,0:T(8,128)(2,1)}, bf16[432,768]{1,0:T(8,128)(2,1)}, u32[]{:S(2)}, u32[]{:S(2)}) collective-permute-start(bf16[432,768]{1,0:T(8,128)(2,1)} %get-tuple-element.47), channel_id=1, source_target_pairs={{0,24},{1,25},{2,26},{3,27},{4,28},{5,29},{6,30},{7,31},{8,16},{9,... | collective-permute-start | bytes 1990664 | tf_op jit(solution)/shard_map/ppermute | solution.py:251
  (81 other events, 955.7 us)

commit v2 on v1

v2 whole, which is shorter than its diff:
```python
from functools import partial

import math
import jax, jax.numpy as jnp
from jax import lax
from jax.experimental import pallas as pl
from jax.experimental.pallas import tpu as pltpu

BLK = 64
LOG2E = 1.4426950408889634

def dot(a, b, dims):
    return lax.dot_general(a, b, (dims, ((), ())), preferred_element_type=jnp.float32)

def meets(seg_ref, r0, tq, c0, tk):
    return (seg_ref[0, r0] <= seg_ref[0, c0 + tk - 1]) & (seg_ref[0, c0] <= seg_ref[0, r0 + tq - 1])

def fwd_kernel(at_ref, seg_s, n_ref, segc_ref, segr_ref, hit_ref, proj_ref, *rest, tq, tk, dh, part):
    out_ref, qf_ref, kf_ref, rinv_ref, qkv_ref, w_ref, vext, sems = rest[-8:]
    copies = [
        pltpu.make_async_copy(piece.at[part], w_ref.at[at_ref[0] ^ d], sems.at[d]) for d, piece in enumerate(rest[:4])
    ]
    for copy in copies:
        copy.start()
    for copy in copies:
        copy.wait()
    weights = w_ref[...].reshape(n_ref.shape[1], qkv_ref.shape[1])

    def project(i, _):
        rows = pl.ds(pl.multiple_of(i * 256, 256), 256)
        qkv_ref[rows, :] = dot(n_ref[rows, :], weights, ((1,), (0,))).astype(jnp.bfloat16)
        return 0

    lax.fori_loop(0, n_ref.shape[0] // 256, project, 0)
    length = qkv_ref.shape[0]
    feats = proj_ref.shape[1]
    quarter = dh ** (-0.25)
    nh = qkv_ref.shape[1] // (3 * dh)
    for h in range(nh):
        base = h * 3 * dh
        for j, f_ref in ((0, qf_ref), (1, kf_ref)):
            def feat_body(i, _, base=base, j=j, f_ref=f_ref, h=h):
                rows = pl.ds(pl.multiple_of(i * 256, 256), 256)
                t = qkv_ref[rows, base + j * dh: base + (j + 1) * dh]
                lin = dot(t, proj_ref[...], ((1,), (0,)))
                tw = t.astype(jnp.float32)
                sq = jnp.sum(tw * tw, axis=1, keepdims=True) * (0.5 * quarter * quarter * LOG2E) + 0.5 * math.log2(feats)
                f_ref[h, rows, :] = jnp.exp2(lin * (quarter * LOG2E) - sq).astype(jnp.bfloat16)
                return 0
            lax.fori_loop(0, length // 256, feat_body, 0)
        v = qkv_ref[:, base + 2 * dh: base + 3 * dh]
        lane = lax.broadcasted_iota(jnp.int32, (length, dh), 1)
        vext[h, :, :] = jnp.concatenate([v, (lane < 1).astype(jnp.bfloat16)], axis=1)

    def q_body(i, _):
        r0 = pl.multiple_of(i * tq, tq)
        qs = [qkv_ref[pl.ds(r0, tq), h * 3 * dh: h * 3 * dh + dh] for h in range(nh)]
        qfs = [qf_ref[h, pl.ds(r0, tq), :] for h in range(nh)]
        segq = segc_ref[pl.ds(r0, tq), :]
        def k_body(j, acc):
            c0 = pl.multiple_of(j * tk, tk)
            same = segq == segr_ref[:, pl.ds(c0, tk)]
            new = []
            for h in range(nh):
                k = qkv_ref[pl.ds(c0, tk), h * 3 * dh + dh: h * 3 * dh + 2 * dh]
                s = dot(qs[h], k, ((1,), (1,)))
                e = jnp.exp2(s * (LOG2E * dh ** -0.5))
                a = dot(qfs[h], kf_ref[h, pl.ds(c0, tk), :], ((1,), (1,)))
                parts = []
                for b in range(tq // BLK):
                    hit = hit_ref[h, pl.ds(i * (tq // BLK) + b, 1), pl.ds(c0, tk)] > 0.5
                    rs = slice(b * BLK, (b + 1) * BLK)
                    parts.append(jnp.where(jnp.broadcast_to(hit, (BLK, tk)), e[rs], a[rs]))
                comb = jnp.where(same, jnp.concatenate(parts, axis=0), 0.0).astype(jnp.bfloat16)
                new.append(acc[h] + dot(comb, vext[h, pl.ds(c0, tk), :], ((1,), (0,))))
            return tuple(new)
        def k_step(j, acc):
            return lax.cond(meets(seg_s, r0, tq, pl.multiple_of(j * tk, tk), tk), lambda a: k_body(j, a), lambda a: a, acc)
        acc = lax.fori_loop(0, length // tk, k_step, tuple(jnp.zeros((tq, 2 * dh), jnp.float32) for _ in range(nh)))
        for h in range(nh):
            rinv = 1.0 / acc[h][:, dh:dh + 1]
            out_ref[pl.ds(r0, tq), h * dh:(h + 1) * dh] = (acc[h][:, :dh] * rinv).astype(jnp.bfloat16)
            rinv_ref[h, pl.ds(r0, tq), :] = rinv
        return 0
    lax.fori_loop(0, length // tq, q_body, 0)

def attn_fwd(at, n1, pieces, part, seg, hit, proj, ahead=(), *, tq=512, tk=256):
    length, width = n1.shape
    dh, feats = proj.shape
    cols = pieces[0].shape[2]
    heads = cols // (3 * dh)
    seg2 = seg.reshape(1, length)
    smem = pl.BlockSpec(memory_space=pltpu.SMEM)
    vmem = pl.BlockSpec(memory_space=pltpu.VMEM)
    anywhere = pl.BlockSpec(memory_space=pl.ANY)
    return pl.pallas_call(
        partial(fwd_kernel, tq=tq, tk=tk, dh=dh, part=part),
        in_specs=[smem] * 2 + [vmem] * 5 + [anywhere] * (4 + len(ahead)),
        out_specs=[vmem] * 6,
        out_shape=[
            jax.ShapeDtypeStruct((length, heads * dh), jnp.bfloat16),
            jax.ShapeDtypeStruct((heads, length, feats), jnp.bfloat16),
            jax.ShapeDtypeStruct((heads, length, feats), jnp.bfloat16),
            jax.ShapeDtypeStruct((heads, length, 1), jnp.float32),
            jax.ShapeDtypeStruct((length, cols), jnp.bfloat16),
            jax.ShapeDtypeStruct((4, width // 4, cols), jnp.bfloat16),
        ],
        scratch_shapes=[pltpu.VMEM((heads, length, 2 * dh), jnp.bfloat16), pltpu.SemaphoreType.DMA((4,))],
        compiler_params=pltpu.CompilerParams(vmem_limit_bytes=48 * 1024 * 1024),
        cost_estimate=pl.CostEstimate(flops=27 * 10**9, bytes_accessed=10**7, transcendentals=10**6),
        name="attn_fwd",
    )(at, seg2, n1, seg.reshape(length, 1), seg2, hit, proj, *pieces, *ahead)


def bwd_kernel(seg_s, qkv_ref, segc_ref, segr_ref, hit_ref, proj_ref, pext_ref, qf_ref, kf_ref, rinv_ref, o_ref, do_ref, *rest, tq, tk, dh):
    dqkv_ref, vext, doext, dq, dk, dv, dqf, dkf = rest[-8:]
    length = qkv_ref.shape[0]
    quarter = dh ** (-0.25)
    nh = qkv_ref.shape[1] // (3 * dh)
    lane = lax.broadcasted_iota(jnp.int32, (length, dh), 1)
    for h in range(nh):
        base = h * 3 * dh
        v = qkv_ref[:, base + 2 * dh: base + 3 * dh]
        vext[h, :, :] = jnp.concatenate([v, (lane < 2).astype(jnp.bfloat16)], axis=1)
        d_o = do_ref[:, h * dh:(h + 1) * dh].astype(jnp.float32)
        o = o_ref[:, h * dh:(h + 1) * dh].astype(jnp.float32)
        rinv = rinv_ref[h]
        delta = -jnp.sum(d_o * o, axis=1, keepdims=True) * rinv
        high = delta.astype(jnp.bfloat16).astype(jnp.float32)
        low = delta - high
        tail = jnp.where(lane == 0, high, jnp.where(lane == 1, low, 0.0))
        doext[h, :, :] = jnp.concatenate([d_o * rinv, tail], axis=1).astype(jnp.bfloat16)
    dq[...] = jnp.zeros_like(dq)
    dk[...] = jnp.zeros_like(dk)
    dv[...] = jnp.zeros_like(dv)
    dqf[...] = jnp.zeros_like(dqf)
    dkf[...] = jnp.zeros_like(dkf)

    def q_body(i, _):
        r0 = pl.multiple_of(i * tq, tq)
        rows = pl.ds(r0, tq)
        segq = segc_ref[rows, :]
        def k_body(j, _):
            c0 = pl.multiple_of(j * tk, tk)
            cols = pl.ds(c0, tk)
            same = segq == segr_ref[:, cols]
            for h in range(nh):
                base = h * 3 * dh
                q = qkv_ref[rows, base: base + dh]
                k = qkv_ref[cols, base + dh: base + 2 * dh]
                qf = qf_ref[h, rows, :]
                kf = kf_ref[h, cols, :]
                s = dot(q, k, ((1,), (1,)))
                e = jnp.exp2(s * (LOG2E * dh ** -0.5))
                a = dot(qf, kf, ((1,), (1,)))
                dc = dot(doext[h, rows, :], vext[h, cols, :], ((1,), (1,)))
                dc = jnp.where(same, dc, 0.0)
                combs, dss, das = [], [], []
                for b in range(tq // BLK):
                    hit = hit_ref[h, pl.ds(i * (tq // BLK) + b, 1), cols] > 0.5
                    hit = jnp.broadcast_to(hit, (BLK, tk))
                    rs = slice(b * BLK, (b + 1) * BLK)
                    combs.append(jnp.where(hit, e[rs], a[rs]))
                    dss.append(jnp.where(hit, dc[rs] * e[rs], 0.0))
                    das.append(jnp.where(hit, 0.0, dc[rs]))
                comb = jnp.where(same, jnp.concatenate(combs, axis=0), 0.0).astype(jnp.bfloat16)
                ds = jnp.concatenate(dss, axis=0).astype(jnp.bfloat16)
                da = jnp.concatenate(das, axis=0).astype(jnp.bfloat16)
                dq[h, rows, :] += dot(ds, k, ((1,), (0,)))
                dqf[h, rows, :] += dot(da, kf, ((1,), (0,)))
                dk[h, cols, :] += dot(ds, q, ((0,), (0,)))
                dkf[h, cols, :] += dot(da, qf, ((0,), (0,)))
                dv[h, cols, :] += dot(comb, doext[h, rows, :dh], ((0,), (0,)))
            return 0
        def k_step(j, _):
            @pl.when(meets(seg_s, r0, tq, pl.multiple_of(j * tk, tk), tk))
            def _():
                k_body(j, 0)
            return 0
        lax.fori_loop(0, length // tk, k_step, 0)
        return 0
    lax.fori_loop(0, length // tq, q_body, 0)

    for h in range(nh):
        base = h * 3 * dh
        for j, dt, dfeat, f_ref in ((0, dq, dqf, qf_ref), (1, dk, dkf, kf_ref)):
            def back(i, _, base=base, j=j, dt=dt, dfeat=dfeat, f_ref=f_ref, h=h):
                rows = pl.ds(pl.multiple_of(i * 256, 256), 256)
                dpre = dfeat[h, rows, :] * f_ref[h, rows, :].astype(jnp.float32)
                hi_ = dpre.astype(jnp.bfloat16)
                lo_ = (dpre - hi_.astype(jnp.float32)).astype(jnp.bfloat16)
                thr = dot(hi_, pext_ref[...], ((1,), (0,))) + dot(lo_, pext_ref[...], ((1,), (0,)))
                t = qkv_ref[rows, base + j * dh: base + (j + 1) * dh].astype(jnp.float32)
                g = dt[h, rows, :] * dh ** -0.5 + quarter * thr[:, :dh] - (quarter * quarter) * t * thr[:, dh:dh + 1]
                dqkv_ref[rows, base + j * dh: base + (j + 1) * dh] = g.astype(jnp.bfloat16)
                return 0
            lax.fori_loop(0, length // 256, back, 0)
        dqkv_ref[:, base + 2 * dh: base + 3 * dh] = dv[h].astype(jnp.bfloat16)

def attn_bwd(qkv, seg, hit, proj, qf, kf, rinv, o, d_o, ahead=(), *, tq=512, tk=256):
    length = qkv.shape[0]
    dh, feats = proj.shape
    heads = qkv.shape[1] // (3 * dh)
    seg2 = seg.reshape(1, length)
    pext = jnp.concatenate([proj.T, jnp.ones((feats, 1), proj.dtype), jnp.zeros((feats, dh - 1), proj.dtype)], axis=1)
    f32 = jnp.float32
    vmem = pl.BlockSpec(memory_space=pltpu.VMEM)
    return pl.pallas_call(
        partial(bwd_kernel, tq=tq, tk=tk, dh=dh),
        in_specs=[pl.BlockSpec(memory_space=pltpu.SMEM)] + [vmem] * 11 + [pl.BlockSpec(memory_space=pl.ANY)] * len(ahead),
        out_specs=vmem,
        out_shape=jax.ShapeDtypeStruct((length, heads * 3 * dh), jnp.bfloat16),
        scratch_shapes=[
            pltpu.VMEM((heads, length, 2 * dh), jnp.bfloat16),
            pltpu.VMEM((heads, length, 2 * dh), jnp.bfloat16),
            pltpu.VMEM((heads, length, dh), f32),
            pltpu.VMEM((heads, length, dh), f32),
            pltpu.VMEM((heads, length, dh), f32),
            pltpu.VMEM((heads, length, feats), f32),
            pltpu.VMEM((heads, length, feats), f32),
        ],
        compiler_params=pltpu.CompilerParams(vmem_limit_bytes=52 * 1024 * 1024),
        cost_estimate=pl.CostEstimate(flops=38 * 10**9, bytes_accessed=2 * 10**7, transcendentals=10**6),
        name="attn_bwd",
    )(seg2, qkv, seg.reshape(length, 1), seg2, hit, proj, pext, qf, kf, rinv, o, d_o, *ahead)


def hit_lanes(lists, length):
    nb = lists.shape[1]
    ids = lax.broadcasted_iota(jnp.int32, (1, 1, length), 2) // BLK
    out = lists[:, :, 0:1] == ids
    for s in range(1, lists.shape[2]):
        out = out | (lists[:, :, s:s + 1] == ids)
    return out.astype(jnp.float32)

from jax.sharding import PartitionSpec as P


def gelu_pair(u):
    mag = jnp.abs(u)
    t = 1.0 / (1.0 + (0.3275911 * 0.7071067811865476) * mag)
    bell = jnp.exp2(u * u * (-0.5 * LOG2E))
    poly = t * (0.127414796 + t * (-0.142248368 + t * (0.7107068705 + t * (-0.7265760135 + t * 0.5307027145))))
    tail = poly * bell
    cdf = jnp.where(u >= 0.0, 1.0 - tail, tail)
    return u * cdf, cdf + u * bell * 0.3989422804014327


def mlp_kernel(n_ref, dy_ref, up_ref, down_ref, act_ref, dpre_ref, own_ref, oth_ref, acc, *, tile, rows):
    x = pl.program_id(0)
    tokens, width = n_ref.shape
    hid = act_ref.shape[1]
    up = up_ref[...].reshape(width, hid)
    down = down_ref[...].reshape(hid, width)
    for j in range(hid // tile):
        up_t = up[:, j * tile:(j + 1) * tile]
        down_t = down[j * tile:(j + 1) * tile, :]
        def body(i, _, j=j, up_t=up_t, down_t=down_t):
            rs = pl.ds(pl.multiple_of(i * rows, rows), rows)
            pre = dot(n_ref[rs, :], up_t, ((1,), (0,)))
            d_act = dot(dy_ref[rs, :], down_t, ((1,), (1,)))
            act, slope = gelu_pair(pre)
            d_pre = (d_act * slope).astype(jnp.bfloat16)
            act_ref[rs, j * tile:(j + 1) * tile] = act.astype(jnp.bfloat16)
            dpre_ref[rs, j * tile:(j + 1) * tile] = d_pre
            part = dot(d_pre, up_t, ((1,), (1,)))
            if j == 0:
                @pl.when(x == 0)
                def _():
                    acc[rs, :] = part
                @pl.when(x > 0)
                def _():
                    acc[rs, :] += part
            else:
                acc[rs, :] += part
            return 0
        lax.fori_loop(0, tokens // rows, body, 0)

    @pl.when(x == pl.num_programs(0) - 1)
    def _():
        own_ref[...] = acc[:tokens // 2, :]
        oth_ref[...] = acc[tokens // 2:, :].astype(jnp.bfloat16)


def mlp_first(n2, dy, pack, piece, *, tile=256, rows=256):
    tokens, width = n2.shape
    cuts, parts = pack.shape[0], pack.shape[1]
    hid = cuts * piece
    half = tokens // 2
    bf16, f32 = jnp.bfloat16, jnp.float32
    whole = pl.BlockSpec((tokens, width), lambda x: (0, 0))
    return pl.pallas_call(
        partial(mlp_kernel, tile=tile, rows=rows),
        grid=(parts,),
        in_specs=[
            whole,
            whole,
            pl.BlockSpec((cuts, 1, piece, width), lambda x: (0, x, 0, 0)),
            pl.BlockSpec((cuts, 1, piece, width), lambda x: (0, x, 1, 0)),
        ],
        out_specs=[
            pl.BlockSpec((tokens, hid), lambda x: (0, x)),
            pl.BlockSpec((tokens, hid), lambda x: (0, x)),
            pl.BlockSpec((half, width), lambda x: (0, 0)),
            pl.BlockSpec((half, width), lambda x: (0, 0)),
        ],
        out_shape=[
            jax.ShapeDtypeStruct((tokens, parts * hid), bf16),
            jax.ShapeDtypeStruct((tokens, parts * hid), bf16),
            jax.ShapeDtypeStruct((half, width), f32),
            jax.ShapeDtypeStruct((half, width), bf16),
        ],
        scratch_shapes=[pltpu.VMEM((tokens, width), f32)],
        compiler_params=pltpu.CompilerParams(vmem_limit_bytes=48 * 1024 * 1024),
        cost_estimate=pl.CostEstimate(flops=25 * 10**9, bytes_accessed=2 * 10**7, transcendentals=3 * 10**6),
        name="mlp_first",
    )(n2, dy, pack, pack)


def mlp_grad_kernel(n_ref, dy_ref, act_ref, dpre_ref, down_ref, own_ref, oth_ref, grad_ref, acc, *, tile, piece):
    x = pl.program_id(0)
    tokens, width = n_ref.shape
    hid = act_ref.shape[1]
    half = tokens // 2
    down = down_ref[...].reshape(hid, width)
    tn = ((0,), (0,))
    def out_rows(i, _):
        rs = pl.ds(pl.multiple_of(i * tile, tile), tile)
        part = dot(act_ref[rs, :], down, ((1,), (0,)))
        @pl.when(x == 0)
        def _():
            acc[rs, :] = part
        @pl.when(x > 0)
        def _():
            acc[rs, :] += part
        return 0
    lax.fori_loop(0, tokens // tile, out_rows, 0)
    for j in range(width // (4 * piece)):
        cut = slice(4 * j * piece, 4 * (j + 1) * piece)
        up_g = dot(n_ref[:, cut], dpre_ref[...], tn).astype(jnp.bfloat16)
        grad_ref[2 * j:2 * j + 2, :, 0, :piece, :] = up_g.reshape(2, 2, piece, hid)
        down_g = dot(act_ref[:, cut], dy_ref[...], tn).astype(jnp.bfloat16)
        grad_ref[2 * j:2 * j + 2, :, 0, piece:2 * piece, :] = down_g.reshape(2, 2, piece, width)

    @pl.when(x == pl.num_programs(0) - 1)
    def _():
        own_ref[...] = acc[:half, :]
        oth_ref[...] = acc[half:, :].astype(jnp.bfloat16)


def mlp_second(n2, dy, acted, d_pre, pack, piece, *, tile=256):
    tokens, width = n2.shape
    cuts, parts = pack.shape[0], pack.shape[1]
    hid = cuts * piece
    half = tokens // 2
    bf16, f32 = jnp.bfloat16, jnp.float32
    whole = pl.BlockSpec((tokens, width), lambda x: (0, 0))
    cols = pl.BlockSpec((tokens, hid), lambda x: (0, x))
    side = pl.BlockSpec((half, width), lambda x: (0, 0))
    return pl.pallas_call(
        partial(mlp_grad_kernel, tile=tile, piece=piece),
        grid=(parts,),
        in_specs=[whole, whole, cols, cols, pl.BlockSpec((cuts, 1, piece, width), lambda x: (0, x, 1, 0))],
        out_specs=[side, side, pl.BlockSpec((4, 2, 1, 2 * piece, width), lambda x: (0, 0, x, 0, 0))],
        out_shape=[
            jax.ShapeDtypeStruct((half, width), f32),
            jax.ShapeDtypeStruct((half, width), bf16),
            jax.ShapeDtypeStruct((4, 2, parts, 2 * piece, width), bf16),
        ],
        scratch_shapes=[pltpu.VMEM((tokens, width), f32)],
        compiler_params=pltpu.CompilerParams(vmem_limit_bytes=48 * 1024 * 1024),
        cost_estimate=pl.CostEstimate(flops=17 * 10**9, bytes_accessed=2 * 10**7, transcendentals=0),
        name="mlp_second",
    )(n2, dy, acted, d_pre, pack)


norm_eps = 1e-05


def norm_rows(values):
    center = values - jnp.mean(values, axis=1, keepdims=True)
    scale = lax.rsqrt(jnp.mean(center * center, axis=1, keepdims=True) + norm_eps)
    return center * scale, scale


def norm_back(grad, xhat, scale, gain):
    dx = grad * gain
    return scale * (
        dx - jnp.mean(dx, axis=1, keepdims=True) - xhat * jnp.mean(dx * xhat, axis=1, keepdims=True)
    )


def own_group(i):
    return (i & 3) // 2 == (i >> 2) & 1


def far_group(i):
    return not own_group(i)


def shards(
    activations, segment_ids, block_lists, feature_proj, input_norm_gain, input_norm_bias, qkv_weight,
    out_weight, middle_norm_gain, middle_norm_bias, up_weight, down_weight, out_grad,
):
    rows_n, heads_n = lax.axis_size("row"), lax.axis_size("head")
    total = rows_n * heads_n
    r, z = lax.axis_index("row"), lax.axis_index("head")
    c, p = r % 2, (r // 2) % 4
    groups = rows_n // 8
    pairs = [[2 * i, 2 * i + 1] for i in range(rows_n // 2)]
    planes = [[8 * g + i for i in range(8)] for g in range(groups)]
    quads = [[8 * g + 2 * i + k for i in range(4)] for g in range(groups) for k in range(2)]
    width = input_norm_gain.shape[0]
    quarter = width // heads_n
    seq_count, length = segment_ids.shape
    half = length // 2
    lists_here = block_lists.shape[1]
    bf16, f32 = jnp.bfloat16, jnp.float32
    nn, nt, tn = ((1,), (0,)), ((1,), (1,)), ((0,), (0,))
    local = (z // 2) == c
    par = z % 2

    def move(v, mask, only=None):
        moves = [(i, i ^ mask) for i in range(total) if only is None or only(i)]
        return lax.ppermute(v, ("row", "head"), moves)

    def later(i, dep):
        one = dep.reshape(-1)[0]
        return i + (one != one).astype(jnp.int32)

    def deal_z(v):
        return lax.all_to_all(v, "head", 0, 0, tiled=True)

    def tied(v, dep):
        one = dep.reshape(-1)[0]
        return v + (one != one).astype(v.dtype)

    def deal(v, side):
        v = v.T

        def token_half(k):
            return jnp.stack([lax.dynamic_slice_in_dim(v, s * length + k * half, half, 1) for s in range(seq_count)])

        keep, got = token_half(side), move(token_half(1 - side), 4)
        return jnp.concatenate([jnp.where(side == 0, keep, got), jnp.where(side == 0, got, keep)], 0)

    def collect(v):
        v = v.reshape(2, seq_count, quarter, half)
        keep = lax.dynamic_index_in_dim(v, c, 0, keepdims=False)
        got = move(lax.dynamic_index_in_dim(v, 1 - c, 0, keepdims=False), 4)
        low, high = jnp.where(c == 0, keep, got), jnp.where(c == 0, got, keep)
        return jnp.concatenate([w[s] for s in range(seq_count) for w in (low, high)], 1).T

    def fetch_z(mine):
        return [mine] + [move(mine, d, own_group) for d in (1, 2, 3)]

    def choose(got, here):
        return jnp.stack([jnp.where(here, got[0], got[2]), jnp.where(here, got[1], got[3])])

    def fetch_plane(both):
        return [both] + [move(both, 8 * d) for d in (1, 2, 3)]

    def give_z(same, other):
        fin = same.astype(f32) + move(other, 1, own_group).astype(f32)
        fin = fin + move(same, 2, far_group).astype(f32) + move(other, 3, far_group).astype(f32)
        if groups > 1:
            fin = lax.psum(fin, "row", axis_index_groups=[[8 * g + i for g in range(groups)] for i in range(8)])
        fin = fin.astype(bf16)
        fin = jnp.where(local, fin, move(fin, 4))
        n = fin.shape[0] // 2
        return lax.dynamic_slice_in_dim(fin, c * n, n, 0)

    def gather_plane(v):
        return lax.all_gather(v, "row", axis=0, axis_index_groups=planes)

    cut = lambda w, n, at: lax.dynamic_slice_in_dim(w, at * n, n, 0)

    aux = jnp.concatenate([block_lists.reshape(seq_count, -1), segment_ids], 1).astype(bf16)
    aux_got = move(aux, 4)
    aux = jnp.where(c == 0, jnp.concatenate([aux, aux_got], 0), jnp.concatenate([aux_got, aux], 0))
    n_list = aux.shape[1] - length
    seg = lax.dynamic_index_in_dim(aux[:, n_list:], z, 0, keepdims=False).astype(jnp.int32)

    x_half = deal_z(deal(activations, c)).reshape(width, half).T
    x = x_half.astype(f32)

    n_qkv, n_hid, n_out = width // 4, down_weight.shape[0] // 8, out_weight.shape[0] // 8
    cols = qkv_weight.shape[1]
    extra = 16
    rider = aux[:, :n_list].reshape(-1)
    rider = jnp.pad(rider, (0, extra * cols - rider.shape[0])).reshape(extra, cols)
    both = choose(fetch_z(jnp.concatenate([cut(qkv_weight, n_qkv, p), rider], 0)), local)
    lists = both[:, n_qkv:].reshape(2, -1)[:, :4 * n_list].reshape(2, 4, n_list).astype(jnp.int32)
    lists = lax.dynamic_index_in_dim(lists, z, 1, keepdims=False).reshape((2, lists_here) + block_lists.shape[2:])
    wq_pieces = fetch_plane(both[:, :n_qkv])
    at = jnp.full((1,), p, jnp.int32)

    q8 = r % 8
    n_up = width // 8
    mine = jnp.concatenate([cut(up_weight, n_up, q8), cut(down_weight, n_hid, q8), cut(out_weight, n_out, q8)], 0)
    pack = lax.all_gather(mine, "head", axis=0)
    pack = jnp.broadcast_to(pack.reshape((1, 2, 2) + mine.shape), (4, 2, 2) + mine.shape).reshape((8, 2) + mine.shape)
    pack_send = pack
    pack = lax.all_to_all(pack, "row", 0, 0, axis_index_groups=planes, tiled=True)
    dy_four = deal(out_grad, later(c, x_half))
    dy_half = jnp.zeros((heads_n, quarter, half), bf16)
    for d in range(heads_n):
        part = lax.dynamic_index_in_dim(dy_four, z ^ d, 0, keepdims=False)
        dy_half = lax.dynamic_update_index_in_dim(dy_half, move(part, d) if d else part, z ^ d, 0)
    dy_half = dy_half.reshape(width, half).T

    shift = c * half
    seg = lax.dynamic_slice_in_dim(jnp.concatenate([seg, seg]), shift, length, 0)
    hits = []
    for own in lists:
        own = lax.dynamic_slice_in_dim(jnp.concatenate([own, own], 1), shift // BLK, length // BLK, 1)
        hit = hit_lanes(own, length)
        hits.append(lax.dynamic_slice_in_dim(jnp.concatenate([hit, hit], 2), shift, length, 2))

    def mm(a, b, dims):
        return lax.dot_general(a, b, (dims, ((), ())), preferred_element_type=f32)

    xhat1, scale1 = norm_rows(x)
    n1_half = (xhat1 * input_norm_gain + input_norm_bias).astype(bf16)
    n1 = jnp.concatenate([n1_half, move(n1_half, 4)], 0)
    att = []
    for i in range(2):
        att.append(attn_fwd(at, n1, wq_pieces, i, seg, hits[i], feature_proj, (pack_send, dy_half) if i else ()))
    qkv = [v[4] for v in att]
    wq = [v[5].reshape(width, -1) for v in att]
    outs = pack[:, :, n_up + n_hid:].transpose(1, 0, 2, 3).reshape(2, -1, width)
    outw = [lax.dynamic_index_in_dim(outs, i, 0, keepdims=False) for i in (par, 1 - par)]
    heads_out = [v[0] for v in att]

    away = (mm(heads_out[0][half:], outw[0], nn) + mm(heads_out[1][half:], outw[1], nn)).astype(bf16)
    near = mm(heads_out[0][:half], outw[0], nn) + mm(heads_out[1][:half], outw[1], nn)
    resid = x + near + move(away, 4).astype(f32)
    xhat2, scale2 = norm_rows(resid.astype(bf16).astype(f32))
    n2_half = (xhat2 * middle_norm_gain + middle_norm_bias).astype(bf16)
    n2 = jnp.concatenate([n2_half, move(n2_half, 4)], 0)
    dy = jnp.concatenate([dy_half, move(dy_half, 4)], 0)
    acted, d_pre, dn_own, dn_oth = mlp_first(n2, dy, pack, n_hid)
    d_n2 = dn_own + move(dn_oth, 4).astype(f32)
    mo_own, mo_oth, grads = mlp_second(n2, dy, acted, d_pre, pack, n_hid)
    block_half = (resid + mo_own + move(mo_oth, 4).astype(f32)).astype(bf16)
    block_got = deal_z(block_half.T.reshape(heads_n, quarter, half))
    block_out = collect(block_got)
    d_resid = dy_half.astype(f32) + norm_back(d_n2, xhat2, scale2, middle_norm_gain)
    d_half = d_resid.astype(bf16)
    d_branch = jnp.concatenate([d_half, move(d_half, 4)], 0)
    grads = lax.psum_scatter(
        grads.reshape(-1, width), "row", scatter_dimension=0, axis_index_groups=quads, tiled=True
    ).reshape(2, 2, -1, width)
    keep = lax.dynamic_index_in_dim(grads, c, 0, keepdims=False)
    got = move(lax.dynamic_index_in_dim(grads, 1 - c, 0, keepdims=False), 4)
    four = jnp.concatenate([jnp.where(c == 0, keep, got), jnp.where(c == 0, got, keep)], 0)
    four_flat = four.reshape(-1, width)
    mlp_slice = mlp_grads = lax.psum_scatter(four_flat, "head", scatter_dimension=0, tiled=True)
    if groups > 1:
        mlp_grads = lax.psum(mlp_grads, "row", axis_index_groups=[[8 * g + i for g in range(groups)] for i in range(8)])
    mlp_grads = gather_plane(mlp_grads)
    up_grad = mlp_grads[:, :n_up].reshape(width, -1).astype(f32)
    down_grad = mlp_grads[:, n_up:].reshape(-1, width).astype(f32)

    def sum_plane(v):
        v = lax.all_to_all(v, "row", 0, 0, axis_index_groups=quads, tiled=True)
        return jnp.sum(v.astype(f32), 0).astype(bf16)

    out_g = [mm(v, d_branch, tn).astype(bf16).reshape(4, -1, cols) for v in heads_out]
    n_outg = out_g[0].shape[1]
    d_qkv, qkv_g = [], []
    for i in range(2):
        d_heads = mm(d_branch, outw[i], nt).astype(bf16)
        ahead = (block_got, four_flat) if i else (mo_oth,)
        d_qkv.append(attn_bwd(qkv[i], seg, hits[i], feature_proj, *att[i][1:4], heads_out[i], d_heads, ahead))
        part = mm(n1, d_qkv[i], tn)
        if i:
            part = tied(tied(part, qkv_g[0]), mlp_slice)
        part = part.astype(bf16).reshape(4, n_qkv, -1)
        qkv_g.append(sum_plane(part if i else jnp.concatenate([part] + out_g, 1)))
    first, second = qkv_g
    second = tied(second, mlp_grads)
    qkv_g = [first[:n_qkv + n_outg], jnp.concatenate([second, first[n_qkv + n_outg:]], 0)]
    away = (mm(d_qkv[0][half:], wq[0], nt) + mm(d_qkv[1][half:], wq[1], nt)).astype(bf16)
    near = mm(d_qkv[0][:half], wq[0], nt) + mm(d_qkv[1][:half], wq[1], nt)
    d_n1 = near + move(away, 4).astype(f32)
    d_in = norm_back(d_n1, xhat1, scale1, input_norm_gain)
    vec = jnp.stack([jnp.sum(d_n1 * xhat1, 0), jnp.sum(d_n1, 0), jnp.sum(d_n2 * xhat2, 0), jnp.sum(d_n2, 0)])

    def split(v):
        high = v.astype(bf16)
        return jnp.concatenate([high, (v - high.astype(f32)).astype(bf16)], 0)

    ride = 128
    rider = jnp.pad(split(vec).reshape(8, heads_n, quarter).transpose(1, 2, 0), ((0, 0), (0, 0), (0, ride - 8)))
    send = (d_resid + d_in).astype(bf16).T.reshape(heads_n, quarter, half)
    got = deal_z(jnp.concatenate([send, rider], 2))
    input_grad = collect(got[:, :, :half]).astype(f32)
    vec = jnp.sum(got[:, :, half:half + 8].astype(f32), 0).T
    rider = split(vec[:4] + vec[4:]).reshape(-1)
    rider = jnp.pad(rider, (0, extra * cols - rider.shape[0])).reshape(extra, cols)
    got = gather_plane(jnp.concatenate([give_z(*qkv_g), rider], 0))
    n_half = got.shape[1] - extra
    both = got[:, :n_half].reshape(4, 2 * n_half, cols)
    qkv_grad = both[:, :n_qkv].reshape(width, -1).astype(f32)
    out_w_grad = both[:, n_qkv:].reshape(-1, width).astype(f32)
    vec = jnp.sum(got[:, n_half:].astype(f32), 0)
    vec = vec.reshape(-1)[:8 * quarter].reshape(2, 4, quarter)
    vec = vec[0] + vec[1]
    if groups > 1:
        vec = lax.psum(vec, "row", axis_index_groups=[[8 * g + i for g in range(groups)] for i in range(8)])
    return (
        block_out, input_grad, vec[0], vec[1], qkv_grad, out_w_grad, vec[2], vec[3], up_grad, down_grad,
    )


def solution(mesh):
    return jax.shard_map(
        shards,
        mesh=mesh,
        in_specs=(
            P("row", "head"), P("row", None), P("row", "head", None, None), P(), P(), P(), P(None, "head"),
            P("head", None), P(), P(), P(None, "head"), P("head", None), P("row", "head"),
        ),
        out_specs=(
            P("row", "head"), P("row", "head"), P("head"), P("head"), P(None, "head"), P("head", None),
            P("head"), P("head"), P(None, "head"), P("head", None),
        ),
        check_vma=False,
    )
```

time: 628 us -> 470 us (0.75)
  waiting for transfers between devices: 196 us -> 92.6 us
  starting transfers between devices: 132 us -> 62 us
  Pallas kernels: 107 us -> 144 us
  matrix products: 66.7 us -> 30.4 us
  other arithmetic: 25.3 us -> 48.1 us
  between operations: 2.93 us -> 20.9 us
  blocking collectives: 15.6 us -> 0 us
  local copies, waits for them, and re-layouts: 73.7 us -> 64.4 us
    ppermute x74 -> x27, waiting for transfers between devices: 196 us -> 41.5 us  [move(): return lax.ppermute(v, ('row', 'head'), moves)]
    ppermute x74 -> x27, starting transfers between devices: 132 us -> 32.2 us  [move(): return lax.ppermute(v, ('row', 'head'), moves)]
    pallas_call x2 -> x6, Pallas kernels: 107 us -> 144 us  [the longest x2 60.5 us: attn_bwd(): pl.pallas_call(partial(bwd_kernel, tq=tq, tk=tk, dh=dh), in_specs=[pl.Blo...]
    dot_general x16 -> x14, matrix products: 66.7 us -> 30.4 us  [mm(): return lax.dot_general(a, b, (dims, ((), ())), preferred_element_type=f32)]
    all_to_all x0 -> x6, waiting for transfers between devices: none -> 34.7 us  [the longest x3 26.8 us: deal_z(): return lax.all_to_all(v, 'head', 0, 0, tiled=True)]
    all_to_all x0 -> x6, starting transfers between devices: none -> 29.7 us  [the longest x3 16 us: deal_z(): return lax.all_to_all(v, 'head', 0, 0, tiled=True)]
    all_gather x0 -> x3, waiting for transfers between devices: none -> 16.2 us  [the longest x2 16.2 us: gather_plane(): return lax.all_gather(v, 'row', axis=0, axis_index_groups=planes)]
    all_gather x1 -> x0, blocking collectives: 15.6 us -> none  [shards(): lists_all = lax.all_gather(block_lists, 'head', axis=1, tiled=True)]
  transfers between devices with their start and end apart: 74 -> 38, of which waited for: 29 -> 16; matrix products, arithmetic and copies ran while one was open for 22% -> 25% of each run, Pallas kernels for 7% -> 24%
where the time goes in v2:
time: 470 us; the launch traced here: 462 us
  Pallas kernels  144 us (31%)
  waiting for transfers between devices  92.6 us (20%)
  local copies, waits for them, and re-layouts  64.4 us (14%)
  starting transfers between devices  62 us (13%)
  other arithmetic  48.1 us (10%)
  matrix products  30.4 us (6%)
  between operations  20.9 us (4%)
    pallas_call x2, Pallas kernels, attn_bwd(): pl.pallas_call(partial(bwd_kernel, tq=tq, tk=tk, dh=dh), in_specs=[pl.Blo...  60.5 us
    pallas_call x2, Pallas kernels, attn_fwd(): pl.pallas_call(partial(fwd_kernel, tq=tq, tk=tk, dh=dh, part=part), in_sp...  48.3 us
    ppermute x27, waiting for transfers between devices, move(): return lax.ppermute(v, ('row', 'head'), moves)  41.5 us
    ppermute x27, starting transfers between devices, move(): return lax.ppermute(v, ('row', 'head'), moves)  32.2 us
    dot_general x14, matrix products, mm(): return lax.dot_general(a, b, (dims, ((), ())), preferred_element_type=f32)  30.4 us
    all_to_all x3, waiting for transfers between devices, deal_z(): return lax.all_to_all(v, 'head', 0, 0, tiled=True)  26.8 us
    pallas_call x1, Pallas kernels, mlp_first(): pl.pallas_call(partial(mlp_kernel, tile=tile, rows=rows), grid=(parts,),...  21.2 us
    all_gather x2, waiting for transfers between devices, gather_plane(): return lax.all_gather(v, 'row', axis=0, axis_index_groups=planes)  16.2 us
  transfers between devices with their start and end apart: 38, of which 16 were waited for; matrix products, arithmetic and copies ran while one was open for 25% of the time, Pallas kernels for 24%

profile of v2, /device:TPU:0, one launch (start us, length us, event | category | flops | bytes accessed | tf_op | source)
XLA Modules:
  0.0 462.1 jit_solution(8873853291306183704)
XLA Ops:
  13.4 5.9 %collective-permute-start.3 = (bf16[208,576]{1,0:T(8,128)(2,1)S(1)}, bf16[208,576]{1,0:T(8,128)(2,1)S(1)}, u32[]{:S(2)}, u32[]{:S(2)}) collective-permute-start(bf16[208,576]{1,0:T(8,128)(2,1)S(1)} %pad_maximum_fusion.14), channel_id=1, source_target_pairs={{0,2},{1,3},{6,4},{7,5},{8,10},{9,11},{14,12},{15,13},{16,18},{17,... | collective-permute-start | bytes 718856 | tf_op jit(solution)/shard_map/ppermute | solution.py:425
  20.3 3.5 collective-permute-start.4
  23.8 2.0 collective-permute-start.5
  26.2 9.9 %collective-permute-done.4 = bf16[208,576]{1,0:T(8,128)(2,1)S(1)} collective-permute-done((bf16[208,576]{1,0:T(8,128)(2,1)S(1)}, bf16[208,576]{1,0:T(8,128)(2,1)S(1)}, u32[]{:S(2)}, u32[]{:S(2)}) %collective-permute-start.4) | collective-permute-done | bytes 239648 | tf_op jit(solution)/shard_map/ppermute | solution.py:425
  38.7 7.1 %all-to-all-start = ((bf16[4,192,512]{2,1,0:T(8,128)(2,1)}), bf16[4,192,512]{2,1,0:T(8,128)(2,1)S(1)}, u32[]{:S(2)}, u32[]{:S(2)}) async-start(bf16[4,192,512]{2,1,0:T(8,128)(2,1)} %pad_maximum_fusion.6), calls=%async_computation | async-start | bytes 1572864 | tf_op jit(solution)/shard_map/all_to_all | solution.py:432
  51.2 18.5 %all-to-all-done = bf16[4,192,512]{2,1,0:T(8,128)(2,1)S(1)} async-done(((bf16[4,192,512]{2,1,0:T(8,128)(2,1)}), bf16[4,192,512]{2,1,0:T(8,128)(2,1)S(1)}, u32[]{:S(2)}, u32[]{:S(2)}) %all-to-all-start) | async-done | bytes 786464 | tf_op jit(solution)/shard_map/all_to_all | solution.py:432
  83.7 4.1 broadcast_in_dim.40
  87.8 4.8 %all-to-all-start.1 = ((bf16[8,2,216,768]{3,2,1,0:T(8,128)(2,1)}), bf16[8,2,216,768]{3,2,1,0:T(8,128)(2,1)}, u32[]{:S(2)}, u32[]{:S(2)}) async-start(bf16[8,2,216,768]{3,2,1,0:T(8,128)(2,1)} %bitcast.216), calls=%async_computation.1 | async-start | bytes 10616832 | tf_op jit(solution)/shard_map/all_to_all | solution.py:504
  92.7 3.3 collective-permute-start.11
  97.0 8.5 %collective-permute-done.11 = bf16[192,512]{1,0:T(8,128)(2,1)S(1)} collective-permute-done((bf16[192,512]{1,0:T(8,128)(2,1)}, bf16[192,512]{1,0:T(8,128)(2,1)S(1)}, u32[]{:S(2)}, u32[]{:S(2)}) %collective-permute-start.11) | collective-permute-done | bytes 196640 | tf_op jit(solution)/shard_map/ppermute | solution.py:425
  105.5 2.6 collective-permute-start.12
  108.1 6.1 %collective-permute-done.12 = bf16[192,512]{1,0:T(8,128)(2,1)S(1)} collective-permute-done((bf16[192,512]{1,0:T(8,128)(2,1)S(1)}, bf16[192,512]{1,0:T(8,128)(2,1)S(1)}, u32[]{:S(2)}, u32[]{:S(2)}) %collective-permute-start.12) | collective-permute-done | bytes 196640 | tf_op jit(solution)/shard_map/ppermute | solution.py:425
  116.6 2.6 pad_maximum_fusion.1.n_ref
  121.1 24.2 %attn_fwd.2 = (bf16[1024,192]{1,0:T(8,128)(2,1)S(1)}, bf16[3,1024,256]{2,1,0:T(8,128)(2,1)}, bf16[3,1024,256]{2,1,0:T(8,128)(2,1)}, f32[3,1024,1]{2,1,0:T(8,128)...) custom-call(s32[1]{0:T(128)} %bitcast.10.at_ref, s32[1,1024]{1,0:T(1,128)S(1)} %bitcast.207, ...), custom_call_target="tpu_custom_call" | custom-call | flops 27000000512 | bytes 10000000 | tf_op jit(solution)/shard_map/attn_fwd/pallas_call | solution.py:96
  149.7 24.1 %attn_fwd.3 = (bf16[1024,192]{1,0:T(8,128)(2,1)S(1)}, bf16[3,1024,256]{2,1,0:T(8,128)(2,1)}, bf16[3,1024,256]{2,1,0:T(8,128)(2,1)}, f32[3,1024,1]{2,1,0:T(8,128)...) custom-call(s32[1]{0:T(128)} %bitcast.10.at_ref, s32[1,1024]{1,0:T(1,128)S(1)} %bitcast.209, ...), custom_call_target="tpu_custom_call" | custom-call | flops 27000000512 | bytes 10000000 | tf_op jit(solution)/shard_map/attn_fwd/pallas_call | solution.py:96
  181.1 2.0 collective-permute-done.14
  183.2 21.2 %mlp_first.1 = (bf16[1024,1536]{1,0:T(8,128)(2,1)}, bf16[1024,1536]{1,0:T(8,128)(2,1)}, f32[512,768]{1,0:T(8,128)S(1)}, bf16[512,768]{1,0:T(8,128)(2,1)S(1)}) custom-call(bf16[1024,768]{1,0:T(8,128)(2,1)S(1)} %pad_maximum_fusion.2.n_ref, bf16[1024,768]{1,0:T(8,128)(2,1)S(1)} %pad_maximum_fusion.3.dy_ref, ...), custom_call_target="tpu_custom_call" | custom-call | flops 24999999488 | bytes 20000000 | tf_op jit(solution)/shard_map/mlp_first/pallas_call | solution.py:292
  205.4 13.7 %mlp_second.1 = (f32[512,768]{1,0:T(8,128)S(1)}, bf16[512,768]{1,0:T(8,128)(2,1)S(1)}, bf16[4,2,2,192,768]{4,3,2,1,0:T(8,128)(2,1)}) custom-call(bf16[1024,768]{1,0:T(8,128)(2,1)S(1)} %pad_maximum_fusion.2.n_ref, bf16[1024,768]{1,0:T(8,128)(2,1)S(1)} %pad_maximum_fusion.3.dy_ref, bf16[1024,1536]{1,0:T(8,128)(2,1)} %get-tuple-element.31.act_ref, ...), custom_call_target="tpu_custom_call" | custom-call | flops 16999999488 | bytes 20000000 | tf_op jit(solution)/shard_map/mlp_second/pallas_call | solution.py:360
  223.7 2.1 fusion.28
  225.9 2.2 fusion.92
  228.5 3.5 fusion.32
  233.1 4.2 all-to-all-start.2
  240.3 2.3 convolution_convert_fusion.2
  243.6 2.8 convolution_convert_fusion.3
  246.4 2.2 reshape.288
  249.7 30.3 %attn_bwd.2 = bf16[1024,576]{1,0:T(8,128)(2,1)} custom-call(s32[1,1024]{1,0:T(1,128)S(1)} %bitcast.211, bf16[1024,576]{1,0:T(8,128)(2,1)} %copy-done.26, s32[1024,1]{1,0:T(8,128)S(1)} %copy-done.11, s32[1,1024]{1,0:T(1,128)S(1)} %bitcast.212, f32[3,16,1024]{2,1,0:T(8,128)S(1)} %copy-done.17, bf16[64,256]{1,0:T(8,128)(2,1)S(1)} %copy-done.18, ...), custom_call_target="tpu_custom_call" | custom-call | flops 38000001024 | bytes 20000000 | tf_op jit(solution)/shard_map/attn_bwd/pallas_call | solution.py:208
  285.1 3.8 convolution_convert_fusion
  288.9 2.3 copy.169
  291.2 2.7 pad_maximum_fusion
  296.3 4.5 all-to-all-start.4
  300.8 30.2 %attn_bwd.3 = bf16[1024,576]{1,0:T(8,128)(2,1)} custom-call(s32[1,1024]{1,0:T(1,128)S(1)} %bitcast.213, bf16[1024,576]{1,0:T(8,128)(2,1)} %get-tuple-element.42.qkv_ref, s32[1024,1]{1,0:T(8,128)S(1)} %copy-done.11, s32[1,1024]{1,0:T(1,128)S(1)} %bitcast.214, f32[3,16,1024]{2,1,0:T(8,128)S(1)} %copy-done.15, bf16[64,256]{1,0:T(8,128)(2,1)S(1)} %copy-done.18, ...), custom_call_target="tpu_custom_call" | custom-call | flops 38000001024 | bytes 20000000 | tf_op jit(solution)/shard_map/attn_bwd/pallas_call | solution.py:208
  331.0 3.1 fusion.34
  334.2 3.3 add_convert_fusion.1
  338.1 3.1 fusion.39
  345.4 2.1 fusion.37
  347.6 3.3 fusion.15
  353.2 3.4 add_convert_fusion
  356.6 2.2 copy.170
  358.8 4.4 all-to-all-start.5
  363.6 2.9 fusion.33
  369.1 7.9 %all-to-all-done.5 = bf16[4,192,576]{2,1,0:T(8,128)(2,1)} async-done(((bf16[4,192,576]{2,1,0:T(8,128)(2,1)}), bf16[4,192,576]{2,1,0:T(8,128)(2,1)}, u32[]{:S(2)}, u32[]{:S(2)}) %all-to-all-start.5) | async-done | bytes 884768 | tf_op jit(solution)/shard_map/all_to_all | solution.py:566
  376.9 4.7 %all-to-all-start.3 = ((bf16[4,192,640]{2,1,0:T(8,128)(2,1)}), bf16[4,192,640]{2,1,0:T(8,128)(2,1)S(1)}, u32[]{:S(2)}, u32[]{:S(2)}) async-start(bf16[4,192,640]{2,1,0:T(8,128)(2,1)} %fusion.31), calls=%async_computation.4 | async-start | bytes 1966080 | tf_op jit(solution)/shard_map/all_to_all | solution.py:432
  389.0 5.6 %reshape.292 = bf16[1179648]{0:T(1024)(128)(2,1)} reshape(bf16[1536,768]{1,0:T(8,128)(2,1)} %all-gather.9.cloned.1.call-done) | data formatting | bytes 4718592 | tf_op jit(solution)/shard_map/reshape | solution.py:435
  399.3 3.9 collective-permute-start.23
  403.3 8.3 %all-to-all-done.3 = bf16[4,192,640]{2,1,0:T(8,128)(2,1)S(1)} async-done(((bf16[4,192,640]{2,1,0:T(8,128)(2,1)}), bf16[4,192,640]{2,1,0:T(8,128)(2,1)S(1)}, u32[]{:S(2)}, u32[]{:S(2)}) %all-to-all-start.3) | async-done | bytes 983072 | tf_op jit(solution)/shard_map/all_to_all | solution.py:432
  412.6 3.8 collective-permute-done.24
  416.3 3.4 collective-permute-done.23
  430.3 16.2 %all-gather.11.cloned.1.call-done = bf16[1152,576]{1,0:T(8,128)(2,1)} async-done(((bf16[144,576]{1,0:T(8,128)(2,1)}), bf16[1152,576]{1,0:T(8,128)(2,1)}) %all-gather.11.cloned.1.call-update) | async-done | bytes 1327120 | tf_op jit(solution)/shard_map/all_gather | solution.py:474
  (335 shorter events, 102.1 us)
Async XLA Ops:
  7.2 76.5 %all-gather.7.cloned.1.call-start = ((), (), s32[]{:S(2)}) async-start(), calls=%async_computation.10 | async-start | bytes 1658880 | tf_op jit(solution)/shard_map/all_gather | solution.py:501
  9.0 4.1 collective-permute-start.1
  10.8 25.6 %collective-permute-start = (bf16[2,192,512]{2,1,0:T(8,128)(2,1)S(1)}, bf16[2,192,512]{2,1,0:T(8,128)(2,1)}, u32[]{:S(2)}, u32[]{:S(2)}) collective-permute-start(bf16[2,192,512]{2,1,0:T(8,128)(2,1)S(1)} %pad_maximum_fusion.9), channel_id=1, source_target_pairs={{0,4},{1,5},{2,6},{3,7},{4,0},{5,1},{6,2},{7,3},{8,12},{9,13},{10,... | collective-permute-start | bytes 1179656 | tf_op jit(solution)/shard_map/ppermute | solution.py:425
  13.4 12.8 %collective-permute-start.3 = (bf16[208,576]{1,0:T(8,128)(2,1)S(1)}, bf16[208,576]{1,0:T(8,128)(2,1)S(1)}, u32[]{:S(2)}, u32[]{:S(2)}) collective-permute-start(bf16[208,576]{1,0:T(8,128)(2,1)S(1)} %pad_maximum_fusion.14), channel_id=1, source_target_pairs={{0,2},{1,3},{6,4},{7,5},{8,10},{9,11},{14,12},{15,13},{16,18},{17,... | collective-permute-start | bytes 718856 | tf_op jit(solution)/shard_map/ppermute | solution.py:425
  20.3 15.9 %collective-permute-start.4 = (bf16[208,576]{1,0:T(8,128)(2,1)S(1)}, bf16[208,576]{1,0:T(8,128)(2,1)S(1)}, u32[]{:S(2)}, u32[]{:S(2)}) collective-permute-start(bf16[208,576]{1,0:T(8,128)(2,1)S(1)} %pad_maximum_fusion.14), channel_id=1, source_target_pairs={{0,1},{1,0},{6,7},{7,6},{8,9},{9,8},{14,15},{15,14},{16,17},{17,16... | collective-permute-start | bytes 718856 | tf_op jit(solution)/shard_map/ppermute | solution.py:425
  23.8 12.6 %collective-permute-start.5 = (bf16[208,576]{1,0:T(8,128)(2,1)S(1)}, bf16[208,576]{1,0:T(8,128)(2,1)}, u32[]{:S(2)}, u32[]{:S(2)}) collective-permute-start(bf16[208,576]{1,0:T(8,128)(2,1)S(1)} %pad_maximum_fusion.14), channel_id=1, source_target_pairs={{0,3},{1,2},{6,5},{7,4},{8,11},{9,10},{14,13},{15,12},{16,19},{17,... | collective-permute-start | bytes 718856 | tf_op jit(solution)/shard_map/ppermute | solution.py:425
  26.1 121.3 %copy-start.10 = (s32[1024,1]{1,0:T(8,128)}, s32[1024,1]{1,0:T(8,128)S(1)}, u32[]{:S(2)}) copy-start(s32[1024,1]{1,0:T(8,128)S(1)} %copy.154.segc_ref) | copy-start | bytes 12292
  36.5 83.6 %copy-start.12 = (bf16[2,192,576]{2,1,0:T(8,128)(2,1)}, bf16[2,192,576]{2,1,0:T(8,128)(2,1)S(1)}, u32[]{:S(2)}) copy-start(bf16[2,192,576]{2,1,0:T(8,128)(2,1)S(1)} %pad_maximum_fusion.7.rest_0_) | copy-start | bytes 1327108
  38.7 31.0 %all-to-all-start = ((bf16[4,192,512]{2,1,0:T(8,128)(2,1)}), bf16[4,192,512]{2,1,0:T(8,128)(2,1)S(1)}, u32[]{:S(2)}, u32[]{:S(2)}) async-start(bf16[4,192,512]{2,1,0:T(8,128)(2,1)} %pad_maximum_fusion.6), calls=%async_computation | async-start | bytes 1572864 | tf_op jit(solution)/shard_map/all_to_all | solution.py:432
  45.7 73.5 %collective-permute-start.6 = (bf16[2,192,576]{2,1,0:T(8,128)(2,1)S(1)}, bf16[2,192,576]{2,1,0:T(8,128)(2,1)S(1)}, u32[]{:S(2)}, u32[]{:S(2)}) collective-permute-start(bf16[2,192,576]{2,1,0:T(8,128)(2,1)S(1)} %pad_maximum_fusion.7.rest_0_), channel_id=1, source_target_pairs={{0,8},{1,9},{2,10},{3,11},{4,12},{5,13},{6,14},{7,15},{8,0},{9,1},... | collective-permute-start | bytes 1327112 | tf_op jit(solution)/shard_map/ppermute | solution.py:425
  47.3 71.9 %collective-permute-start.7 = (bf16[2,192,576]{2,1,0:T(8,128)(2,1)S(1)}, bf16[2,192,576]{2,1,0:T(8,128)(2,1)S(1)}, u32[]{:S(2)}, u32[]{:S(2)}) collective-permute-start(bf16[2,192,576]{2,1,0:T(8,128)(2,1)S(1)} %pad_maximum_fusion.7.rest_0_), channel_id=1, source_target_pairs={{0,16},{1,17},{2,18},{3,19},{4,20},{5,21},{6,22},{7,23},{8,24},{9,... | collective-permute-start | bytes 1327112 | tf_op jit(solution)/shard_map/ppermute | solution.py:425
  48.8 71.2 %collective-permute-start.8 = (bf16[2,192,576]{2,1,0:T(8,128)(2,1)S(1)}, bf16[2,192,576]{2,1,0:T(8,128)(2,1)}, u32[]{:S(2)}, u32[]{:S(2)}) collective-permute-start(bf16[2,192,576]{2,1,0:T(8,128)(2,1)S(1)} %pad_maximum_fusion.7.rest_0_), channel_id=1, source_target_pairs={{0,24},{1,25},{2,26},{3,27},{4,28},{5,29},{6,30},{7,31},{8,16},{9,... | collective-permute-start | bytes 1327112 | tf_op jit(solution)/shard_map/ppermute | solution.py:425
  71.9 10.4 %copy-start.27 = (bf16[768,512]{0,1:T(8,128)(2,1)}, bf16[768,512]{0,1:T(8,128)(2,1)S(1)}, u32[]{:S(2)}) copy-start(bf16[768,512]{0,1:T(8,128)(2,1)S(1)} %copy.149) | copy-start | bytes 2359300
  77.4 1.8 collective-permute-start.9
  80.4 12.4 %collective-permute-start.10 = (bf16[192,512]{1,0:T(8,128)(2,1)}, bf16[192,512]{1,0:T(8,128)(2,1)}, u32[]{:S(2)}, u32[]{:S(2)}) collective-permute-start(bf16[192,512]{1,0:T(8,128)(2,1)} %get-tuple-element.137), channel_id=1, source_target_pairs={{0,1},{1,0},{2,3},{3,2},{4,5},{5,4},{6,7},{7,6},{8,9},{9,8},{10,11... | collective-permute-start | bytes 589832 | tf_op jit(solution)/shard_map/ppermute | solution.py:425
  83.6 33.0 %collective-permute-start.2 = (bf16[512,768]{1,0:T(8,128)(2,1)}, bf16[512,768]{1,0:T(8,128)(2,1)}, u32[]{:S(2)}, u32[]{:S(2)}) collective-permute-start(bf16[512,768]{1,0:T(8,128)(2,1)} %fusion.14), channel_id=1, source_target_pairs={{0,4},{1,5},{2,6},{3,7},{4,0},{5,1},{6,2},{7,3},{8,12},{9,13},{10,... | collective-permute-start | bytes 2359304 | tf_op jit(solution)/shard_map/ppermute | solution.py:425
  83.7 36.4 %copy-start.16 = (f32[3,16,1024]{2,1,0:T(8,128)}, f32[3,16,1024]{2,1,0:T(8,128)S(1)}, u32[]{:S(2)}) copy-start(f32[3,16,1024]{2,1,0:T(8,128)S(1)} %fusion.71.hit_ref) | copy-start | bytes 589828
  87.8 86.0 %all-to-all-start.1 = ((bf16[8,2,216,768]{3,2,1,0:T(8,128)(2,1)}), bf16[8,2,216,768]{3,2,1,0:T(8,128)(2,1)}, u32[]{:S(2)}, u32[]{:S(2)}) async-start(bf16[8,2,216,768]{3,2,1,0:T(8,128)(2,1)} %bitcast.216), calls=%async_computation.1 | async-start | bytes 10616832 | tf_op jit(solution)/shard_map/all_to_all | solution.py:504
  92.7 187.3 %reduce-scatter.3.cloned.1.call-start = ((), (), s32[]{:S(2)}) async-start(), calls=%async_computation.8 | async-start | bytes 5898240 | tf_op jit(solution)/shard_map/reduce_scatter | solution.py:551
  92.7 12.8 %collective-permute-start.11 = (bf16[192,512]{1,0:T(8,128)(2,1)}, bf16[192,512]{1,0:T(8,128)(2,1)S(1)}, u32[]{:S(2)}, u32[]{:S(2)}) collective-permute-start(bf16[192,512]{1,0:T(8,128)(2,1)} %get-tuple-element.138), channel_id=1, source_target_pairs={{0,2},{1,3},{2,0},{3,1},{4,6},{5,7},{6,4},{7,5},{8,10},{9,11},{10,... | collective-permute-start | bytes 589832 | tf_op jit(solution)/shard_map/ppermute | solution.py:425
  105.5 8.8 %collective-permute-start.12 = (bf16[192,512]{1,0:T(8,128)(2,1)S(1)}, bf16[192,512]{1,0:T(8,128)(2,1)S(1)}, u32[]{:S(2)}, u32[]{:S(2)}) collective-permute-start(bf16[192,512]{1,0:T(8,128)(2,1)S(1)} %get-tuple-element.135), channel_id=1, source_target_pairs={{0,3},{1,2},{2,1},{3,0},{4,7},{5,6},{6,5},{7,4},{8,11},{9,10},{10,... | collective-permute-start | bytes 589832 | tf_op jit(solution)/shard_map/ppermute | solution.py:425
  119.2 26.1 %copy-start.21 = (bf16[2,192,576]{2,1,0:T(8,128)(2,1)}, bf16[2,192,576]{2,1,0:T(8,128)(2,1)S(1)}, u32[]{:S(2)}) copy-start(bf16[2,192,576]{2,1,0:T(8,128)(2,1)S(1)} %collective-permute-done.6.rest_1_) | copy-start | bytes 1327108
  121.1 26.4 %copy-start.14 = (f32[3,16,1024]{2,1,0:T(8,128)S(1)}, f32[3,16,1024]{2,1,0:T(8,128)}, u32[]{:S(2)}) copy-start(f32[3,16,1024]{2,1,0:T(8,128)} %fusion.69.hit_ref) | copy-start | bytes 589828
  121.1 26.4 %copy-start.25 = (bf16[2,192,576]{2,1,0:T(8,128)(2,1)S(1)}, bf16[2,192,576]{2,1,0:T(8,128)(2,1)}, u32[]{:S(2)}) copy-start(bf16[2,192,576]{2,1,0:T(8,128)(2,1)} %copy-done.23) | copy-start | bytes 1327108
  147.5 30.8 %copy-start.7 = (bf16[1024,192]{1,0:T(8,128)(2,1)}, bf16[1024,192]{1,0:T(8,128)(2,1)S(1)}, u32[]{:S(2)}) copy-start(bf16[1024,192]{1,0:T(8,128)(2,1)S(1)} %get-tuple-element.29.o_ref) | copy-start | bytes 1179652
  175.9 2.4 collective-permute-start.13
  176.0 5.0 %collective-permute-start.15 = (bf16[512,768]{1,0:T(8,128)(2,1)S(1)}, bf16[512,768]{1,0:T(8,128)(2,1)S(1)}, u32[]{:S(2)}, u32[]{:S(2)}) collective-permute-start(bf16[512,768]{1,0:T(8,128)(2,1)S(1)} %bitcast.200), channel_id=1, source_target_pairs={{0,4},{1,5},{2,6},{3,7},{4,0},{5,1},{6,2},{7,3},{8,12},{9,13},{10,... | collective-permute-start | bytes 2359304 | tf_op jit(solution)/shard_map/ppermute | solution.py:425
  180.8 2.4 collective-permute-start.14
  221.2 2.6 collective-permute-start.18
  221.4 7.1 %collective-permute-start.16 = (bf16[512,768]{1,0:T(8,128)(2,1)}, bf16[512,768]{1,0:T(8,128)(2,1)}, u32[]{:S(2)}, u32[]{:S(2)}) collective-permute-start(bf16[512,768]{1,0:T(8,128)(2,1)} %copy-done.19), channel_id=1, source_target_pairs={{0,4},{1,5},{2,6},{3,7},{4,0},{5,1},{6,2},{7,3},{8,12},{9,13},{10,... | collective-permute-start | bytes 2359304 | tf_op jit(solution)/shard_map/ppermute | solution.py:425
  228.1 9.3 %collective-permute-start.19 = (bf16[512,768]{1,0:T(8,128)(2,1)}, bf16[512,768]{1,0:T(8,128)(2,1)S(1)}, u32[]{:S(2)}, u32[]{:S(2)}) collective-permute-start(bf16[512,768]{1,0:T(8,128)(2,1)} %get-tuple-element.123), channel_id=1, source_target_pairs={{0,4},{1,5},{2,6},{3,7},{4,0},{5,1},{6,2},{7,3},{8,12},{9,13},{10,... | collective-permute-start | bytes 2359304 | tf_op jit(solution)/shard_map/ppermute | solution.py:425
  233.1 63.1 %all-to-all-start.2 = ((bf16[4,192,512]{2,1,0:T(8,128)(2,1)}), bf16[4,192,512]{2,1,0:T(8,128)(2,1)}, u32[]{:S(2)}, u32[]{:S(2)}) async-start(bf16[4,192,512]{2,1,0:T(8,128)(2,1)} %bitcast.39), calls=%async_computation.2 | async-start | bytes 1572864 | tf_op jit(solution)/shard_map/all_to_all | solution.py:432
  237.3 96.8 %reduce-scatter.5.cloned.1.call-start = ((), (), s32[]{:S(2)}) async-start(), calls=%async_computation.9 | async-start | bytes 1474560 | tf_op jit(solution)/shard_map/reduce_scatter | solution.py:558
  281.9 12.0 %collective-permute-start.20 = (bf16[2,192,768]{2,1,0:T(8,128)(2,1)}, bf16[2,192,768]{2,1,0:T(8,128)(2,1)}, u32[]{:S(2)}, u32[]{:S(2)}) collective-permute-start(bf16[2,192,768]{2,1,0:T(8,128)(2,1)} %dynamic-slice_bitcast_fusion), channel_id=1, source_target_pairs={{0,4},{1,5},{2,6},{3,7},{4,0},{5,1},{6,2},{7,3},{8,12},{9,13},{10,... | collective-permute-start | bytes 1769480 | tf_op jit(solution)/shard_map/ppermute | solution.py:425
  296.3 44.9 %all-to-all-start.4 = ((bf16[4,320,576]{2,1,0:T(8,128)(2,1)}), bf16[4,320,576]{2,1,0:T(8,128)(2,1)}, u32[]{:S(2)}, u32[]{:S(2)}) async-start(bf16[4,320,576]{2,1,0:T(8,128)(2,1)} %pad_maximum_fusion), calls=%async_computation.5 | async-start | bytes 3276800 | tf_op jit(solution)/shard_map/all_to_all | solution.py:566
  300.8 88.3 %all-gather.9.cloned.1.call-start = ((), (), s32[]{:S(2)}) async-start(), calls=%async_computation.11 | async-start | bytes 2654208 | tf_op jit(solution)/shard_map/all_gather | solution.py:474
  337.5 10.0 %collective-permute-start.21 = (bf16[512,768]{1,0:T(8,128)(2,1)}, bf16[512,768]{1,0:T(8,128)(2,1)}, u32[]{:S(2)}, u32[]{:S(2)}) collective-permute-start(bf16[512,768]{1,0:T(8,128)(2,1)} %add_convert_fusion.1), channel_id=1, source_target_pairs={{0,4},{1,5},{2,6},{3,7},{4,0},{5,1},{6,2},{7,3},{8,12},{9,13},{10,... | collective-permute-start | bytes 2359304 | tf_op jit(solution)/shard_map/ppermute | solution.py:425
  343.1 42.4 %copy-start.36 = (bf16[320,576]{1,0:T(8,128)(2,1)}, bf16[320,576]{1,0:T(8,128)(2,1)S(1)}, u32[]{:S(2)}) copy-start(bf16[320,576]{1,0:T(8,128)(2,1)S(1)} %reduce_sum.162) | copy-start | bytes 1105924
  358.8 18.1 %all-to-all-start.5 = ((bf16[4,192,576]{2,1,0:T(8,128)(2,1)}), bf16[4,192,576]{2,1,0:T(8,128)(2,1)}, u32[]{:S(2)}, u32[]{:S(2)}) async-start(bf16[4,192,576]{2,1,0:T(8,128)(2,1)} %bitcast.230), calls=%async_computation.7 | async-start | bytes 1966080 | tf_op jit(solution)/shard_map/all_to_all | solution.py:566
  376.9 34.7 %all-to-all-start.3 = ((bf16[4,192,640]{2,1,0:T(8,128)(2,1)}), bf16[4,192,640]{2,1,0:T(8,128)(2,1)S(1)}, u32[]{:S(2)}, u32[]{:S(2)}) async-start(bf16[4,192,640]{2,1,0:T(8,128)(2,1)} %fusion.31), calls=%async_computation.4 | async-start | bytes 1966080 | tf_op jit(solution)/shard_map/all_to_all | solution.py:432
  381.7 64.9 %all-gather.11.cloned.1.call-start = ((), (), s32[]{:S(2)}) async-start(), calls=%async_computation.12 | async-start | bytes 1658880 | tf_op jit(solution)/shard_map/all_gather | solution.py:474
  382.7 1.8 collective-permute-start.17
  386.3 30.0 %collective-permute-start.24 = (bf16[256,576]{1,0:T(8,128)(2,1)}, bf16[256,576]{1,0:T(8,128)(2,1)}, u32[]{:S(2)}, u32[]{:S(2)}) collective-permute-start(bf16[256,576]{1,0:T(8,128)(2,1)} %slice.248), channel_id=1, source_target_pairs={{2,0},{3,1},{4,6},{5,7},{10,8},{11,9},{12,14},{13,15},{18,16},{19,... | collective-permute-start | bytes 884744 | tf_op jit(solution)/shard_map/ppermute | solution.py:425
  398.0 18.3 %collective-permute-start.25 = (bf16[256,576]{1,0:T(8,128)(2,1)}, bf16[256,576]{1,0:T(8,128)(2,1)}, u32[]{:S(2)}, u32[]{:S(2)}) collective-permute-start(bf16[256,576]{1,0:T(8,128)(2,1)} %pad_maximum_fusion.13), channel_id=1, source_target_pairs={{2,1},{3,0},{4,7},{5,6},{10,9},{11,8},{12,15},{13,14},{18,17},{19,... | collective-permute-start | bytes 884744 | tf_op jit(solution)/shard_map/ppermute | solution.py:425
  399.3 20.5 %collective-permute-start.23 = (bf16[256,576]{1,0:T(8,128)(2,1)}, bf16[256,576]{1,0:T(8,128)(2,1)}, u32[]{:S(2)}, u32[]{:S(2)}) collective-permute-start(bf16[256,576]{1,0:T(8,128)(2,1)} %pad_maximum_fusion.13), channel_id=1, source_target_pairs={{0,1},{1,0},{6,7},{7,6},{8,9},{9,8},{14,15},{15,14},{16,17},{17,16... | collective-permute-start | bytes 884744 | tf_op jit(solution)/shard_map/ppermute | solution.py:425
  403.2 16.5 %copy-start.37 = (bf16[320,576]{1,0:T(8,128)(2,1)S(1)}, bf16[320,576]{1,0:T(8,128)(2,1)}, u32[]{:S(2)}) copy-start(bf16[320,576]{1,0:T(8,128)(2,1)} %copy-done.36) | copy-start | bytes 1105924
  412.5 12.1 %collective-permute-start.22 = (bf16[2,192,512]{2,1,0:T(8,128)(2,1)}, bf16[2,192,512]{2,1,0:T(8,128)(2,1)S(1)}, u32[]{:S(2)}, u32[]{:S(2)}) collective-permute-start(bf16[2,192,512]{2,1,0:T(8,128)(2,1)} %dynamic-slice_bitcast_fusion.1), channel_id=1, source_target_pairs={{0,4},{1,5},{2,6},{3,7},{4,0},{5,1},{6,2},{7,3},{8,12},{9,13},{10,... | collective-permute-start | bytes 1179656 | tf_op jit(solution)/shard_map/ppermute | solution.py:425
  421.1 1.7 collective-permute-start.26
  (50 other events, 147.3 us)
Sparse Core Ops, SparseCore 0:
  20.2 42.8 all-gather.6
  221.3 56.8 reduce-scatter.2
  296.4 30.5 reduce-scatter.4
  334.3 30.4 all-gather.8
  423.6 22.8 all-gather.10

commit v3 on v2

v3 whole, which is shorter than its diff:
```python
from functools import partial

import math
import jax, jax.numpy as jnp
from jax import lax
from jax.experimental import pallas as pl
from jax.experimental.pallas import tpu as pltpu

BLK = 64
LOG2E = 1.4426950408889634

def dot(a, b, dims):
    return lax.dot_general(a, b, (dims, ((), ())), preferred_element_type=jnp.float32)

def meets(seg_ref, r0, tq, c0, tk):
    return (seg_ref[0, r0] <= seg_ref[0, c0 + tk - 1]) & (seg_ref[0, c0] <= seg_ref[0, r0 + tq - 1])

def fwd_kernel(at_ref, seg_s, own_ref, oth_ref, segc_ref, segr_ref, hit_ref, proj_ref, *rest, tq, tk, dh, part):
    out_ref, qf_ref, kf_ref, rinv_ref, qkv_ref, w_ref, wo_ref, *sums, done_ref, vext, sems = rest[-(11 if part == 0 else 12):]
    done_ref[0] = 0
    cut = w_ref.shape[1]
    slots = [at_ref[0] ^ d for d in range(4)]
    copies = [
        pltpu.make_async_copy(piece.at[part, pl.ds(0, cut), :], w_ref.at[slots[d]], sems.at[0, d])
        for d, piece in enumerate(rest[:4])
    ] + [
        pltpu.make_async_copy(piece.at[part, pl.ds(cut, wo_ref.shape[1]), :], wo_ref.at[slots[d]], sems.at[1, d])
        for d, piece in enumerate(rest[:4])
    ]
    for copy in copies:
        copy.start()
    for copy in copies:
        copy.wait()
    weights = w_ref[...].reshape(qkv_ref.shape[1], own_ref.shape[1])
    for side, n_ref in enumerate((own_ref, oth_ref)):
        def project(i, _, base=side * own_ref.shape[0], n_ref=n_ref):
            r0 = pl.multiple_of(i * 256, 256)
            qkv_ref[pl.ds(base + r0, 256), :] = dot(n_ref[pl.ds(r0, 256), :], weights, ((1,), (1,))).astype(jnp.bfloat16)
            return 0

        lax.fori_loop(0, n_ref.shape[0] // 256, project, 0)
    length = qkv_ref.shape[0]
    feats = proj_ref.shape[1]
    quarter = dh ** (-0.25)
    nh = qkv_ref.shape[1] // (3 * dh)
    for h in range(nh):
        base = h * 3 * dh
        for j, f_ref in ((0, qf_ref), (1, kf_ref)):
            def feat_body(i, _, base=base, j=j, f_ref=f_ref, h=h):
                rows = pl.ds(pl.multiple_of(i * 256, 256), 256)
                t = qkv_ref[rows, base + j * dh: base + (j + 1) * dh]
                lin = dot(t, proj_ref[...], ((1,), (0,)))
                tw = t.astype(jnp.float32)
                sq = jnp.sum(tw * tw, axis=1, keepdims=True) * (0.5 * quarter * quarter * LOG2E) + 0.5 * math.log2(feats)
                f_ref[h, rows, :] = jnp.exp2(lin * (quarter * LOG2E) - sq).astype(jnp.bfloat16)
                return 0
            lax.fori_loop(0, length // 256, feat_body, 0)
        v = qkv_ref[:, base + 2 * dh: base + 3 * dh]
        lane = lax.broadcasted_iota(jnp.int32, (length, dh), 1)
        vext[h, :, :] = jnp.concatenate([v, (lane < 1).astype(jnp.bfloat16)], axis=1)

    def q_body(i, _):
        r0 = pl.multiple_of(i * tq, tq)
        qs = [qkv_ref[pl.ds(r0, tq), h * 3 * dh: h * 3 * dh + dh] for h in range(nh)]
        qfs = [qf_ref[h, pl.ds(r0, tq), :] for h in range(nh)]
        segq = segc_ref[pl.ds(r0, tq), :]
        def k_body(j, acc):
            c0 = pl.multiple_of(j * tk, tk)
            same = segq == segr_ref[:, pl.ds(c0, tk)]
            new = []
            for h in range(nh):
                k = qkv_ref[pl.ds(c0, tk), h * 3 * dh + dh: h * 3 * dh + 2 * dh]
                s = dot(qs[h], k, ((1,), (1,)))
                e = jnp.exp2(s * (LOG2E * dh ** -0.5))
                a = dot(qfs[h], kf_ref[h, pl.ds(c0, tk), :], ((1,), (1,)))
                parts = []
                for b in range(tq // BLK):
                    hit = hit_ref[h, pl.ds(i * (tq // BLK) + b, 1), pl.ds(c0, tk)] > 0.5
                    rs = slice(b * BLK, (b + 1) * BLK)
                    parts.append(jnp.where(jnp.broadcast_to(hit, (BLK, tk)), e[rs], a[rs]))
                comb = jnp.where(same, jnp.concatenate(parts, axis=0), 0.0).astype(jnp.bfloat16)
                new.append(acc[h] + dot(comb, vext[h, pl.ds(c0, tk), :], ((1,), (0,))))
            return tuple(new)
        def k_step(j, acc):
            return lax.cond(meets(seg_s, r0, tq, pl.multiple_of(j * tk, tk), tk), lambda a: k_body(j, a), lambda a: a, acc)
        acc = lax.fori_loop(0, length // tk, k_step, tuple(jnp.zeros((tq, 2 * dh), jnp.float32) for _ in range(nh)))
        for h in range(nh):
            rinv = 1.0 / acc[h][:, dh:dh + 1]
            out_ref[pl.ds(r0, tq), h * dh:(h + 1) * dh] = (acc[h][:, :dh] * rinv).astype(jnp.bfloat16)
            rinv_ref[h, pl.ds(r0, tq), :] = rinv
        return 0
    lax.fori_loop(0, length // tq, q_body, 0)

    w_out = wo_ref[...].reshape(out_ref.shape[1], own_ref.shape[1])
    add_parts(lambda rows: dot(out_ref[rows, :], w_out, ((1,), (0,))), None if part == 0 else rest[4], sums, length, part == 0)


def add_parts(product, before, sums, length, first):
    half = length // 2

    def body(i, _):
        rows = pl.ds(pl.multiple_of(i * 256, 256), 256)
        part = product(rows)
        if first:
            sums[0][rows, :] = part
        else:
            total = part + before[rows, :]
            @pl.when(i < half // 256)
            def _():
                sums[0][rows, :] = total
            @pl.when(i >= half // 256)
            def _():
                sums[1][pl.ds(pl.multiple_of(i * 256 - half, 256), 256), :] = total.astype(jnp.bfloat16)
        return 0

    lax.fori_loop(0, length // 256, body, 0)


def sum_shapes(length, width, first):
    whole = lambda n, dtype: jax.ShapeDtypeStruct((n, width), dtype)
    return [whole(length, jnp.float32)] if first else [whole(length // 2, jnp.float32), whole(length // 2, jnp.bfloat16)]


def attn_fwd(at, n_own, n_oth, pieces, part, seg, hit, proj, before=None, ahead=(), *, tq=512, tk=256):
    length, width = 2 * n_own.shape[0], n_own.shape[1]
    dh, feats = proj.shape
    heads = hit.shape[0]
    cols = 3 * heads * dh
    seg2 = seg.reshape(1, length)
    first = before is None
    smem = pl.BlockSpec(memory_space=pltpu.SMEM)
    vmem = pl.BlockSpec(memory_space=pltpu.VMEM)
    anywhere = pl.BlockSpec(memory_space=pltpu.HBM)
    return pl.pallas_call(
        partial(fwd_kernel, tq=tq, tk=tk, dh=dh, part=part),
        in_specs=[smem] * 2 + [vmem] * 6 + [anywhere] * 4 + [vmem] * (not first) + [anywhere] * len(ahead),
        out_specs=[vmem] * (8 if first else 9) + [smem],
        out_shape=[
            jax.ShapeDtypeStruct((length, heads * dh), jnp.bfloat16),
            jax.ShapeDtypeStruct((heads, length, feats), jnp.bfloat16),
            jax.ShapeDtypeStruct((heads, length, feats), jnp.bfloat16),
            jax.ShapeDtypeStruct((heads, length, 1), jnp.float32),
            jax.ShapeDtypeStruct((length, cols), jnp.bfloat16),
            jax.ShapeDtypeStruct((4, cols // 4, width), jnp.bfloat16),
            jax.ShapeDtypeStruct((4, heads * dh // 4, width), jnp.bfloat16),
        ]
        + sum_shapes(length, width, first)
        + [jax.ShapeDtypeStruct((1,), jnp.int32)],
        scratch_shapes=[pltpu.VMEM((heads, length, 2 * dh), jnp.bfloat16), pltpu.SemaphoreType.DMA((2, 4))],
        compiler_params=pltpu.CompilerParams(vmem_limit_bytes=48 * 1024 * 1024),
        cost_estimate=pl.CostEstimate(flops=27 * 10**9, bytes_accessed=10**7, transcendentals=10**6),
        name="attn_fwd",
    )(at, seg2, n_own, n_oth, seg.reshape(length, 1), seg2, hit, proj, *pieces, *(() if first else (before,)), *ahead)


def bwd_kernel(at_ref, seg_s, qkv_ref, segc_ref, segr_ref, hit_ref, proj_ref, pext_ref, qf_ref, kf_ref, rinv_ref, o_ref,
               d_own, d_oth, w_out, n_own, n_oth, w_ref, *rest, tq, tk, dh, first):
    *outs, done_ref, dqkv_ref, do_ref, grad_s, vext, doext, dq, dk, dv, dqf, dkf = rest[-(13 if first else 17):]
    sums = outs[1:] if first else outs[4:]
    done_ref[0] = 0
    length = qkv_ref.shape[0]
    half = length // 2
    quarter = dh ** (-0.25)
    nh = qkv_ref.shape[1] // (3 * dh)
    for side, d_ref in enumerate((d_own, d_oth)):
        do_ref[side * half:(side + 1) * half, :] = dot(d_ref[...], w_out[...], ((1,), (1,))).astype(jnp.bfloat16)
    lane = lax.broadcasted_iota(jnp.int32, (length, dh), 1)
    for h in range(nh):
        base = h * 3 * dh
        v = qkv_ref[:, base + 2 * dh: base + 3 * dh]
        vext[h, :, :] = jnp.concatenate([v, (lane < 2).astype(jnp.bfloat16)], axis=1)
        d_o = do_ref[:, h * dh:(h + 1) * dh].astype(jnp.float32)
        o = o_ref[:, h * dh:(h + 1) * dh].astype(jnp.float32)
        rinv = rinv_ref[h]
        delta = -jnp.sum(d_o * o, axis=1, keepdims=True) * rinv
        high = delta.astype(jnp.bfloat16).astype(jnp.float32)
        low = delta - high
        tail = jnp.where(lane == 0, high, jnp.where(lane == 1, low, 0.0))
        doext[h, :, :] = jnp.concatenate([d_o * rinv, tail], axis=1).astype(jnp.bfloat16)
    dq[...] = jnp.zeros_like(dq)
    dk[...] = jnp.zeros_like(dk)
    dv[...] = jnp.zeros_like(dv)
    dqf[...] = jnp.zeros_like(dqf)
    dkf[...] = jnp.zeros_like(dkf)

    def q_body(i, _):
        r0 = pl.multiple_of(i * tq, tq)
        rows = pl.ds(r0, tq)
        segq = segc_ref[rows, :]
        def k_body(j, _):
            c0 = pl.multiple_of(j * tk, tk)
            cols = pl.ds(c0, tk)
            same = segq == segr_ref[:, cols]
            for h in range(nh):
                base = h * 3 * dh
                q = qkv_ref[rows, base: base + dh]
                k = qkv_ref[cols, base + dh: base + 2 * dh]
                qf = qf_ref[h, rows, :]
                kf = kf_ref[h, cols, :]
                s = dot(q, k, ((1,), (1,)))
                e = jnp.exp2(s * (LOG2E * dh ** -0.5))
                a = dot(qf, kf, ((1,), (1,)))
                dc = dot(doext[h, rows, :], vext[h, cols, :], ((1,), (1,)))
                dc = jnp.where(same, dc, 0.0)
                combs, dss, das = [], [], []
                for b in range(tq // BLK):
                    hit = hit_ref[h, pl.ds(i * (tq // BLK) + b, 1), cols] > 0.5
                    hit = jnp.broadcast_to(hit, (BLK, tk))
                    rs = slice(b * BLK, (b + 1) * BLK)
                    combs.append(jnp.where(hit, e[rs], a[rs]))
                    dss.append(jnp.where(hit, dc[rs] * e[rs], 0.0))
                    das.append(jnp.where(hit, 0.0, dc[rs]))
                comb = jnp.where(same, jnp.concatenate(combs, axis=0), 0.0).astype(jnp.bfloat16)
                ds = jnp.concatenate(dss, axis=0).astype(jnp.bfloat16)
                da = jnp.concatenate(das, axis=0).astype(jnp.bfloat16)
                dq[h, rows, :] += dot(ds, k, ((1,), (0,)))
                dqf[h, rows, :] += dot(da, kf, ((1,), (0,)))
                dk[h, cols, :] += dot(ds, q, ((0,), (0,)))
                dkf[h, cols, :] += dot(da, qf, ((0,), (0,)))
                dv[h, cols, :] += dot(comb, doext[h, rows, :dh], ((0,), (0,)))
            return 0
        def k_step(j, _):
            @pl.when(meets(seg_s, r0, tq, pl.multiple_of(j * tk, tk), tk))
            def _():
                k_body(j, 0)
            return 0
        lax.fori_loop(0, length // tk, k_step, 0)
        return 0
    lax.fori_loop(0, length // tq, q_body, 0)

    for h in range(nh):
        base = h * 3 * dh
        for j, dt, dfeat, f_ref in ((0, dq, dqf, qf_ref), (1, dk, dkf, kf_ref)):
            def back(i, _, base=base, j=j, dt=dt, dfeat=dfeat, f_ref=f_ref, h=h):
                rows = pl.ds(pl.multiple_of(i * 256, 256), 256)
                dpre = dfeat[h, rows, :] * f_ref[h, rows, :].astype(jnp.float32)
                hi_ = dpre.astype(jnp.bfloat16)
                lo_ = (dpre - hi_.astype(jnp.float32)).astype(jnp.bfloat16)
                thr = dot(hi_, pext_ref[...], ((1,), (0,))) + dot(lo_, pext_ref[...], ((1,), (0,)))
                t = qkv_ref[rows, base + j * dh: base + (j + 1) * dh].astype(jnp.float32)
                g = dt[h, rows, :] * dh ** -0.5 + quarter * thr[:, :dh] - (quarter * quarter) * t * thr[:, dh:dh + 1]
                dqkv_ref[rows, base + j * dh: base + (j + 1) * dh] = g.astype(jnp.bfloat16)
                return 0
            lax.fori_loop(0, length // 256, back, 0)
        dqkv_ref[:, base + 2 * dh: base + 3 * dh] = dv[h].astype(jnp.bfloat16)

    weights = w_ref[...].reshape(qkv_ref.shape[1], n_own.shape[1])
    add_parts(lambda rows: dot(dqkv_ref[rows, :], weights, ((1,), (0,))), rest[0], sums, length, first)

    tn = ((0,), (0,))
    cut = w_ref.shape[1]
    grad = dot(dqkv_ref[:half, :], n_own[...], tn) + dot(dqkv_ref[half:, :], n_oth[...], tn)
    grad_s[:, :cut, :] = grad.astype(jnp.bfloat16).reshape(4, cut, n_own.shape[1])
    out = dot(o_ref[:half, :], d_own[...], tn) + dot(o_ref[half:, :], d_oth[...], tn)
    grad_s[:, cut:, :] = out.astype(jnp.bfloat16).reshape(4, o_ref.shape[1] // 4, n_own.shape[1])
    if first:
        outs[0][...] = grad_s[...]
    else:
        for d in range(4):
            outs[d][...] = grad_s[at_ref[0] ^ d]


def attn_bwd(at, qkv, seg, hit, proj, qf, kf, rinv, o, d_own, d_oth, w_out, n_own, n_oth, wq, before=None, ahead=(), *, tq=512, tk=256):
    length = qkv.shape[0]
    dh, feats = proj.shape
    width = n_own.shape[1]
    heads = qkv.shape[1] // (3 * dh)
    seg2 = seg.reshape(1, length)
    pext = jnp.concatenate([proj.T, jnp.ones((feats, 1), proj.dtype), jnp.zeros((feats, dh - 1), proj.dtype)], axis=1)
    f32, bf16 = jnp.float32, jnp.bfloat16
    smem = pl.BlockSpec(memory_space=pltpu.SMEM)
    vmem = pl.BlockSpec(memory_space=pltpu.VMEM)
    anywhere = pl.BlockSpec(memory_space=pltpu.HBM)
    first = before is None
    piece = jax.ShapeDtypeStruct(((qkv.shape[1] + o.shape[1]) // 4, width), bf16)
    return pl.pallas_call(
        partial(bwd_kernel, tq=tq, tk=tk, dh=dh, first=first),
        in_specs=[smem] * 2 + [vmem] * (16 if first else 17) + [anywhere] * len(ahead),
        out_specs=[vmem] * (2 if first else 6) + [smem],
        out_shape=([jax.ShapeDtypeStruct((4,) + piece.shape, bf16)] if first else [piece] * 4) + sum_shapes(length, width, first)
        + [jax.ShapeDtypeStruct((1,), jnp.int32)],
        scratch_shapes=[
            pltpu.VMEM(qkv.shape, bf16),
            pltpu.VMEM(o.shape, bf16),
            pltpu.VMEM((4,) + piece.shape, bf16),
            pltpu.VMEM((heads, length, 2 * dh), bf16),
            pltpu.VMEM((heads, length, 2 * dh), bf16),
            pltpu.VMEM((heads, length, dh), f32),
            pltpu.VMEM((heads, length, dh), f32),
            pltpu.VMEM((heads, length, dh), f32),
            pltpu.VMEM((heads, length, feats), f32),
            pltpu.VMEM((heads, length, feats), f32),
        ],
        compiler_params=pltpu.CompilerParams(vmem_limit_bytes=56 * 1024 * 1024),
        cost_estimate=pl.CostEstimate(flops=42 * 10**9, bytes_accessed=2 * 10**7, transcendentals=10**6),
        name="attn_bwd",
    )(at, seg2, qkv, seg.reshape(length, 1), seg2, hit, proj, pext, qf, kf, rinv, o, d_own, d_oth, w_out, n_own, n_oth, wq,
      *(() if first else (before,)), *ahead)


def hit_lanes(lists, length):
    nb = lists.shape[1]
    ids = lax.broadcasted_iota(jnp.int32, (1, 1, length), 2) // BLK
    out = lists[:, :, 0:1] == ids
    for s in range(1, lists.shape[2]):
        out = out | (lists[:, :, s:s + 1] == ids)
    return out.astype(jnp.float32)

from jax.sharding import PartitionSpec as P


def gelu_pair(u):
    mag = jnp.abs(u)
    t = 1.0 / (1.0 + (0.3275911 * 0.7071067811865476) * mag)
    bell = jnp.exp2(u * u * (-0.5 * LOG2E))
    poly = t * (0.127414796 + t * (-0.142248368 + t * (0.7107068705 + t * (-0.7265760135 + t * 0.5307027145))))
    tail = poly * bell
    cdf = jnp.where(u >= 0.0, 1.0 - tail, tail)
    return u * cdf, cdf + u * bell * 0.3989422804014327


def mlp_kernel(n_own, n_oth, dy_own, dy_oth, w_ref, *rest, tile, rows, first):
    act_ref, dpre_ref, *sums, acc = rest[-(4 if first else 5):]
    half, width = n_own.shape
    piece = w_ref.shape[1] // 2
    hid = act_ref.shape[1]
    up = w_ref[:, :piece, :].reshape(width, hid)
    down = w_ref[:, piece:, :].reshape(hid, width)
    for j in range(hid // tile):
        up_t = up[:, j * tile:(j + 1) * tile]
        down_t = down[j * tile:(j + 1) * tile, :]
        for side, (n_ref, dy_ref) in enumerate(((n_own, dy_own), (n_oth, dy_oth))):
            def body(i, _, j=j, up_t=up_t, down_t=down_t, n_ref=n_ref, dy_ref=dy_ref, base=side * half):
                r0 = pl.multiple_of(i * rows, rows)
                src = pl.ds(r0, rows)
                rs = pl.ds(base + r0, rows)
                pre = dot(n_ref[src, :], up_t, ((1,), (0,)))
                d_act = dot(dy_ref[src, :], down_t, ((1,), (1,)))
                act, slope = gelu_pair(pre)
                d_pre = (d_act * slope).astype(jnp.bfloat16)
                act_ref[rs, j * tile:(j + 1) * tile] = act.astype(jnp.bfloat16)
                dpre_ref[rs, j * tile:(j + 1) * tile] = d_pre
                part = dot(d_pre, up_t, ((1,), (1,)))
                if j == 0 and first:
                    acc[rs, :] = part
                elif j == 0:
                    acc[rs, :] = part + rest[0][rs, :]
                else:
                    acc[rs, :] += part
                return 0
            lax.fori_loop(0, half // rows, body, 0)
    if first:
        sums[0][...] = acc[...]
    else:
        sums[0][...] = acc[:half, :]
        sums[1][...] = acc[half:, :].astype(jnp.bfloat16)


def mlp_first(n2, dy, pack, before=None, ahead=(), *, tile=256, rows=256):
    tokens, width = 2 * n2[0].shape[0], n2[0].shape[1]
    hid = pack.shape[0] * pack.shape[1] // 2
    bf16, f32 = jnp.bfloat16, jnp.float32
    first = before is None
    vmem = pl.BlockSpec(memory_space=pltpu.VMEM)
    return pl.pallas_call(
        partial(mlp_kernel, tile=tile, rows=rows, first=first),
        in_specs=[vmem] * (5 if first else 6) + [pl.BlockSpec(memory_space=pltpu.HBM)] * len(ahead),
        out_specs=[vmem] * (3 if first else 4),
        out_shape=[jax.ShapeDtypeStruct((tokens, hid), bf16)] * 2 + sum_shapes(tokens, width, first),
        scratch_shapes=[pltpu.VMEM((tokens, width), f32)],
        compiler_params=pltpu.CompilerParams(vmem_limit_bytes=48 * 1024 * 1024),
        cost_estimate=pl.CostEstimate(flops=12 * 10**9, bytes_accessed=2 * 10**7, transcendentals=10**6),
        name="mlp_first",
    )(*n2, *dy, pack, *(() if first else (before,)), *ahead)


def mlp_grad_kernel(n_own, n_oth, dy_own, dy_oth, act_ref, dpre_ref, w_ref, *rest, first):
    *sums, grad_ref = rest[-(2 if first else 3):]
    half, width = n_own.shape
    piece = w_ref.shape[1] // 2
    hid = act_ref.shape[1]
    down = w_ref[:, piece:, :].reshape(hid, width)
    tn = ((0,), (0,))
    add_parts(lambda rs: dot(act_ref[rs, :], down, ((1,), (0,))), None if first else rest[0], sums, 2 * half, first)
    for j in range(width // (4 * piece)):
        cut = slice(4 * j * piece, 4 * (j + 1) * piece)
        up_g = dot(n_own[:, cut], dpre_ref[:half, :], tn) + dot(n_oth[:, cut], dpre_ref[half:, :], tn)
        grad_ref[2 * j:2 * j + 2, :, 0, :piece, :] = up_g.astype(jnp.bfloat16).reshape(2, 2, piece, hid)
        down_g = dot(act_ref[:half, cut], dy_own[...], tn) + dot(act_ref[half:, cut], dy_oth[...], tn)
        grad_ref[2 * j:2 * j + 2, :, 0, piece:, :] = down_g.astype(jnp.bfloat16).reshape(2, 2, piece, width)


def mlp_second(n2, dy, acted, d_pre, pack, before=None, grads=None):
    tokens, width = 2 * n2[0].shape[0], n2[0].shape[1]
    bf16, f32 = jnp.bfloat16, jnp.float32
    first = before is None
    whole = lambda shape: pl.BlockSpec(shape, lambda i: (0,) * len(shape))
    args = [*n2, *dy, acted, d_pre, pack] + ([] if first else [before])
    sums = sum_shapes(tokens, width, first)
    shape = (4, 2, 2, pack.shape[1], width)
    return pl.pallas_call(
        partial(mlp_grad_kernel, first=first),
        grid=(1,),
        in_specs=[whole(v.shape) for v in args] + [pl.BlockSpec(memory_space=pltpu.HBM)] * (not first),
        out_specs=[whole(v.shape) for v in sums]
        + [pl.BlockSpec((4, 2, 1) + shape[3:], lambda i: (0, 0, 0 if first else 1, 0, 0))],
        out_shape=sums + [jax.ShapeDtypeStruct(shape, bf16)],
        input_output_aliases={} if first else {len(args): len(sums)},
        compiler_params=pltpu.CompilerParams(vmem_limit_bytes=48 * 1024 * 1024),
        cost_estimate=pl.CostEstimate(flops=8 * 10**9, bytes_accessed=2 * 10**7, transcendentals=0),
        name="mlp_second",
    )(*args, *([] if first else [grads]))


def call(kernel, name, args, outs, ahead=(), smem=(), scratch=(), passed=()):
    vmem = pl.BlockSpec(memory_space=pltpu.VMEM)
    anywhere = pl.BlockSpec(memory_space=pltpu.HBM)
    n_in = len(smem) + len(args)
    return pl.pallas_call(
        kernel,
        in_specs=[pl.BlockSpec(memory_space=pltpu.SMEM)] * len(smem)
        + [vmem] * len(args)
        + [anywhere] * (len(passed) + len(ahead)),
        out_specs=[vmem] * len(outs) + [anywhere] * len(passed),
        out_shape=list(outs) + [jax.ShapeDtypeStruct(v.shape, v.dtype) for v in passed],
        input_output_aliases={n_in + i: len(outs) + i for i in range(len(passed))},
        scratch_shapes=list(scratch),
        compiler_params=pltpu.CompilerParams(vmem_limit_bytes=48 * 1024 * 1024),
        cost_estimate=pl.CostEstimate(flops=10**9, bytes_accessed=4 * 10**6, transcendentals=0),
        name=name,
    )(*smem, *args, *passed, *ahead)


norm_eps = 1e-05


def norm_rows(values):
    center = values - jnp.mean(values, axis=1, keepdims=True)
    scale = lax.rsqrt(jnp.mean(center * center, axis=1, keepdims=True) + norm_eps)
    return center * scale, scale


def norm_back(grad, xhat, scale, gain):
    dx = grad * gain
    return scale * (
        dx - jnp.mean(dx, axis=1, keepdims=True) - xhat * jnp.mean(dx * xhat, axis=1, keepdims=True)
    )


ROWS = 128


def enter_kernel(dealt_ref, gain_ref, bias_ref, *rest):
    x_ref, n_ref = rest[-2:]
    width = x_ref.shape[1]
    for i in range(x_ref.shape[0] // ROWS):
        rows = slice(i * ROWS, (i + 1) * ROWS)
        x = dealt_ref[:, :, rows].reshape(width, ROWS).astype(jnp.float32).T
        x_ref[rows, :] = x.astype(jnp.bfloat16)
        n_ref[rows, :] = (norm_rows(x)[0] * gain_ref[...] + bias_ref[...]).astype(jnp.bfloat16)


def turn_kernel(z_ref, d0, d1, d2, d3, *rest):
    out_ref, turned = rest[2], rest[-1]
    for d, part in enumerate((d0, d1, d2, d3)):
        turned[z_ref[0] ^ d] = part[...]
    for i in range(out_ref.shape[0] // ROWS):
        rows = slice(i * ROWS, (i + 1) * ROWS)
        out_ref[rows, :] = turned[:, :, rows].reshape(out_ref.shape[1], ROWS).astype(jnp.float32).T.astype(jnp.bfloat16)


def pick_kernel(which_ref, own_ref, got_ref, *rest):
    out_ref = rest[0]
    rows = pl.ds(pl.multiple_of(which_ref[1] * out_ref.shape[0], 16), out_ref.shape[0])

    @pl.when(which_ref[0] == 1)
    def _():
        out_ref[...] = own_ref[rows, :]

    @pl.when(which_ref[0] == 0)
    def _():
        out_ref[...] = got_ref[rows, :]


def middle_kernel(x_ref, near_ref, got_ref, gain_ref, bias_ref, *rest):
    resid_ref, n_ref = rest[-2:]
    for i in range(x_ref.shape[0] // ROWS):
        rows = slice(i * ROWS, (i + 1) * ROWS)
        resid = x_ref[rows, :].astype(jnp.float32) + near_ref[rows, :] + got_ref[rows, :].astype(jnp.float32)
        resid_ref[rows, :] = resid
        xhat = norm_rows(resid.astype(jnp.bfloat16).astype(jnp.float32))[0]
        n_ref[rows, :] = (xhat * gain_ref[...] + bias_ref[...]).astype(jnp.bfloat16)


def middle_back_kernel(own_ref, got_ref, resid_ref, dy_ref, gain_ref, *rest):
    d_ref, low_ref, vec_ref = rest[-3:]
    total = None
    for i in range(own_ref.shape[0] // ROWS):
        rows = slice(i * ROWS, (i + 1) * ROWS)
        grad = own_ref[rows, :] + got_ref[rows, :].astype(jnp.float32)
        xhat, scale = norm_rows(resid_ref[rows, :].astype(jnp.bfloat16).astype(jnp.float32))
        sums = [jnp.sum(grad * xhat, axis=0, keepdims=True), jnp.sum(grad, axis=0, keepdims=True)]
        total = sums if total is None else [a + b for a, b in zip(total, sums)]
        d = dy_ref[rows, :].astype(jnp.float32) + norm_back(grad, xhat, scale, gain_ref[...])
        d_ref[rows, :] = d
        low_ref[rows, :] = d.astype(jnp.bfloat16)
    vec_ref[0:1, :] = total[0]
    vec_ref[1:2, :] = total[1]


def block_kernel(resid_ref, own_ref, got_ref, *rest):
    out_ref = rest[-1]
    parts, quarter, _ = out_ref.shape
    for i in range(own_ref.shape[0] // ROWS):
        rows = slice(i * ROWS, (i + 1) * ROWS)
        out = resid_ref[rows, :] + own_ref[rows, :] + got_ref[rows, :].astype(jnp.float32)
        out_ref[:, :, rows] = out.T.astype(jnp.bfloat16).reshape(parts, quarter, ROWS)


def leave_kernel(near_ref, got_ref, x_ref, d_ref, gain_ref, vec_ref, *rest):
    out_ref = rest[-1]
    parts, quarter = out_ref.shape[0], near_ref.shape[1] // out_ref.shape[0]
    total = None
    for i in range(near_ref.shape[0] // ROWS):
        rows = slice(i * ROWS, (i + 1) * ROWS)
        grad = near_ref[rows, :] + got_ref[rows, :].astype(jnp.float32)
        xhat, scale = norm_rows(x_ref[rows, :].astype(jnp.float32))
        sums = [jnp.sum(grad * xhat, axis=0, keepdims=True), jnp.sum(grad, axis=0, keepdims=True)]
        total = sums if total is None else [a + b for a, b in zip(total, sums)]
        out = d_ref[rows, :] + norm_back(grad, xhat, scale, gain_ref[...])
        out_ref[:, :quarter, rows] = out.T.astype(jnp.bfloat16).reshape(parts, quarter, ROWS)
    vec = jnp.concatenate(total + [vec_ref[0:1, :], vec_ref[1:2, :]], axis=0)
    high = vec.astype(jnp.bfloat16).astype(jnp.float32)
    both = jnp.concatenate([high, vec - high], axis=0)
    tail = out_ref.shape[1] - quarter
    for k in range(parts):
        mine = both[:, k * quarter:(k + 1) * quarter]
        mine = jnp.concatenate([mine, jnp.zeros((8, out_ref.shape[2] - quarter), jnp.float32)], axis=1)
        mine = jnp.concatenate([mine, jnp.zeros((tail - 8, out_ref.shape[2]), jnp.float32)], axis=0)
        out_ref[k, quarter:, :] = mine.astype(jnp.bfloat16)


def sum_kernel(a, b, c, d, *rest, out_at):
    total = a[...].astype(jnp.float32) + b[...].astype(jnp.float32) + c[...].astype(jnp.float32) + d[...].astype(jnp.float32)
    rest[out_at][...] = total.astype(jnp.bfloat16)


def sum_slices_kernel(a, *rest):
    rest[-2][...] = jnp.sum(a[...].astype(jnp.float32), axis=0).astype(jnp.bfloat16)


def sum_four(pieces, name, ahead=(), passed=()):
    out = [jax.ShapeDtypeStruct(pieces[0].shape, jnp.bfloat16)]
    at = len(passed) + len(ahead)
    return call(partial(sum_kernel, out_at=at), name, pieces, out, ahead=ahead, passed=passed)


def own_group(i):
    return (i & 3) // 2 == (i >> 2) & 1


def far_group(i):
    return not own_group(i)


def shards(
    activations, segment_ids, block_lists, feature_proj, input_norm_gain, input_norm_bias, qkv_weight,
    out_weight, middle_norm_gain, middle_norm_bias, up_weight, down_weight, out_grad,
):
    rows_n, heads_n = lax.axis_size("row"), lax.axis_size("head")
    total = rows_n * heads_n
    r, z = lax.axis_index("row"), lax.axis_index("head")
    c, p = r % 2, (r // 2) % 4
    groups = rows_n // 8
    pairs = [[2 * i, 2 * i + 1] for i in range(rows_n // 2)]
    planes = [[8 * g + i for i in range(8)] for g in range(groups)]
    quads = [[8 * g + 2 * i + k for i in range(4)] for g in range(groups) for k in range(2)]
    width = input_norm_gain.shape[0]
    quarter = width // heads_n
    seq_count, length = segment_ids.shape
    half = length // 2
    lists_here = block_lists.shape[1]
    bf16, f32 = jnp.bfloat16, jnp.float32
    local = (z // 2) == c
    par = z % 2

    def move(v, mask, only=None):
        moves = [(i, i ^ mask) for i in range(total) if only is None or only(i)]
        return lax.ppermute(v, ("row", "head"), moves)

    def later(i, dep):
        one = lax.slice(dep, (0,) * dep.ndim, (1,) * dep.ndim).reshape(())
        return i + (one != one).astype(jnp.int32)

    def deal_z(v):
        return lax.all_to_all(v, "head", 0, 0, tiled=True)

    def tied(v, dep):
        one = lax.slice(dep, (0,) * dep.ndim, (1,) * dep.ndim).reshape(())
        return v + (one != one).astype(v.dtype)

    def deal(v, side):
        v = v.T

        def token_half(k):
            return jnp.stack([lax.dynamic_slice_in_dim(v, s * length + k * half, half, 1) for s in range(seq_count)])

        keep, got = token_half(side), move(token_half(1 - side), 4)
        return jnp.concatenate([jnp.where(side == 0, keep, got), jnp.where(side == 0, got, keep)], 0)

    def collect(v):
        v = v.reshape(2, seq_count, quarter, half)
        keep = lax.dynamic_index_in_dim(v, c, 0, keepdims=False)
        got = move(lax.dynamic_index_in_dim(v, 1 - c, 0, keepdims=False), 4)
        low, high = jnp.where(c == 0, keep, got), jnp.where(c == 0, got, keep)
        return jnp.concatenate([w[s] for s in range(seq_count) for w in (low, high)], 1).T

    def fetch_z(mine):
        return [mine] + [move(mine, d, own_group) for d in (1, 2, 3)]

    def choose(got, here):
        return jnp.stack([jnp.where(here, got[0], got[2]), jnp.where(here, got[1], got[3])])

    def fetch_plane(both):
        return [both] + [move(both, 8 * d) for d in (1, 2, 3)]

    def give_z(same, other, ahead):
        parts = (same, move(other, 1, own_group), move(same, 2, far_group), move(other, 3, far_group))
        (fin,) = sum_four(parts, "sum_z", ahead=(ahead,))
        if groups > 1:
            fin = lax.psum(fin.astype(f32), "row", axis_index_groups=[[8 * g + i for g in range(groups)] for i in range(8)])
            fin = fin.astype(bf16)
        return call(
            pick_kernel, "pick", (fin, move(fin, 4)), (jax.ShapeDtypeStruct((fin.shape[0] // 2, width), bf16),),
            smem=(jnp.stack([local.astype(jnp.int32), c]),),
        )[0]

    def gather_plane(v):
        return lax.all_gather(v, "row", axis=0, axis_index_groups=planes)

    cut = lambda w, n, at: lax.dynamic_slice_in_dim(w, at * n, n, 0)

    aux = jnp.concatenate([block_lists.reshape(seq_count, -1), segment_ids], 1).astype(bf16)
    aux_got = move(aux, 4)
    aux = jnp.where(c == 0, jnp.concatenate([aux, aux_got], 0), jnp.concatenate([aux_got, aux], 0))
    n_list = aux.shape[1] - length
    seg = lax.dynamic_index_in_dim(aux[:, n_list:], z, 0, keepdims=False).astype(jnp.int32)

    four = deal(activations, c)
    gain1, bias1, gain2, bias2 = (
        v.reshape(1, width) for v in (input_norm_gain, input_norm_bias, middle_norm_gain, middle_norm_bias)
    )
    shape_of = jax.ShapeDtypeStruct
    half_low, half_wide = shape_of((half, width), bf16), shape_of((half, width), f32)
    dy_four = deal(out_grad, c)
    x_half, n1_half = call(enter_kernel, "enter", (deal_z(four), gain1, bias1), (half_low, half_low), ahead=(dy_four,))

    n_qkv, n_out = qkv_weight.shape[1] // 4, out_weight.shape[0] // 4
    extra = 16
    rider = aux[:, :n_list].reshape(-1)
    rider = jnp.pad(rider, (0, extra * width - rider.shape[0])).reshape(extra, width)
    p_late = later(p, four)
    mine = [cut(qkv_weight.T, n_qkv, p_late), cut(out_weight, n_out, p_late), rider]
    both = choose(fetch_z(jnp.concatenate(mine, 0)), local)
    lists = both[:, n_qkv + n_out:].reshape(2, -1)[:, :4 * n_list].reshape(2, 4, n_list).astype(jnp.int32)
    lists = lax.dynamic_index_in_dim(lists, z, 1, keepdims=False).reshape((2, lists_here) + block_lists.shape[2:])
    pieces = fetch_plane(both[:, :n_qkv + n_out])
    at = jnp.full((1,), p, jnp.int32)

    n_up, n_hid = width // 8, down_weight.shape[0] // 8
    q8 = later(r % 8, x_half)
    mine = jnp.concatenate([cut(up_weight, n_up, q8), cut(down_weight, n_hid, q8)], 0)
    all_z = lax.all_gather(mine, "head", axis=0).reshape((1, 2, 2) + mine.shape)
    send = [jnp.broadcast_to(all_z[:, :, i], (4, 2) + mine.shape).reshape((8,) + mine.shape) for i in range(2)]
    packs = [lax.all_to_all(v, "row", 0, 0, axis_index_groups=planes, tiled=True) for v in send]

    shift = c * half
    seg = lax.dynamic_slice_in_dim(jnp.concatenate([seg, seg]), shift, length, 0)
    hits = []
    for own in lists:
        own = lax.dynamic_slice_in_dim(jnp.concatenate([own, own], 1), shift // BLK, length // BLK, 1)
        hit = hit_lanes(own, length)
        hits.append(lax.dynamic_slice_in_dim(jnp.concatenate([hit, hit], 2), shift, length, 2))

    n1 = (n1_half, move(n1_half, 4))
    att = [attn_fwd(at, *n1, pieces, 0, seg, hits[0], feature_proj)]
    z_late = z + att[0][-1][0]
    dy_parts = [lax.dynamic_index_in_dim(dy_four, z_late ^ d, 0, keepdims=False) for d in range(heads_n)]
    dy_got = [move(v, d) if d else v for d, v in enumerate(dy_parts)]
    att.append(attn_fwd(at, *n1, pieces, 1, seg, hits[1], feature_proj, att[0][7], (send[0], *dy_parts)))
    heads_out = [v[0] for v in att]
    qkv = [v[4] for v in att]
    wq = [v[5] for v in att]
    outw = [v[6].reshape(-1, width) for v in att]
    dy_half, near, away = call(
        turn_kernel, "turn", dy_got, (half_low,), smem=(z.reshape(1),), passed=att[1][7:9],
        scratch=(pltpu.VMEM((heads_n, quarter, half), bf16),),
    )
    resid, n2_half = call(
        middle_kernel, "middle", (x_half, near, move(away, 4), gain2, bias2), (half_wide, half_low), ahead=(packs[0],)
    )
    n2 = (n2_half, move(n2_half, 4))
    dy = (dy_half, move(dy_half, 4))
    acted, d_pre, dn = mlp_first(n2, dy, packs[0])
    mo, grads = mlp_second(n2, dy, acted, d_pre, packs[0])
    acted, d_pre, dn_own, dn_oth = mlp_first(n2, dy, packs[1], dn, (mo,))
    mo_own, mo_oth, grads = mlp_second(n2, dy, acted, d_pre, packs[1], mo, grads)
    d_resid, d_half, vec2 = call(
        middle_back_kernel, "middle_back", (dn_own, move(dn_oth, 4), resid, dy_half, gain2),
        (half_wide, half_low, shape_of((2, width), f32)),
    )
    (block_send,) = call(
        block_kernel, "block", (resid, mo_own, move(mo_oth, 4)), (shape_of((heads_n, quarter, half), bf16),)
    )
    block_got = deal_z(block_send)
    block_out = collect(block_got)
    d_branch = (d_half, move(d_half, 4))
    grads = lax.psum_scatter(
        grads.reshape(-1, width), "row", scatter_dimension=0, axis_index_groups=quads, tiled=True
    ).reshape(2, 2, -1, width)
    back = [
        attn_bwd(at, qkv[0], seg, hits[0], feature_proj, *att[0][1:4], heads_out[0], *d_branch, outw[0], *n1, wq[0], None, (mo_oth,))
    ]
    c_late = later(c + back[0][2][0], block_got)
    keep = lax.dynamic_index_in_dim(grads, c_late, 0, keepdims=False)
    got = move(lax.dynamic_index_in_dim(grads, 1 - c_late, 0, keepdims=False), 4)
    four = jnp.concatenate([jnp.where(c == 0, keep, got), jnp.where(c == 0, got, keep)], 0)
    four_flat = four.reshape(-1, width)
    mlp_slice = mlp_grads = lax.psum_scatter(four_flat, "head", scatter_dimension=0, tiled=True)
    if groups > 1:
        mlp_grads = lax.psum(mlp_grads, "row", axis_index_groups=[[8 * g + i for g in range(groups)] for i in range(8)])

    back.append(
        attn_bwd(
            at, qkv[1], seg, hits[1], feature_proj, *att[1][1:4], heads_out[1], *d_branch, outw[1], *n1, wq[1], back[0][1],
            (block_got, four_flat),
        )
    )
    def across(pieces):
        return [pieces[0]] + [move(pieces[d], 8 * d) for d in (1, 2, 3)]

    first = lax.all_to_all(back[0][0], "row", 0, 0, axis_index_groups=quads, tiled=True)
    first, *passed = call(
        sum_slices_kernel, "sum_first", (first,), (shape_of(first.shape[1:], bf16),), passed=(mlp_grads,), ahead=(back[1][0],)
    )
    (mlp_grads,) = passed
    pieces, (near, away) = back[1][:4], back[1][4:6]
    mlp_grads = gather_plane(mlp_grads)
    up_grad = mlp_grads[:, :n_up].reshape(width, -1).astype(f32)
    down_grad = mlp_grads[:, n_up:].reshape(-1, width).astype(f32)
    (send,) = call(
        leave_kernel, "leave", (near, move(away, 4), x_half, d_resid, gain1, vec2),
        (shape_of((heads_n, quarter + 16, half), bf16),), ahead=(first,),
    )
    (second,) = sum_four(across(pieces), "sum_second", ahead=(send,))
    got = deal_z(send)
    qkv_slice = give_z(first, second, got)
    input_grad = collect(got[:, :quarter]).astype(f32)
    vec = jnp.sum(got[:, quarter:quarter + 8, :quarter].astype(f32), 0)
    qkv_slice = tied(qkv_slice, mlp_grads)
    got = gather_plane(qkv_slice)
    vec = tied(vec[:4] + vec[4:], qkv_slice)
    for mask in (4, 8, 16):
        vec = vec + move(vec, mask)
    if groups > 1:
        vec = lax.psum(vec, "row", axis_index_groups=[[8 * g + i for g in range(groups)] for i in range(8)])
    both = got.reshape(4, n_qkv + n_out, width)
    qkv_grad = both[:, :n_qkv].reshape(-1, width).astype(f32).T
    out_w_grad = both[:, n_qkv:].reshape(-1, width).astype(f32)
    return (
        block_out, input_grad, vec[0], vec[1], qkv_grad, out_w_grad, vec[2], vec[3], up_grad, down_grad,
    )


def solution(mesh):
    return jax.shard_map(
        shards,
        mesh=mesh,
        in_specs=(
            P("row", "head"), P("row", None), P("row", "head", None, None), P(), P(), P(), P(None, "head"),
            P("head", None), P(), P(), P(None, "head"), P("head", None), P("row", "head"),
        ),
        out_specs=(
            P("row", "head"), P("row", "head"), P("head"), P("head"), P(None, "head"), P("head", None),
            P("head"), P("head"), P(None, "head"), P("head", None),
        ),
        check_vma=False,
    )
```

time: 470 us -> 426 us (0.906)
  Pallas kernels: 144 us -> 189 us
  matrix products: 30.4 us -> 0 us
  other arithmetic: 48.1 us -> 20.5 us
  waiting for transfers between devices: 92.6 us -> 67.1 us
  local copies, waits for them, and re-layouts: 64.4 us -> 41.5 us
  starting transfers between devices: 62 us -> 76.5 us
    pallas_call x4 -> x16, Pallas kernels: 95.4 us -> 135 us  [the longest x2 76.8 us: attn_bwd(): pl.pallas_call(partial(bwd_kernel, tq=tq, tk=tk, dh=dh, first=first), in_...]
    dot_general x14 -> x0, matrix products: 30.4 us -> none  [mm(): return lax.dot_general(a, b, (dims, ((), ())), preferred_element_type=f32)]
    ppermute x27 -> x33, starting transfers between devices: 32.2 us -> 50.2 us  [move(): return lax.ppermute(v, ('row', 'head'), moves)]
    all_to_all x3, waiting for transfers between devices: 26.8 us -> 11.3 us  [deal_z(): return lax.all_to_all(v, 'head', 0, 0, tiled=True)]
    reshape x12 -> x5, local copies, waits for them, and re-layouts: 14.5 us -> 0.06 us  [the longest x1 0.05 us: shards(): jnp.pad(rider, (0, extra * width - rider.shape[0])).reshape(extra, width)]
    reduce_sum x9 -> x1, other arithmetic: 10.6 us -> 0.01 us  [shards(): vec = jnp.sum(got[:, quarter:quarter + 8, :quarter].astype(f32), 0)]
    concatenate x10 -> x2, other arithmetic: 8.8 us -> 1.5 us  [the longest x1 0.75 us: shards(): jnp.concatenate([cut(up_weight, n_up, q8), cut(down_weight, n_hid, q8)], 0)]
    convert_element_type x8 -> x1, local copies, waits for them, and re-layouts: 7.38 us -> 0.09 us  [shards(): both[:, n_qkv + n_out:].reshape(2, -1)[:, :4 * n_list].reshape(2, 4, n_list)]
  transfers between devices with their start and end apart: 38 -> 44, of which waited for: 16 -> 17; matrix products, arithmetic and copies ran while one was open for 25% -> 7% of each run, Pallas kernels for 24% -> 40%
where the time goes in v3:
time: 426 us; the launch traced here: 418 us
  Pallas kernels  189 us (44%)
  starting transfers between devices  76.5 us (18%)
  waiting for transfers between devices  67.1 us (16%)
  local copies, waits for them, and re-layouts  41.5 us (10%)
  between operations  23.1 us (5%)
  other arithmetic  20.5 us (5%)
    pallas_call x2, Pallas kernels, attn_bwd(): pl.pallas_call(partial(bwd_kernel, tq=tq, tk=tk, dh=dh, first=first), in_...  76.8 us
    pallas_call x2, Pallas kernels, attn_fwd(): pl.pallas_call(partial(fwd_kernel, tq=tq, tk=tk, dh=dh, part=part), in_sp...  53.8 us
    ppermute x33, starting transfers between devices, move(): return lax.ppermute(v, ('row', 'head'), moves)  50.2 us
    ppermute x33, waiting for transfers between devices, move(): return lax.ppermute(v, ('row', 'head'), moves)  38.9 us
    pallas_call x2, Pallas kernels, mlp_first(): pl.pallas_call(partial(mlp_kernel, tile=tile, rows=rows, first=first), in...  25.5 us
    unnamed x114, local copies, waits for them, and re-layouts  22.5 us
    pallas_call x2, Pallas kernels, mlp_second(): pl.pallas_call(partial(mlp_grad_kernel, first=first), grid=(1,), in_specs...  19.6 us
    pallas_call x10, Pallas kernels, call(): pl.pallas_call(kernel, in_specs=[pl.BlockSpec(memory_space=pltpu.SMEM)] *...  13.2 us
  transfers between devices with their start and end apart: 44, of which 17 were waited for; matrix products, arithmetic and copies ran while one was open for 7% of the time, Pallas kernels for 40%

profile of v3, /device:TPU:0, one launch (start us, length us, event | category | flops | bytes accessed | tf_op | source)
XLA Modules:
  0.0 417.8 jit_solution(5785097296162988152)
XLA Ops:
  17.7 4.8 %collective-permute-start.5 = (bf16[208,768]{1,0:T(8,128)(2,1)}, bf16[208,768]{1,0:T(8,128)(2,1)}, u32[]{:S(2)}, u32[]{:S(2)}) collective-permute-start(bf16[208,768]{1,0:T(8,128)(2,1)} %pad_maximum_fusion.8), channel_id=1, source_target_pairs={{0,1},{1,0},{6,7},{7,6},{8,9},{9,8},{14,15},{15,14},{16,17},{17,16... | collective-permute-start | bytes 958472 | tf_op jit(solution)/shard_map/ppermute | solution.py:589
  22.5 4.1 collective-permute-start.6
  26.7 2.0 collective-permute-start.4
  29.6 3.6 all-to-all-start
  34.5 2.0 collective-permute-done.4
  37.7 1.6 collective-permute-start.7
  39.2 1.5 collective-permute-start.8
  41.9 11.3 %all-to-all-done.dealt_ref = bf16[4,192,512]{2,1,0:T(8,128)(2,1)S(1)} async-done(((bf16[4,192,512]{2,1,0:T(8,128)(2,1)}), bf16[4,192,512]{2,1,0:T(8,128)(2,1)S(1)}, u32[]{:S(2)}, u32[]{:S(2)}) %all-to-all-start) | async-done | bytes 786464 | tf_op jit(solution)/shard_map/all_to_all | solution.py:596
  53.2 1.7 enter.1
  54.9 6.3 %collective-permute-start.3 = (bf16[512,768]{1,0:T(8,128)(2,1)}, bf16[512,768]{1,0:T(8,128)(2,1)S(1)}, u32[]{:S(2)}, u32[]{:S(2)}) collective-permute-start(bf16[512,768]{1,0:T(8,128)(2,1)} %get-tuple-element.62.own_ref.n_own), channel_id=1, source_target_pairs={{0,4},{1,5},{2,6},{3,7},{4,0},{5,1},{6,2},{7,3},{8,12},{9,13},{10,... | collective-permute-start | bytes 2359304 | tf_op jit(solution)/shard_map/ppermute | solution.py:589
  65.5 26.4 %attn_fwd.2 = (bf16[1024,192]{1,0:T(8,128)(2,1)S(1)}, bf16[3,1024,256]{2,1,0:T(8,128)(2,1)}, bf16[3,1024,256]{2,1,0:T(8,128)(2,1)}, f32[3,1024,1]{2,1,0:T(8,128)...) custom-call(s32[1]{0:T(128)} %bitcast.17.at_ref, ...), custom_call_target="tpu_custom_call" | custom-call | flops 27000000512 | bytes 10000000 | tf_op jit(solution)/shard_map/attn_fwd/pallas_call | solution.py:134
  95.5 9.8 %collective-permute-start.10 = (bf16[192,512]{1,0:T(8,128)(2,1)S(1)}, bf16[192,512]{1,0:T(8,128)(2,1)S(1)}, u32[]{:S(2)}, u32[]{:S(2)}) collective-permute-start(bf16[192,512]{1,0:T(8,128)(2,1)S(1)} %get-tuple-element.126.rest_7_), channel_id=1, source_target_pairs={{0,1},{1,0},{2,3},{3,2},{4,5},{5,4},{6,7},{7,6},{8,9},{9,8},{10,11... | collective-permute-start | bytes 589832 | tf_op jit(solution)/shard_map/ppermute | solution.py:589
  107.7 2.1 slice_bitcast_fusion
  109.8 1.6 broadcast_in_dim.19
  111.4 4.6 %all-to-all-start.1 = ((bf16[8,192,768]{2,1,0:T(8,128)(2,1)}), bf16[8,192,768]{2,1,0:T(8,128)(2,1)}, u32[]{:S(2)}, u32[]{:S(2)}) async-start(bf16[8,192,768]{2,1,0:T(8,128)(2,1)} %bitcast.170), calls=%async_computation.1 | async-start | bytes 4718592 | tf_op jit(solution)/shard_map/all_to_all | solution.py:675
  116.0 27.4 %attn_fwd.3 = (bf16[1024,192]{1,0:T(8,128)(2,1)S(1)}, bf16[3,1024,256]{2,1,0:T(8,128)(2,1)}, bf16[3,1024,256]{2,1,0:T(8,128)(2,1)}, f32[3,1024,1]{2,1,0:T(8,128)...) custom-call(s32[1]{0:T(128)} %bitcast.17.at_ref, ...), custom_call_target="tpu_custom_call" | custom-call | flops 27000000512 | bytes 10000000 | tf_op jit(solution)/shard_map/attn_fwd/pallas_call | solution.py:134
  144.3 1.5 copy-done.10
  147.9 1.8 collective-permute-done.13.got_ref
  151.1 1.6 middle.1
  154.2 1.6 broadcast_in_dim.21
  155.8 4.4 %all-to-all-start.2 = ((bf16[8,192,768]{2,1,0:T(8,128)(2,1)}), bf16[8,192,768]{2,1,0:T(8,128)(2,1)}, u32[]{:S(2)}, u32[]{:S(2)}) async-start(bf16[8,192,768]{2,1,0:T(8,128)(2,1)} %bitcast.172), calls=%async_computation.2 | async-start | bytes 4718592 | tf_op jit(solution)/shard_map/all_to_all | solution.py:675
  160.7 12.5 %mlp_first.2 = (bf16[1024,768]{1,0:T(8,128)(2,1)S(1)}, bf16[1024,768]{1,0:T(8,128)(2,1)}, f32[1024,768]{1,0:T(8,128)}) custom-call(bf16[512,768]{1,0:T(8,128)(2,1)} %get-tuple-element.70.n_own, bf16[512,768]{1,0:T(8,128)(2,1)S(1)} %collective-permute-done.14.n_oth, bf16[512,768]{1,0:T(8,128)(2,1)S(1)} %get-tuple-element.71.dy_own.dy_ref, ...), custom_call_target="tpu_custom_call" | custom-call | flops 12000000000 | bytes 20000000 | tf_op jit(solution)/shard_map/mlp_first/pallas_call | solution.py:365
  173.2 9.2 %mlp_second.2 = (f32[1024,768]{1,0:T(8,128)}, bf16[4,2,2,192,768]{4,3,2,1,0:T(8,128)(2,1)}) custom-call(bf16[512,768]{1,0:T(8,128)(2,1)} %get-tuple-element.70.n_own, bf16[512,768]{1,0:T(8,128)(2,1)S(1)} %collective-permute-done.14.n_oth, bf16[512,768]{1,0:T(8,128)(2,1)S(1)} %get-tuple-element.71.dy_own.dy_ref, ...), custom_call_target="tpu_custom_call" | custom-call | flops 8000000000 | bytes 20000000 | tf_op jit(solution)/shard_map/mlp_second/pallas_call | solution.py:401
  182.4 7.3 %all-to-all-done.2.w_ref = bf16[8,192,768]{2,1,0:T(8,128)(2,1)} async-done(((bf16[8,192,768]{2,1,0:T(8,128)(2,1)}), bf16[8,192,768]{2,1,0:T(8,128)(2,1)}, u32[]{:S(2)}, u32[]{:S(2)}) %all-to-all-start.2) | async-done | bytes 2359328 | tf_op jit(solution)/shard_map/all_to_all | solution.py:675
  189.7 13.0 %mlp_first.3 = (bf16[1024,768]{1,0:T(8,128)(2,1)S(1)}, bf16[1024,768]{1,0:T(8,128)(2,1)}, f32[512,768]{1,0:T(8,128)}, bf16[512,768]{1,0:T(8,128)(2,1)S(1)}) custom-call(bf16[512,768]{1,0:T(8,128)(2,1)} %get-tuple-element.70.n_own, bf16[512,768]{1,0:T(8,128)(2,1)S(1)} %collective-permute-done.14.n_oth, bf16[512,768]{1,0:T(8,128)(2,1)S(1)} %get-tuple-element.71.dy_own.dy_ref, ...), custom_call_target="tpu_custom_call" | custom-call | flops 12000000000 | bytes 20000000 | tf_op jit(solution)/shard_map/mlp_first/pallas_call | solution.py:365
  203.8 10.5 %mlp_second.3 = (f32[512,768]{1,0:T(8,128)S(1)}, bf16[512,768]{1,0:T(8,128)(2,1)}, bf16[4,2,2,192,768]{4,3,2,1,0:T(8,128)(2,1)}) custom-call(bf16[512,768]{1,0:T(8,128)(2,1)} %get-tuple-element.70.n_own, bf16[512,768]{1,0:T(8,128)(2,1)S(1)} %collective-permute-done.14.n_oth, ...), custom_call_target="tpu_custom_call", output_to_operand_aliasing={{2}: (8, {})} | custom-call | flops 8000000000 | bytes 20000000 | tf_op jit(solution)/shard_map/mlp_second/pallas_call | solution.py:401
  217.1 2.9 collective-permute-done.18.got_ref
  219.9 1.9 copy-done.9
  221.8 3.8 middle_back.1
  229.2 2.3 block.1
  231.5 4.2 %all-to-all-start.3 = ((bf16[4,192,512]{2,1,0:T(8,128)(2,1)}), bf16[4,192,512]{2,1,0:T(8,128)(2,1)S(1)}, u32[]{:S(2)}, u32[]{:S(2)}) async-start(bf16[4,192,512]{2,1,0:T(8,128)(2,1)} %block.1), calls=%async_computation.3 | async-start | bytes 1572864 | tf_op jit(solution)/shard_map/all_to_all | solution.py:596
  236.7 37.7 %attn_bwd.2 = (bf16[4,192,768]{2,1,0:T(8,128)(2,1)}, f32[1024,768]{1,0:T(8,128)}, s32[1]{0:T(128)}) custom-call(s32[1]{0:T(128)} %bitcast.17.at_ref, s32[1,1024]{1,0:T(1,128)} %bitcast.164, bf16[1024,576]{1,0:T(8,128)(2,1)} %get-tuple-element.91.qkv_ref, s32[1024,1]{1,0:T(8,128)} %copy-done.13, s32[1,1024]{1,0:T(1,128)} %bitcast.165, ...), custom_call_target="tpu_custom_call" | custom-call | flops 41999998976 | bytes 20000000 | tf_op jit(solution)/shard_map/attn_bwd/pallas_call | solution.py:276
  278.2 3.5 all-to-all-start.4
  284.5 39.1 %attn_bwd.3 = (bf16[192,768]{1,0:T(8,128)(2,1)}, bf16[192,768]{1,0:T(8,128)(2,1)}, bf16[192,768]{1,0:T(8,128)(2,1)}, bf16[192,768]{1,0:T(8,128)(2,1)}, f32[512,7...) custom-call(s32[1]{0:T(128)} %bitcast.17.at_ref, s32[1,1024]{1,0:T(1,128)} %bitcast.166, ...), custom_call_target="tpu_custom_call" | custom-call | flops 41999998976 | bytes 20000000 | tf_op jit(solution)/shard_map/attn_bwd/pallas_call | solution.py:276
  327.8 2.1 collective-permute-done.21.got_ref
  332.3 2.5 leave.1.rest_0_
  334.7 5.1 %all-to-all-start.5 = ((bf16[4,208,512]{2,1,0:T(8,128)(2,1)}), bf16[4,208,512]{2,1,0:T(8,128)(2,1)S(1)}, u32[]{:S(2)}, u32[]{:S(2)}) async-start(bf16[4,208,512]{2,1,0:T(8,128)(2,1)} %leave.1.rest_0_), calls=%async_computation.7 | async-start | bytes 1703936 | tf_op jit(solution)/shard_map/all_to_all | solution.py:596
  340.1 1.8 collective-permute-start.23
  345.0 5.8 %collective-permute-done.23.b = bf16[192,768]{1,0:T(8,128)(2,1)S(1)} collective-permute-done((bf16[192,768]{1,0:T(8,128)(2,1)}, bf16[192,768]{1,0:T(8,128)(2,1)S(1)}, u32[]{:S(2)}, u32[]{:S(2)}) %collective-permute-start.23) | collective-permute-done | bytes 294944 | tf_op jit(solution)/shard_map/ppermute | solution.py:589
  350.7 6.3 %collective-permute-done.24.c = bf16[192,768]{1,0:T(8,128)(2,1)S(1)} collective-permute-done((bf16[192,768]{1,0:T(8,128)(2,1)}, bf16[192,768]{1,0:T(8,128)(2,1)S(1)}, u32[]{:S(2)}, u32[]{:S(2)}) %collective-permute-start.24) | collective-permute-done | bytes 294944 | tf_op jit(solution)/shard_map/ppermute | solution.py:589
  357.0 6.5 %collective-permute-done.25.d = bf16[192,768]{1,0:T(8,128)(2,1)S(1)} collective-permute-done((bf16[192,768]{1,0:T(8,128)(2,1)S(1)}, bf16[192,768]{1,0:T(8,128)(2,1)S(1)}, u32[]{:S(2)}, u32[]{:S(2)}) %collective-permute-start.25) | collective-permute-done | bytes 294944 | tf_op jit(solution)/shard_map/ppermute | solution.py:589
  363.7 4.0 collective-permute-start.26
  369.1 1.9 collective-permute-start.22
  372.5 5.7 %collective-permute-done.28.d = bf16[192,768]{1,0:T(8,128)(2,1)S(1)} collective-permute-done((bf16[192,768]{1,0:T(8,128)(2,1)S(1)}, bf16[192,768]{1,0:T(8,128)(2,1)S(1)}, u32[]{:S(2)}, u32[]{:S(2)}) %collective-permute-start.28) | collective-permute-done | bytes 294944 | tf_op jit(solution)/shard_map/ppermute | solution.py:589
  390.4 1.7 bitcast_convert_fusion.1
  392.9 1.7 bitcast_convert_fusion
  394.5 1.7 collective-permute-done.32
  396.8 9.5 %all-gather.11.cloned.1.call-done = bf16[768,768]{1,0:T(8,128)(2,1)} async-done(((bf16[96,768]{1,0:T(8,128)(2,1)}), bf16[768,768]{1,0:T(8,128)(2,1)}) %all-gather.11.cloned.1.call-update) | async-done | bytes 1179664 | tf_op jit(solution)/shard_map/all_gather | solution.py:639
  (268 shorter events, 69.1 us)
Async XLA Ops:
  8.7 4.4 %collective-permute-start = (bf16[2,192,512]{2,1,0:T(8,128)(2,1)S(1)}, bf16[2,192,512]{2,1,0:T(8,128)(2,1)}, u32[]{:S(2)}, u32[]{:S(2)}) collective-permute-start(bf16[2,192,512]{2,1,0:T(8,128)(2,1)S(1)} %pad_maximum_fusion.5), channel_id=1, source_target_pairs={{0,4},{1,5},{2,6},{3,7},{4,0},{5,1},{6,2},{7,3},{8,12},{9,13},{10,... | collective-permute-start | bytes 1179656 | tf_op jit(solution)/shard_map/ppermute | solution.py:589
  10.8 22.5 %collective-permute-start.1 = (bf16[2,192,512]{2,1,0:T(8,128)(2,1)}, bf16[2,192,512]{2,1,0:T(8,128)(2,1)}, u32[]{:S(2)}, u32[]{:S(2)}) collective-permute-start(bf16[2,192,512]{2,1,0:T(8,128)(2,1)} %pad_maximum_fusion.7), channel_id=1, source_target_pairs={{0,4},{1,5},{2,6},{3,7},{4,0},{5,1},{6,2},{7,3},{8,12},{9,13},{10,... | collective-permute-start | bytes 1179656 | tf_op jit(solution)/shard_map/ppermute | solution.py:589
  11.2 1.3 collective-permute-start.2
  11.7 41.5 %copy-start.23 = (f32[1,768]{1,0:T(1,128)}, f32[1,768]{1,0:T(1,128)S(1)}, u32[]{:S(2)}) copy-start(f32[1,768]{1,0:T(1,128)S(1)} %reshape.175.gain_ref) | copy-start | bytes 9220
  12.7 103.2 %copy-start.22 = (s32[1024]{0:T(1024)}, s32[1024]{0:T(1024)S(1)}, u32[]{:S(2)}) copy-start(s32[1024]{0:T(1024)S(1)} %fusion.20) | copy-start | bytes 12292
  13.0 103.0 %copy-start.13 = (s32[1024,1]{1,0:T(8,128)}, s32[1024,1]{1,0:T(8,128)S(1)}, u32[]{:S(2)}) copy-start(s32[1024,1]{1,0:T(8,128)S(1)} %copy.43.segc_ref) | copy-start | bytes 12292
  17.7 18.9 %collective-permute-start.5 = (bf16[208,768]{1,0:T(8,128)(2,1)}, bf16[208,768]{1,0:T(8,128)(2,1)}, u32[]{:S(2)}, u32[]{:S(2)}) collective-permute-start(bf16[208,768]{1,0:T(8,128)(2,1)} %pad_maximum_fusion.8), channel_id=1, source_target_pairs={{0,1},{1,0},{6,7},{7,6},{8,9},{9,8},{14,15},{15,14},{16,17},{17,16... | collective-permute-start | bytes 958472 | tf_op jit(solution)/shard_map/ppermute | solution.py:589
  22.5 14.1 %collective-permute-start.6 = (bf16[208,768]{1,0:T(8,128)(2,1)}, bf16[208,768]{1,0:T(8,128)(2,1)}, u32[]{:S(2)}, u32[]{:S(2)}) collective-permute-start(bf16[208,768]{1,0:T(8,128)(2,1)} %pad_maximum_fusion.8), channel_id=1, source_target_pairs={{0,3},{1,2},{6,5},{7,4},{8,11},{9,10},{14,13},{15,12},{16,19},{17,... | collective-permute-start | bytes 958472 | tf_op jit(solution)/shard_map/ppermute | solution.py:589
  26.7 9.8 %collective-permute-start.4 = (bf16[208,768]{1,0:T(8,128)(2,1)}, bf16[208,768]{1,0:T(8,128)(2,1)}, u32[]{:S(2)}, u32[]{:S(2)}) collective-permute-start(bf16[208,768]{1,0:T(8,128)(2,1)} %pad_maximum_fusion.8), channel_id=1, source_target_pairs={{0,2},{1,3},{6,4},{7,5},{8,10},{9,11},{14,12},{15,13},{16,18},{17,... | collective-permute-start | bytes 958472 | tf_op jit(solution)/shard_map/ppermute | solution.py:589
  29.6 23.6 %all-to-all-start = ((bf16[4,192,512]{2,1,0:T(8,128)(2,1)}), bf16[4,192,512]{2,1,0:T(8,128)(2,1)S(1)}, u32[]{:S(2)}, u32[]{:S(2)}) async-start(bf16[4,192,512]{2,1,0:T(8,128)(2,1)} %pad_maximum_fusion.2), calls=%async_computation | async-start | bytes 1572864 | tf_op jit(solution)/shard_map/all_to_all | solution.py:596
  33.2 74.4 %all-gather.7.cloned.1.call-start = ((), (), s32[]{:S(2)}) async-start(), calls=%async_computation.10 | async-start | bytes 1474560 | tf_op jit(solution)/shard_map/all_gather | solution.py:673
  37.7 27.7 %collective-permute-start.7 = (bf16[2,192,768]{2,1,0:T(8,128)(2,1)S(1)}, bf16[2,192,768]{2,1,0:T(8,128)(2,1)}, u32[]{:S(2)}, u32[]{:S(2)}) collective-permute-start(bf16[2,192,768]{2,1,0:T(8,128)(2,1)S(1)} %pad_maximum_fusion.3.rest_0_), channel_id=1, source_target_pairs={{0,8},{1,9},{2,10},{3,11},{4,12},{5,13},{6,14},{7,15},{8,0},{9,1},... | collective-permute-start | bytes 1769480 | tf_op jit(solution)/shard_map/ppermute | solution.py:589
  39.2 26.2 %collective-permute-start.8 = (bf16[2,192,768]{2,1,0:T(8,128)(2,1)S(1)}, bf16[2,192,768]{2,1,0:T(8,128)(2,1)}, u32[]{:S(2)}, u32[]{:S(2)}) collective-permute-start(bf16[2,192,768]{2,1,0:T(8,128)(2,1)S(1)} %pad_maximum_fusion.3.rest_0_), channel_id=1, source_target_pairs={{0,16},{1,17},{2,18},{3,19},{4,20},{5,21},{6,22},{7,23},{8,24},{9,... | collective-permute-start | bytes 1769480 | tf_op jit(solution)/shard_map/ppermute | solution.py:589
  40.7 24.7 %collective-permute-start.9 = (bf16[2,192,768]{2,1,0:T(8,128)(2,1)S(1)}, bf16[2,192,768]{2,1,0:T(8,128)(2,1)}, u32[]{:S(2)}, u32[]{:S(2)}) collective-permute-start(bf16[2,192,768]{2,1,0:T(8,128)(2,1)S(1)} %pad_maximum_fusion.3.rest_0_), channel_id=1, source_target_pairs={{0,24},{1,25},{2,26},{3,27},{4,28},{5,29},{6,30},{7,31},{8,16},{9,... | collective-permute-start | bytes 1769480 | tf_op jit(solution)/shard_map/ppermute | solution.py:589
  54.9 10.5 %collective-permute-start.3 = (bf16[512,768]{1,0:T(8,128)(2,1)}, bf16[512,768]{1,0:T(8,128)(2,1)S(1)}, u32[]{:S(2)}, u32[]{:S(2)}) collective-permute-start(bf16[512,768]{1,0:T(8,128)(2,1)} %get-tuple-element.62.own_ref.n_own), channel_id=1, source_target_pairs={{0,4},{1,5},{2,6},{3,7},{4,0},{5,1},{6,2},{7,3},{8,12},{9,13},{10,... | collective-permute-start | bytes 2359304 | tf_op jit(solution)/shard_map/ppermute | solution.py:589
  61.7 54.3 %copy-start.19 = (f32[3,16,1024]{2,1,0:T(8,128)}, f32[3,16,1024]{2,1,0:T(8,128)S(1)}, u32[]{:S(2)}) copy-start(f32[3,16,1024]{2,1,0:T(8,128)S(1)} %fusion.9.hit_ref) | copy-start | bytes 589828
  95.5 48.8 %collective-permute-start.10 = (bf16[192,512]{1,0:T(8,128)(2,1)S(1)}, bf16[192,512]{1,0:T(8,128)(2,1)S(1)}, u32[]{:S(2)}, u32[]{:S(2)}) collective-permute-start(bf16[192,512]{1,0:T(8,128)(2,1)S(1)} %get-tuple-element.126.rest_7_), channel_id=1, source_target_pairs={{0,1},{1,0},{2,3},{3,2},{4,5},{5,4},{6,7},{7,6},{8,9},{9,8},{10,11... | collective-permute-start | bytes 589832 | tf_op jit(solution)/shard_map/ppermute | solution.py:589
  105.2 39.0 %collective-permute-start.11 = (bf16[192,512]{1,0:T(8,128)(2,1)S(1)}, bf16[192,512]{1,0:T(8,128)(2,1)S(1)}, u32[]{:S(2)}, u32[]{:S(2)}) collective-permute-start(bf16[192,512]{1,0:T(8,128)(2,1)S(1)} %get-tuple-element.127.rest_8_), channel_id=1, source_target_pairs={{0,2},{1,3},{2,0},{3,1},{4,6},{5,7},{6,4},{7,5},{8,10},{9,11},{10,... | collective-permute-start | bytes 589832 | tf_op jit(solution)/shard_map/ppermute | solution.py:589
  106.7 37.5 %collective-permute-start.12 = (bf16[192,512]{1,0:T(8,128)(2,1)S(1)}, bf16[192,512]{1,0:T(8,128)(2,1)S(1)}, u32[]{:S(2)}, u32[]{:S(2)}) collective-permute-start(bf16[192,512]{1,0:T(8,128)(2,1)S(1)} %get-tuple-element.124.rest_9_), channel_id=1, source_target_pairs={{0,3},{1,2},{2,1},{3,0},{4,7},{5,6},{6,5},{7,4},{8,11},{9,10},{10,... | collective-permute-start | bytes 589832 | tf_op jit(solution)/shard_map/ppermute | solution.py:589
  111.4 38.3 %all-to-all-start.1 = ((bf16[8,192,768]{2,1,0:T(8,128)(2,1)}), bf16[8,192,768]{2,1,0:T(8,128)(2,1)}, u32[]{:S(2)}, u32[]{:S(2)}) async-start(bf16[8,192,768]{2,1,0:T(8,128)(2,1)} %bitcast.170), calls=%async_computation.1 | async-start | bytes 4718592 | tf_op jit(solution)/shard_map/all_to_all | solution.py:675
  147.3 2.4 collective-permute-start.13
  147.8 12.9 %collective-permute-start.15 = (bf16[512,768]{1,0:T(8,128)(2,1)S(1)}, bf16[512,768]{1,0:T(8,128)(2,1)S(1)}, u32[]{:S(2)}, u32[]{:S(2)}) collective-permute-start(bf16[512,768]{1,0:T(8,128)(2,1)S(1)} %get-tuple-element.71.dy_own.dy_ref), channel_id=1, source_target_pairs={{0,4},{1,5},{2,6},{3,7},{4,0},{5,1},{6,2},{7,3},{8,12},{9,13},{10,... | collective-permute-start | bytes 2359304 | tf_op jit(solution)/shard_map/ppermute | solution.py:589
  153.9 6.8 %collective-permute-start.14 = (bf16[512,768]{1,0:T(8,128)(2,1)}, bf16[512,768]{1,0:T(8,128)(2,1)S(1)}, u32[]{:S(2)}, u32[]{:S(2)}) collective-permute-start(bf16[512,768]{1,0:T(8,128)(2,1)} %get-tuple-element.70.n_own), channel_id=1, source_target_pairs={{0,4},{1,5},{2,6},{3,7},{4,0},{5,1},{6,2},{7,3},{8,12},{9,13},{10,... | collective-permute-start | bytes 2359304 | tf_op jit(solution)/shard_map/ppermute | solution.py:589
  155.8 33.9 %all-to-all-start.2 = ((bf16[8,192,768]{2,1,0:T(8,128)(2,1)}), bf16[8,192,768]{2,1,0:T(8,128)(2,1)}, u32[]{:S(2)}, u32[]{:S(2)}) async-start(bf16[8,192,768]{2,1,0:T(8,128)(2,1)} %bitcast.172), calls=%async_computation.2 | async-start | bytes 4718592 | tf_op jit(solution)/shard_map/all_to_all | solution.py:675
  160.2 116.8 %reduce-scatter.3.cloned.1.call-start = ((), (), s32[]{:S(2)}) async-start(), calls=%async_computation.8 | async-start | bytes 5898240 | tf_op jit(solution)/shard_map/reduce_scatter | solution.py:718
  216.6 3.4 collective-permute-start.18
  216.6 11.1 %collective-permute-start.16 = (bf16[512,768]{1,0:T(8,128)(2,1)}, bf16[512,768]{1,0:T(8,128)(2,1)}, u32[]{:S(2)}, u32[]{:S(2)}) collective-permute-start(bf16[512,768]{1,0:T(8,128)(2,1)} %get-tuple-element.80.rest_0_), channel_id=1, source_target_pairs={{0,4},{1,5},{2,6},{3,7},{4,0},{5,1},{6,2},{7,3},{8,12},{9,13},{10,... | collective-permute-start | bytes 2359304 | tf_op jit(solution)/shard_map/ppermute | solution.py:589
  226.7 9.0 %collective-permute-start.19 = (bf16[512,768]{1,0:T(8,128)(2,1)}, bf16[512,768]{1,0:T(8,128)(2,1)S(1)}, u32[]{:S(2)}, u32[]{:S(2)}) collective-permute-start(bf16[512,768]{1,0:T(8,128)(2,1)} %get-tuple-element.88.d_own), channel_id=1, source_target_pairs={{0,4},{1,5},{2,6},{3,7},{4,0},{5,1},{6,2},{7,3},{8,12},{9,13},{10,... | collective-permute-start | bytes 2359304 | tf_op jit(solution)/shard_map/ppermute | solution.py:589
  231.5 43.5 %all-to-all-start.3 = ((bf16[4,192,512]{2,1,0:T(8,128)(2,1)}), bf16[4,192,512]{2,1,0:T(8,128)(2,1)S(1)}, u32[]{:S(2)}, u32[]{:S(2)}) async-start(bf16[4,192,512]{2,1,0:T(8,128)(2,1)} %block.1), calls=%async_computation.3 | async-start | bytes 1572864 | tf_op jit(solution)/shard_map/all_to_all | solution.py:596
  278.1 3.7 collective-permute-start.20
  278.2 45.5 %all-to-all-start.4 = ((bf16[4,192,768]{2,1,0:T(8,128)(2,1)}), bf16[4,192,768]{2,1,0:T(8,128)(2,1)S(1)}, u32[]{:S(2)}, u32[]{:S(2)}) async-start(bf16[4,192,768]{2,1,0:T(8,128)(2,1)} %get-tuple-element.105), calls=%async_computation.5 | async-start | bytes 2359296 | tf_op jit(solution)/shard_map/all_to_all | solution.py:742
  281.7 42.0 %reduce-scatter.5.cloned.1.call-start = ((), (), s32[]{:S(2)}) async-start(), calls=%async_computation.9 | async-start | bytes 1474560 | tf_op jit(solution)/shard_map/reduce_scatter | solution.py:729
  284.3 96.4 %all-gather.9.cloned.1.call-start = ((), (), s32[]{:S(2)}) async-start(), calls=%async_computation.11 | async-start | bytes 2654208 | tf_op jit(solution)/shard_map/all_gather | solution.py:639
  327.2 2.7 collective-permute-start.21
  334.7 34.3 %all-to-all-start.5 = ((bf16[4,208,512]{2,1,0:T(8,128)(2,1)}), bf16[4,208,512]{2,1,0:T(8,128)(2,1)S(1)}, u32[]{:S(2)}, u32[]{:S(2)}) async-start(bf16[4,208,512]{2,1,0:T(8,128)(2,1)} %leave.1.rest_0_), calls=%async_computation.7 | async-start | bytes 1703936 | tf_op jit(solution)/shard_map/all_to_all | solution.py:596
  339.8 66.5 %all-gather.11.cloned.1.call-start = ((), (), s32[]{:S(2)}) async-start(), calls=%async_computation.12 | async-start | bytes 1327104 | tf_op jit(solution)/shard_map/all_gather | solution.py:639
  339.9 3.7 collective-permute-start.17
  340.1 10.7 %collective-permute-start.23 = (bf16[192,768]{1,0:T(8,128)(2,1)}, bf16[192,768]{1,0:T(8,128)(2,1)S(1)}, u32[]{:S(2)}, u32[]{:S(2)}) collective-permute-start(bf16[192,768]{1,0:T(8,128)(2,1)} %get-tuple-element.108), channel_id=1, source_target_pairs={{0,8},{1,9},{2,10},{3,11},{4,12},{5,13},{6,14},{7,15},{8,0},{9,1},... | collective-permute-start | bytes 884744 | tf_op jit(solution)/shard_map/ppermute | solution.py:589
  341.8 15.2 %collective-permute-start.24 = (bf16[192,768]{1,0:T(8,128)(2,1)}, bf16[192,768]{1,0:T(8,128)(2,1)S(1)}, u32[]{:S(2)}, u32[]{:S(2)}) collective-permute-start(bf16[192,768]{1,0:T(8,128)(2,1)} %get-tuple-element.109), channel_id=1, source_target_pairs={{0,16},{1,17},{2,18},{3,19},{4,20},{5,21},{6,22},{7,23},{8,24},{9,... | collective-permute-start | bytes 884744 | tf_op jit(solution)/shard_map/ppermute | solution.py:589
  343.3 20.2 %collective-permute-start.25 = (bf16[192,768]{1,0:T(8,128)(2,1)S(1)}, bf16[192,768]{1,0:T(8,128)(2,1)S(1)}, u32[]{:S(2)}, u32[]{:S(2)}) collective-permute-start(bf16[192,768]{1,0:T(8,128)(2,1)S(1)} %copy-done.51), channel_id=1, source_target_pairs={{0,24},{1,25},{2,26},{3,27},{4,28},{5,29},{6,30},{7,31},{8,16},{9,... | collective-permute-start | bytes 884744 | tf_op jit(solution)/shard_map/ppermute | solution.py:589
  343.7 28.8 %collective-permute-start.27 = (bf16[192,768]{1,0:T(8,128)(2,1)S(1)}, bf16[192,768]{1,0:T(8,128)(2,1)S(1)}, u32[]{:S(2)}, u32[]{:S(2)}) collective-permute-start(bf16[192,768]{1,0:T(8,128)(2,1)S(1)} %copy-done.16), channel_id=1, source_target_pairs={{2,0},{3,1},{4,6},{5,7},{10,8},{11,9},{12,14},{13,15},{18,16},{19,... | collective-permute-start | bytes 884744 | tf_op jit(solution)/shard_map/ppermute | solution.py:589
  363.7 8.8 %collective-permute-start.26 = (bf16[192,768]{1,0:T(8,128)(2,1)S(1)}, bf16[192,768]{1,0:T(8,128)(2,1)S(1)}, u32[]{:S(2)}, u32[]{:S(2)}) collective-permute-start(bf16[192,768]{1,0:T(8,128)(2,1)S(1)} %sum_second.1), channel_id=1, source_target_pairs={{0,1},{1,0},{6,7},{7,6},{8,9},{9,8},{14,15},{15,14},{16,17},{17,16... | collective-permute-start | bytes 884744 | tf_op jit(solution)/shard_map/ppermute | solution.py:589
  367.6 10.5 %collective-permute-start.28 = (bf16[192,768]{1,0:T(8,128)(2,1)S(1)}, bf16[192,768]{1,0:T(8,128)(2,1)S(1)}, u32[]{:S(2)}, u32[]{:S(2)}) collective-permute-start(bf16[192,768]{1,0:T(8,128)(2,1)S(1)} %sum_second.1), channel_id=1, source_target_pairs={{2,1},{3,0},{4,7},{5,6},{10,9},{11,8},{12,15},{13,14},{18,17},{19,... | collective-permute-start | bytes 884744 | tf_op jit(solution)/shard_map/ppermute | solution.py:589
  369.1 11.4 %collective-permute-start.22 = (bf16[2,192,512]{2,1,0:T(8,128)(2,1)S(1)}, bf16[2,192,512]{2,1,0:T(8,128)(2,1)S(1)}, u32[]{:S(2)}, u32[]{:S(2)}) collective-permute-start(bf16[2,192,512]{2,1,0:T(8,128)(2,1)S(1)} %dynamic-slice_bitcast_fusion.1), channel_id=1, source_target_pairs={{0,4},{1,5},{2,6},{3,7},{4,0},{5,1},{6,2},{7,3},{8,12},{9,13},{10,... | collective-permute-start | bytes 1179656 | tf_op jit(solution)/shard_map/ppermute | solution.py:589
  378.3 1.6 collective-permute-start.29
  387.7 1.2 collective-permute-start.30
  389.0 3.6 collective-permute-start.31
  392.6 3.6 collective-permute-start.32
  (48 other events, 240.5 us)
Sparse Core Ops, SparseCore 0:
  65.5 30.6 all-gather.6
  215.6 55.7 reduce-scatter.2
  285.4 30.9 reduce-scatter.4
  327.3 38.0 all-gather.8
  384.0 22.2 all-gather.10
